TPU v7x, 32 devices: a whole 2x2x4 slice. The times are simulated.
32 devices in a mesh: dp: 8 (over y, x, core), chan: 4 (over z).
Axes of the slice: x: 2, y: 2, z: 4, core: 2. Of those that a mesh axis runs over, the one named last changes fastest.
Arguments:
- images: bfloat16 [512, 64, 192], P('dp', 'chan'), may hold values from -6 to 6
- labels: int32 [512], P('dp'), may hold values from 0 to 999
- resolution: int32 [512], P('dp'), may hold values from 6 to 8
- class_weight: float32 [1000], replicated, may hold values from 0.5 to 7.5
- column_master: float32 [1826, 1152], P(None, 'chan'), may hold values from -0.4375 to 0.4375
- column_first: float32 [1826, 1152], P(None, 'chan'), may hold values from -9.536743e-06 to 9.536743e-06
- column_second: float32 [1826, 1152], P(None, 'chan'), may hold values from 2e-14 to 3.2e-13
- column_average: float32 [1826, 1152], P(None, 'chan'), may hold values from -0.4375 to 0.4375
- row_master: float32 [1152, 2800], P('chan'), may hold values from -0.1875 to 0.1875
- row_first: float32 [1152, 2800], P('chan'), may hold values from -9.536743e-06 to 9.536743e-06
- row_second: float32 [1152, 2800], P('chan'), may hold values from 2e-14 to 3.2e-13
- row_average: float32 [1152, 2800], P('chan'), may hold values from -0.1875 to 0.1875
- head_master: float32 [3560, 1280], P(None, ('dp', 'chan')), may hold values from -0.3125 to 0.3125
- head_first: float32 [3560, 1280], P(None, ('dp', 'chan')), may hold values from -9.536743e-06 to 9.536743e-06
- head_second: float32 [3560, 1280], P(None, ('dp', 'chan')), may hold values from 2e-14 to 3.2e-13
- head_average: float32 [3560, 1280], P(None, ('dp', 'chan')), may hold values from -0.3125 to 0.3125
- route_master: float32 [512, 8], replicated, may hold values from -3 to 3
- route_first: float32 [512, 8], replicated, may hold values from -9.536743e-06 to 9.536743e-06
- route_second: float32 [512, 8], replicated, may hold values from 2e-14 to 3.2e-13
- route_average: float32 [512, 8], replicated, may hold values from -3 to 3
Outputs:
- column_moment: float32 [1826, 1152], P(None, 'chan')
- column_variance: float32 [1826, 1152], P(None, 'chan')
- column_updated: float32 [1826, 1152], P(None, 'chan')
- column_smoothed: float32 [1826, 1152], P(None, 'chan')
- column_halves: bfloat16 [1826, 1152], P(None, 'chan')
- row_moment: float32 [1152, 2800], P('chan')
- row_variance: float32 [1152, 2800], P('chan')
- row_updated: float32 [1152, 2800], P('chan')
- row_smoothed: float32 [1152, 2800], P('chan')
- row_halves: bfloat16 [1152, 2800], P('chan')
- head_moment: float32 [3560, 1280], P(None, ('dp', 'chan'))
- head_variance: float32 [3560, 1280], P(None, ('dp', 'chan'))
- head_updated: float32 [3560, 1280], P(None, ('dp', 'chan'))
- head_smoothed: float32 [3560, 1280], P(None, ('dp', 'chan'))
- head_halves: bfloat16 [3560, 1280], P(None, ('dp', 'chan'))
- route_moment: float32 [512, 8], replicated
- route_variance: float32 [512, 8], replicated
- route_updated: float32 [512, 8], replicated
- route_smoothed: float32 [512, 8], replicated
- route_halves: bfloat16 [512, 8], replicated
- loss_total: float32 [], replicated
- weight_total: float32 [], replicated
- clip_norm: float32 [], replicated
All inputs are finite; a program needn't handle non-finite values.
Results may differ from a plain program's by a relative error of at most 0.0059.
Values may be sent and summed in bfloat16 or wider, within the bound.
No kernel may reach another device: no remote copies, remote signals or barrier semaphores. Data moves between devices by JAX's collectives and lax.ppermute only.
A program may use at most 576 MiB of HBM per device.

v0:
```python
import jax
import jax.numpy as jnp
from jax import lax
from jax.sharding import PartitionSpec as P

C0 = 192
C2 = 320
SE = 48
CLASSES = 1000
NE = 8
KERNEL = 5
MAP = 8
STEP = 10


HIGH = lax.Precision.HIGHEST
BIG = lax.Precision.DEFAULT
BETA_ONE = 0.9
BETA_TWO = 0.999
EPSILON = 1e-08
DECAY = 0.05
RATE = 0.05
CLIP = 0.02
SMOOTH = 0.9


def round_value(values):
    return lax.optimization_barrier(values.astype(jnp.bfloat16)).astype(jnp.float32)


def same_value(values):
    return values


def keep_rounded(values):
    return (round_value(values), None)


def keep_plain(values):
    return (values, None)


def pass_grad(kept, grad):
    return (grad,)


def round_grad(kept, grad):
    return (round_value(grad),)


def rounded(values):
    wrapped = jax.custom_vjp(round_value)
    wrapped.defvjp(keep_rounded, pass_grad)
    return wrapped(values)


def rounded_back(values):
    wrapped = jax.custom_vjp(same_value)
    wrapped.defvjp(keep_plain, round_grad)
    return wrapped(values)


def swish(values):
    return values * jax.nn.sigmoid(values)


def depthwise(inputs, kernel):
    batches, channels = (inputs.shape[0], inputs.shape[-1])
    margin = KERNEL // 2
    padded = jnp.pad(
        inputs.reshape(batches, MAP, MAP, channels),
        ((0, 0), (margin, margin), (margin, margin), (0, 0)),
    )
    summed = jnp.zeros((batches, MAP, MAP, channels), jnp.float32)
    for offset in range(KERNEL * KERNEL):
        down_step, side_step = (offset // KERNEL, offset % KERNEL)
        summed = (
            summed
            + padded[:, down_step : down_step + MAP, side_step : side_step + MAP, :]
            * kernel[offset]
        )
    return summed.reshape(batches, MAP * MAP, channels)


def unpack(column_pack, row_pack, head_pack, route_pack):
    taps = KERNEL * KERNEL
    begin = C0 + 2 * taps + SE
    return (
        column_pack[:C0],
        column_pack[C0 : C0 + taps],
        row_pack[:, :C0],
        route_pack[:C0],
        column_pack[begin:].reshape(NE, C0, column_pack.shape[1]),
        column_pack[C0 + taps : C0 + 2 * taps],
        row_pack[:, C0 : C0 + SE],
        column_pack[C0 + 2 * taps : begin],
        row_pack[:, C0 + SE :].reshape(row_pack.shape[0], NE, C2).transpose(1, 0, 2),
        route_pack[C0:],
        head_pack[: NE * C2].reshape(NE, C2, head_pack.shape[1]),
        head_pack[NE * C2 :],
    )


def mask_count(resolution):
    spots = jnp.arange(MAP * MAP, dtype=jnp.int32)
    inside = ((spots // MAP)[None, :] < resolution[:, None]) & (
        (spots % MAP)[None, :] < resolution[:, None]
    )
    return (
        inside.astype(jnp.float32)[:, :, None],
        (resolution * resolution).astype(jnp.float32)[:, None],
    )


def first_block(first_in, first_kernel, first_out, inputs, valid_mask):
    expanded = rounded_back(
        jnp.einsum("bpc,cf->bpf", rounded(inputs), rounded(first_in), precision=BIG)
    )
    depth_out = swish(depthwise(swish(expanded) * valid_mask, first_kernel)) * valid_mask
    return jnp.einsum("bpf,fo->bpo", rounded(depth_out), rounded(first_out), precision=BIG)


def route_logits(router, hidden, valid_mask, pixel_count):
    return jnp.dot(jnp.sum(hidden * valid_mask, 1) / pixel_count, router, precision=HIGH)


def route_weight(hidden, valid_mask, pixel_count, grad_logit):
    return jnp.dot((jnp.sum(hidden * valid_mask, 1) / pixel_count).T, grad_logit, precision=HIGH)


def route_rows(router, valid_mask, pixel_count, grad_logit):
    return valid_mask * (jnp.dot(grad_logit, router.T, precision=HIGH) / pixel_count)[:, None, :]


def second_expand(expert_in, kernel, inputs, gating, valid_mask):
    expanded = rounded_back(
        jnp.einsum("bpc,ecf->bpef", rounded(inputs), rounded(expert_in), precision=BIG)
    )
    mixed = jnp.einsum("bpef,be->bpf", expanded, gating, precision=HIGH)
    return swish(depthwise(swish(mixed) * valid_mask, kernel)) * valid_mask


def squeeze(excite_in, depth_out, pixel_count):
    return jnp.dot(jnp.sum(depth_out, 1) / pixel_count, excite_in, precision=HIGH)


def second_project(excite_out, expert_out, depth_out, squeezed, gating):
    excite = jax.nn.sigmoid(jnp.dot(swish(squeezed), excite_out, precision=HIGH))
    projected = rounded_back(
        jnp.einsum(
            "bpf,efo->bpeo",
            rounded(depth_out * excite[:, None, :]),
            rounded(expert_out),
            precision=BIG,
        )
    )
    return jnp.einsum("bpeo,be->bpo", projected, gating, precision=HIGH)


def head_block(head_experts, hidden, gating, valid_mask, pixel_count):
    expanded = rounded_back(
        jnp.einsum("bpo,eoh->bpeh", rounded(hidden), rounded(head_experts), precision=BIG)
    )
    feature = swish(jnp.einsum("bpeh,be->bph", expanded, gating, precision=HIGH)) * valid_mask
    return jnp.sum(feature, 1) / pixel_count


def plain_loss(logits, onehot, weight):
    top = jnp.max(logits, 1, keepdims=True)
    spread = top[:, 0] + jnp.log(jnp.sum(jnp.exp(logits - top), 1))
    return jnp.sum(weight * (spread - jnp.sum(logits * onehot, 1)))


def class_loss(classifier, pooled, onehot, weight):
    logits = rounded_back(jnp.dot(rounded(pooled), rounded(classifier).T, precision=BIG))
    return plain_loss(logits, onehot, weight)


def adamw(master, first, second, average, grad):
    first = BETA_ONE * first + (1.0 - BETA_ONE) * grad
    second = BETA_TWO * second + (1.0 - BETA_TWO) * grad * grad
    ratio = first / (1.0 - BETA_ONE**STEP) / (jnp.sqrt(second / (1.0 - BETA_TWO**STEP)) + EPSILON)
    master = master - RATE * (ratio + DECAY * master)
    average = SMOOTH * average + (1.0 - SMOOTH) * master
    return (first, second, master, average, master.astype(jnp.bfloat16))


def chan_total(values):
    return lax.psum(values, "chan")


def gather_rows(values):
    return lax.all_gather(values.astype(jnp.bfloat16), "chan", axis=1, tiled=True).astype(
        jnp.float32
    )


def gather_grads(values):
    return lax.all_gather(values.astype(jnp.bfloat16), "chan", axis=1, tiled=True).astype(
        jnp.float32
    )


def spread_rows(values):
    return lax.psum_scatter(values, "chan", scatter_dimension=1, tiled=True)


def own_rows(values, rows_own):
    return lax.dynamic_slice_in_dim(values, lax.axis_index("chan") * rows_own, rows_own, 1)


def on_device(
    images,
    labels,
    resolution,
    class_weight,
    column_master,
    column_first,
    column_second,
    column_average,
    row_master,
    row_first,
    row_second,
    row_average,
    head_master,
    head_first,
    head_second,
    head_average,
    route_master,
    route_first,
    route_second,
    route_average,
):
    chans = lax.axis_size("chan")
    rows_own = images.shape[1]
    valid_mask, pixel_count = mask_count(resolution)
    mask_own = own_rows(valid_mask, rows_own)
    onehot = (labels[:, None] == jnp.arange(CLASSES, dtype=jnp.int32)[None, :]).astype(jnp.float32)
    weight = jnp.dot(onehot, class_weight, precision=HIGH)
    head_local = lax.all_gather(
        head_master.astype(jnp.bfloat16), ("dp", "chan"), axis=1, tiled=True
    ).astype(jnp.float32)
    (
        first_in,
        first_kernel,
        first_out,
        route_in,
        expert_in,
        second_kernel,
        excite_in,
        excite_out,
        expert_out,
        route_out,
        head_experts,
        classifier,
    ) = unpack(column_master, row_master, head_local, route_master)
    entry_own = images.astype(jnp.float32) * mask_own
    entry_full = gather_rows(entry_own)
    partial_one, pull_first = jax.vjp(
        lambda a, b, c: first_block(a, b, c, entry_full, valid_mask),
        first_in,
        first_kernel,
        first_out,
    )
    hidden_own = entry_own + spread_rows(partial_one)
    hidden_full = gather_rows(hidden_own)
    gating = jax.nn.sigmoid(chan_total(route_logits(route_in, hidden_own, mask_own, pixel_count)))
    depth_out, pull_expand = jax.vjp(
        lambda a, b, c, d: second_expand(a, b, c, d, valid_mask),
        expert_in,
        second_kernel,
        hidden_full,
        gating,
    )
    squeeze_part, pull_squeeze = jax.vjp(
        lambda a, b: squeeze(a, b, pixel_count), excite_in, depth_out
    )
    squeezed = chan_total(squeeze_part)
    partial_two, pull_project = jax.vjp(
        second_project, excite_out, expert_out, depth_out, squeezed, gating
    )
    narrow_own = spread_rows(partial_two)
    head_gating = jax.nn.sigmoid(
        chan_total(route_logits(route_out, narrow_own, mask_own, pixel_count))
    )
    pooled_part, pull_head = jax.vjp(
        lambda a, b, c: head_block(a, b, c, mask_own, pixel_count),
        head_experts,
        narrow_own,
        head_gating,
    )
    pooled = chan_total(pooled_part)
    loss_local, pull_loss = jax.vjp(
        lambda a, b: class_loss(a, b, onehot, weight), classifier, pooled
    )
    grad_classifier, grad_pooled = pull_loss(jnp.ones((), jnp.float32))
    grad_heads, grad_narrow, grad_head_gate = pull_head(grad_pooled)
    grad_head_logit = chan_total(grad_head_gate) * head_gating * (1.0 - head_gating)
    grad_route_out = route_weight(narrow_own, mask_own, pixel_count, grad_head_logit)
    grad_narrow_full = gather_grads(
        grad_narrow + route_rows(route_out, mask_own, pixel_count, grad_head_logit)
    )
    grad_excite_out, grad_expert_out, grad_depth_one, grad_squeezed, grad_gate_one = pull_project(
        grad_narrow_full
    )
    grad_excite_in, grad_depth_two = pull_squeeze(chan_total(grad_squeezed))
    grad_expert_in, grad_kernel_two, grad_hidden_part, grad_gate_two = pull_expand(
        grad_depth_one + grad_depth_two
    )
    grad_logit = chan_total(grad_gate_one + grad_gate_two) * gating * (1.0 - gating)
    grad_route_in = route_weight(hidden_own, mask_own, pixel_count, grad_logit)
    grad_hidden_own = lax.psum_scatter(
        grad_hidden_part.astype(jnp.bfloat16), "chan", scatter_dimension=1, tiled=True
    ).astype(jnp.float32) + route_rows(route_in, mask_own, pixel_count, grad_logit)
    grad_branch = gather_grads(grad_hidden_own)
    grad_first_in, grad_first_kernel, grad_first_out = pull_first(grad_branch)
    column_grad = jnp.concatenate(
        [
            grad_first_in,
            grad_first_kernel,
            grad_kernel_two,
            grad_excite_out,
            grad_expert_in.reshape(NE * C0, grad_expert_in.shape[2]),
        ],
        0,
    )
    row_grad = jnp.concatenate(
        [
            grad_first_out,
            grad_excite_in,
            grad_expert_out.transpose(1, 0, 2).reshape(grad_expert_out.shape[1], NE * C2),
        ],
        1,
    )
    head_grad = jnp.concatenate(
        [grad_heads.reshape(NE * C2, grad_heads.shape[2]), grad_classifier / chans], 0
    )
    head_shard = lax.psum_scatter(head_grad, ("dp", "chan"), scatter_dimension=1, tiled=True)
    column_sum, row_sum = lax.psum((column_grad, row_grad), "dp")
    route_grad = jnp.concatenate([grad_route_in, grad_route_out], 0)
    squares = (jnp.sum(column_sum * column_sum) + jnp.sum(row_sum * row_sum)) / lax.axis_size(
        "dp"
    ) + jnp.sum(head_shard * head_shard)
    route_sum, square_sum, loss_total, weight_total = lax.psum(
        (route_grad, squares, loss_local / chans, jnp.sum(weight) / chans), ("dp", "chan")
    )
    clip_norm = jnp.sqrt(square_sum + jnp.sum(route_sum * route_sum)) / weight_total
    factor = jnp.minimum(1.0, CLIP / (clip_norm + 1e-06)) / weight_total
    column_out = adamw(
        column_master, column_first, column_second, column_average, column_sum * factor
    )
    row_out = adamw(row_master, row_first, row_second, row_average, row_sum * factor)
    head_out = adamw(head_master, head_first, head_second, head_average, head_shard * factor)
    route_out_new = adamw(
        route_master, route_first, route_second, route_average, route_sum * factor
    )
    return (
        column_out[0],
        column_out[1],
        column_out[2],
        column_out[3],
        column_out[4],
        row_out[0],
        row_out[1],
        row_out[2],
        row_out[3],
        row_out[4],
        head_out[0],
        head_out[1],
        head_out[2],
        head_out[3],
        head_out[4],
        route_out_new[0],
        route_out_new[1],
        route_out_new[2],
        route_out_new[3],
        route_out_new[4],
        loss_total,
        weight_total,
        clip_norm,
    )


def solution(mesh):
    return jax.shard_map(
        on_device,
        mesh=mesh,
        in_specs=(
            P("dp", "chan", None),
            P("dp"),
            P("dp"),
            P(),
            P(None, "chan"),
            P(None, "chan"),
            P(None, "chan"),
            P(None, "chan"),
            P("chan", None),
            P("chan", None),
            P("chan", None),
            P("chan", None),
            P(None, ("dp", "chan")),
            P(None, ("dp", "chan")),
            P(None, ("dp", "chan")),
            P(None, ("dp", "chan")),
            P(),
            P(),
            P(),
            P(),
        ),
        out_specs=(
            P(None, "chan"),
            P(None, "chan"),
            P(None, "chan"),
            P(None, "chan"),
            P(None, "chan"),
            P("chan", None),
            P("chan", None),
            P("chan", None),
            P("chan", None),
            P("chan", None),
            P(None, ("dp", "chan")),
            P(None, ("dp", "chan")),
            P(None, ("dp", "chan")),
            P(None, ("dp", "chan")),
            P(None, ("dp", "chan")),
            P(),
            P(),
            P(),
            P(),
            P(),
            P(),
            P(),
            P(),
        ),
        check_vma=False,
    )
```

profile of v0, /device:TPU:0, one launch (start us, length us, event | category | flops | bytes accessed | tf_op | source)
XLA Modules:
  0.0 2379.1 jit_solution(15358875072298974848)
XLA Ops:
  20.3 38.8 %all-gather.6.cloned.1.call-done = bf16[64,64,192]{2,1,0:T(8,128)(2,1)} async-done(((bf16[64,16,192]{2,1,0:T(8,128)(2,1)}), bf16[64,64,192]{2,1,0:T(8,128)(2,1)}) %all-gather.6.cloned.1.call-update) | async-done | bytes 1572880 | tf_op jit(solution)/shard_map/all_gather | solution.py:193
  62.0 4.1 fusion.133
  66.9 60.9 %fusion.95 = (bf16[64,64,288]{2,1,0:T(8,128)(2,1)}, f32[64,8,8,288]{3,2,1,0:T(8,128)}) fusion(f32[64,64]{1,0:T(8,128)S(1)} %and_convert_fusion.1, f32[288]{0:T(512)S(1)} %get-tuple-element.96, f32[288]{0:T(512)S(1)} %get-tuple-element.97, f32[288]{0:T(512)S(1)} %get-tuple-element.98, f32[288]{0:T(512)S(1)} %get-tuple-element.99, ...), kind=kLoop, calls=%fused_computation.277 | loop fusion | flops 64880640 | bytes 11841664 | tf_op jit(solution)/shard_map/jvp()/convert_element_type | solution.py:28
  127.8 5.1 fusion.139
  132.9 75.6 %reduce-scatter.5.cloned.1.call-done = f32[64,16,192]{2,1,0:T(8,128)} async-done(((f32[64,64,192]{2,1,0:T(8,128)}), f32[64,16,192]{2,1,0:T(8,128)}) %reduce-scatter.5.cloned.1.call-update) | async-done | bytes 786448 | tf_op jit(solution)/shard_map/reduce_scatter | solution.py:205
  222.4 4.0 convert_element_type.143
  234.4 11.3 psum.91
  246.5 11.5 all-gather.8.cloned.1.call-done
  257.9 21.3 fusion.112
  279.2 79.8 %fusion.6 = f32[64,1,64,288]{3,1,2,0:T(1,128)S(1)} fusion(f32[64,8,1,1]{1,2,3,0:T(1,128)S(1)} %copy.137, f32[64,64,8,288]{3,1,2,0:T(8,128)} %fusion.112), kind=kOutput, calls=%fused_computation.56 | convolution fusion | flops 113246208 | bytes 42469376 | tf_op jit(solution)/shard_map/jvp(bpef,be->bpf)/dot_general | solution.py:139
  359.2 4.0 fusion.136
  363.7 72.8 %multiply_reduce_fusion.2 = (f32[64,288]{1,0:T(8,128)S(1)}, f32[64,8,8,288]{3,2,1,0:T(8,128)}) fusion(f32[64,8,8]{2,1,0:T(8,128)S(1)} %copy-done.44, f32[288]{0:T(512)S(1)} %copy-done.151, f32[288]{0:T(512)S(1)} %get-tuple-element.73, f32[288]{0:T(512)S(1)} %get-tuple-element.74, f32[288]{0:T(512)S(1)} %get-tuple-element.75, f32[288]{0:T(512)S(1)} %get-tuple-element.76, ...), kind=kLoop, calls=%fused_computation.284 | loop fusion | flops 64862208 | bytes 9556096 | tf_op jit(solution)/shard_map/jvp()/reduce_sum | solution.py:144
  438.0 16.7 psum.92
  455.2 3.8 multiply_convert_fusion.3
  459.1 22.5 fusion.107
  481.5 79.7 %fusion.2 = f32[64,1,64,320]{3,1,2,0:T(1,128)S(1)} fusion(f32[64,8,1,1]{1,2,3,0:T(1,128)S(1)} %copy.137, f32[64,64,8,320]{3,1,2,0:T(8,128)} %fusion.107), kind=kOutput, calls=%fused_computation.52 | convolution fusion | flops 125829120 | bytes 47187968 | tf_op jit(solution)/shard_map/jvp(bpeo,be->bpo)/dot_general | solution.py:157
  561.2 6.3 copy.202
  569.6 6.4 slice.498
  576.0 9.5 copy.167
  585.5 91.4 %reduce-scatter.7.cloned.1.call-done = f32[64,16,320]{2,0,1:T(8,128)} async-done(((f32[64,64,320]{2,0,1:T(8,128)}), f32[64,16,320]{2,0,1:T(8,128)}) %reduce-scatter.7.cloned.1.call-update) | async-done | bytes 1310736 | tf_op jit(solution)/shard_map/reduce_scatter | solution.py:205
  680.0 11.0 psum.93
  691.1 19.9 fusion.17
  711.0 66.7 %fusion.10 = f32[64,1,16,1280]{3,1,2,0:T(1,128)S(1)} fusion(f32[64,8,1,1]{1,2,3,0:T(1,128)S(1)} %copy.144, f32[64,16,8,1280]{3,1,2,0:T(8,128)} %fusion.17), kind=kOutput, calls=%fused_computation.61 | convolution fusion | flops 125829120 | bytes 47187968 | tf_op jit(solution)/shard_map/jvp(bpeh,be->bph)/dot_general | solution.py:164
  783.3 21.3 all-reduce.108
  808.6 4.0 fusion.226
  812.6 4.9 fusion.98
  817.5 126.7 %fusion.8 = f32[64,1,8,1]{2,1,3,0:T(1,128)S(1)} fusion(f32[64,16,8,1280]{3,1,2,0:T(8,128)} %fusion.17, f32[64,16,1280,1]{2,0,1,3:T(8,128)S(1)} %fusion.226), kind=kOutput, calls=%fused_computation.59 | convolution fusion | flops 125829120 | bytes 47187968 | tf_op jit(solution)/shard_map/transpose(jvp(bpeh,be->bph))/dot_general | solution.py:164
  944.2 10.0 psum.95
  954.6 10.0 fusion.14
  964.6 17.9 fusion.122
  982.6 61.9 %all-gather.12.cloned.1.call-done = bf16[64,64,320]{2,0,1:T(8,128)(2,1)} async-done(((bf16[64,16,320]{2,0,1:T(8,128)(2,1)}), bf16[64,64,320]{2,0,1:T(8,128)(2,1)}) %all-gather.12.cloned.1.call-update) | async-done | bytes 2621456 | tf_op jit(solution)/shard_map/all_gather | solution.py:199
  1044.5 3.7 copy.123
  1048.3 10.1 fusion.12
  1058.4 14.3 fusion.116
  1072.8 20.5 fusion.82
  1094.8 16.7 psum.96
  1113.0 53.4 %fusion.56 = (f32[288]{0:T(512)}, f32[288]{0:T(512)}, f32[288]{0:T(512)}, f32[288]{0:T(512)}, f32[288]{0:T(512)}, /*index=5*/f32[288]{0:T(512)}, f32[288]{0:T(51...) fusion(f32[64,8,8,288]{3,2,1,0:T(8,128)} %fusion.136, ...), kind=kLoop, calls=%fused_computation.227 | loop fusion | flops 56617920 | bytes 19058944 | tf_op jit(solution)/shard_map/transpose(jvp())/reduce_sum | solution.py:79
  1166.6 35.3 %fusion.74 = (f32[288]{0:T(512)}, f32[288]{0:T(512)}, f32[288]{0:T(512)}, f32[288]{0:T(512)}, f32[288]{0:T(512)S(1)}, /*index=5*/f32[288]{0:T(512)S(1)}, f32[64,...) fusion(f32[64,64,288]{2,1,0:T(8,128)} %get-tuple-element.150, ...), kind=kLoop, calls=%fused_computation.245 | loop fusion | flops 28309824 | bytes 66081024 | tf_op jit(solution)/shard_map/transpose(jvp())/reduce_sum | solution.py:79
  1202.0 27.8 %bitcast_multiply_fusion.97 = (f32[64,8,8,288]{3,2,1,0:T(8,128)}, f32[64,8,8,288]{3,2,1,0:T(8,128)}, f32[64,8,8,288]{3,2,1,0:T(8,128)}, f32[64,8,8,288]{3,2,1,0:...) fusion(f32[64,64,288]{2,1,0:T(8,128)} %get-tuple-element.150, ...), kind=kLoop, calls=%fused_computation.226 | loop fusion | flops 15335424 | bytes 66075264 | tf_op jit(solution)/shard_map/transpose(jvp())/mul | solution.py:79
  1229.8 70.4 %fusion = f32[64,1,8,1]{2,1,3,0:T(1,128)S(1)} fusion(f32[64,64,8,320]{3,1,2,0:T(8,128)} %fusion.107, bf16[64,64,320,1]{2,0,1,3:T(8,128)(2,1)S(1)} %bitcast.454), kind=kOutput, calls=%fused_computation.50 | convolution fusion | flops 125829120 | bytes 44566528 | tf_op jit(solution)/shard_map/transpose(jvp(bpeo,be->bpo))/dot_general | solution.py:157
  1300.3 4.1 copy.130
  1334.7 45.3 %pad_add_fusion.1 = f32[64,12,12,288]{3,2,1,0:T(8,128)} fusion(f32[64,8,8,288]{3,2,1,0:T(8,128)} %get-tuple-element.201, f32[64,8,8,288]{3,2,1,0:T(8,128)} %get-tuple-element.200, f32[64,8,8,288]{3,2,1,0:T(8,128)} %get-tuple-element.199, f32[64,8,8,288]{3,2,1,0:T(8,128)} %get-tuple-element.198, f32[64,8,8,288]{3,2,1,0:T(8,128)} %get-tuple-element.197, ...), kind=kLoop, calls=%fused_computation.67 | loop fusion | flops 47775744 | bytes 100270080 | tf_op jit(solution)/shard_map/transpose(jvp())/add_any | solution.py:79
  1380.0 16.4 fusion.22
  1396.5 9.0 fusion.13
  1406.8 19.9 bitcast_convert_fusion
  1426.7 120.4 %fusion.4 = f32[64,1,8,1]{2,1,3,0:T(1,128)S(1)} fusion(f32[64,64,8,288]{3,1,2,0:T(8,128)} %fusion.112, f32[64,64,288,1]{2,1,0,3:T(8,128)} %bitcast.443), kind=kOutput, calls=%fused_computation.54 | convolution fusion | flops 113246208 | bytes 42469376 | tf_op jit(solution)/shard_map/transpose(jvp(bpef,be->bpf))/dot_general | solution.py:139
  1547.2 9.5 psum.97
  1559.5 13.0 fusion.114
  1577.7 26.2 %all-gather.14.cloned.1.call-done = bf16[64,64,192]{2,1,0:T(8,128)(2,1)} async-done(((bf16[64,16,192]{2,1,0:T(8,128)(2,1)}), bf16[64,64,192]{2,1,0:T(8,128)(2,1)}) %all-gather.14.cloned.1.call-update) | async-done | bytes 1572880 | tf_op jit(solution)/shard_map/all_gather | solution.py:199
  1604.0 40.2 %fusion.50 = (f32[288]{0:T(512)S(1)}, f32[288]{0:T(512)S(1)}, f32[288]{0:T(512)S(1)}, f32[288]{0:T(512)S(1)}, f32[288]{0:T(512)S(1)}, /*index=5*/f32[288]{0:T(51...) fusion(f32[64,8,8,288]{3,2,1,0:T(8,128)} %fusion.133, ...), kind=kOutput, calls=%fused_computation.172 | convolution fusion | flops 493091136 | bytes 72499456 | tf_op jit(solution)/shard_map/transpose(jvp(bpf,fo->bpo))/dot_general | solution.py:120
  1644.3 48.0 %fusion.32 = (f32[288]{0:T(512)S(1)}, f32[288]{0:T(512)S(1)}, f32[288]{0:T(512)S(1)}, f32[288]{0:T(512)S(1)}, f32[288]{0:T(512)S(1)}, /*index=5*/f32[288]{0:T(51...) fusion(f32[64,64,288]{2,1,0:T(8,128)} %get-tuple-element.222, ...), kind=kLoop, calls=%fused_computation.154 | loop fusion | flops 42462144 | bytes 9457920 | tf_op jit(solution)/shard_map/transpose(jvp())/reduce_sum | solution.py:79
  1692.4 27.9 %bitcast_multiply_fusion.48 = (f32[64,8,8,288]{3,2,1,0:T(8,128)}, f32[64,8,8,288]{3,2,1,0:T(8,128)}, f32[64,8,8,288]{3,2,1,0:T(8,128)}, f32[64,8,8,288]{3,2,1,0:...) fusion(f32[64,64,288]{2,1,0:T(8,128)} %get-tuple-element.222, ...), kind=kLoop, calls=%fused_computation.153 | loop fusion | flops 15335424 | bytes 66075264 | tf_op jit(solution)/shard_map/transpose(jvp())/mul | solution.py:79
  1725.6 45.3 %pad_add_fusion = f32[64,12,12,288]{3,2,1,0:T(8,128)} fusion(f32[64,8,8,288]{3,2,1,0:T(8,128)} %get-tuple-element.188, f32[64,8,8,288]{3,2,1,0:T(8,128)} %get-tuple-element.187, f32[64,8,8,288]{3,2,1,0:T(8,128)} %get-tuple-element.186, f32[64,8,8,288]{3,2,1,0:T(8,128)} %get-tuple-element.185, f32[64,8,8,288]{3,2,1,0:T(8,128)} %get-tuple-element.184, ...), kind=kLoop, calls=%fused_computation.66 | loop fusion | flops 47775744 | bytes 100270080 | tf_op jit(solution)/shard_map/transpose(jvp())/add_any | solution.py:79
  1771.1 22.7 multiply_reduce_fusion
  1801.8 4.9 concatenate.13
  1809.2 14.6 fusion.178
  1826.9 6.0 copy.133
  1832.9 14.2 copy.132
  1847.1 14.4 pad_maximum_fusion
  1863.7 39.7 %all-reduce.107.cloned.1.call-done = (f32[1826,288]{0,1:T(8,128)}, f32[288,2800]{1,0:T(8,128)}) async-done(((f32[1826,288]{0,1:T(8,128)}, f32[288,2800]{1,0:T(8,128)}), (f32[1826,288]{0,1:T(8,128)}, f32[288,2800]{1,0:T(8,128)})) %all-reduce.107.cloned.1.call-update) | async-done | bytes 5329168 | tf_op jit(solution)/shard_map/psum | solution.py:339
  1910.9 392.1 %reduce-scatter.11.cloned.1.call-done = f32[3560,40]{0,1:T(8,128)} async-done(((f32[3560,1280]{0,1:T(8,128)}), f32[3560,40]{0,1:T(8,128)}) %reduce-scatter.11.cloned.1.call-update) | async-done | bytes 569616 | tf_op jit(solution)/shard_map/reduce_scatter | solution.py:338
  2305.4 39.0 %all-reduce.102 = (f32[]{:T(128)}, f32[512,8]{0,1:T(8,128)S(1)}, f32[]{:T(128)}, f32[]{:T(128)}) all-reduce(f32[]{:T(128)S(6)} %add.607, f32[512,8]{0,1:T(8,128)S(1)} %pad_maximum_fusion.1, f32[]{:T(128)S(6)} %div.227, f32[]{:T(128)S(6)} %div.251), channel_id=1, replica_groups=mesh['dp'=8,'chan'=4] {'dp','chan'}, use_global_device_ids=true, to_apply=%region_75.76 | all-reduce | flops 4099 | bytes 32792 | tf_op jit(solution)/shard_map/psum | solution.py:344
  2354.0 5.4 fusion.195
  2363.9 4.2 fusion.193
  (582 shorter events, 140.2 us)
Async XLA Ops:
  7.2 798.4 %copy-start = (f32[1000]{0:T(1024)S(1)}, f32[1000]{0:T(1024)}, u32[]{:S(2)}) copy-start(f32[1000]{0:T(1024)} %param.23) | copy-start | bytes 12004
  7.2 51.9 %all-gather.6.cloned.1.call-start = ((), (), s32[]{:S(2)}) async-start(), calls=%async_computation.4 | async-start | bytes 2621440 | tf_op jit(solution)/shard_map/all_gather | solution.py:193
  8.2 447.1 %copy-start.25 = (f32[64,64]{1,0:T(8,128)}, f32[64,64]{1,0:T(8,128)S(1)}, u32[]{:S(2)}) copy-start(f32[64,64]{1,0:T(8,128)S(1)} %and_convert_fusion.1) | copy-start | bytes 49156
  8.2 559.3 %copy-start.45 = (f32[64,16]{1,0:T(8,128)}, f32[64,16]{1,0:T(8,128)S(1)}, u32[]{:S(2)}) copy-start(f32[64,16]{1,0:T(8,128)S(1)} %constant_dynamic-slice_fusion) | copy-start | bytes 12292
  10.3 198.2 %reduce-scatter.5.cloned.1.call-start = ((), (), s32[]{:S(2)}) async-start(), calls=%async_computation.5 | async-start | bytes 5242880 | tf_op jit(solution)/shard_map/reduce_scatter | solution.py:205
  17.9 48.7 %copy-start.91 = (f32[288]{0:T(512)}, f32[288]{0:T(512)S(1)}, u32[]{:S(2)}) copy-start(f32[288]{0:T(512)S(1)} %get-tuple-element.110) | copy-start | bytes 3460
  17.9 48.7 %copy-start.93 = (f32[288]{0:T(512)}, f32[288]{0:T(512)S(1)}, u32[]{:S(2)}) copy-start(f32[288]{0:T(512)S(1)} %get-tuple-element.111) | copy-start | bytes 3460
  17.9 48.7 %copy-start.95 = (f32[288]{0:T(512)}, f32[288]{0:T(512)S(1)}, u32[]{:S(2)}) copy-start(f32[288]{0:T(512)S(1)} %get-tuple-element.112) | copy-start | bytes 3460
  17.9 48.7 %copy-start.97 = (f32[288]{0:T(512)}, f32[288]{0:T(512)S(1)}, u32[]{:S(2)}) copy-start(f32[288]{0:T(512)S(1)} %get-tuple-element.113) | copy-start | bytes 3460
  17.9 48.7 %copy-start.99 = (f32[288]{0:T(512)}, f32[288]{0:T(512)S(1)}, u32[]{:S(2)}) copy-start(f32[288]{0:T(512)S(1)} %get-tuple-element.114) | copy-start | bytes 3460
  17.9 48.7 %copy-start.101 = (f32[288]{0:T(512)}, f32[288]{0:T(512)S(1)}, u32[]{:S(2)}) copy-start(f32[288]{0:T(512)S(1)} %get-tuple-element.115) | copy-start | bytes 3460
  18.0 48.7 %copy-start.103 = (f32[288]{0:T(512)}, f32[288]{0:T(512)S(1)}, u32[]{:S(2)}) copy-start(f32[288]{0:T(512)S(1)} %get-tuple-element.116) | copy-start | bytes 3460
  18.0 48.7 %copy-start.105 = (f32[288]{0:T(512)}, f32[288]{0:T(512)S(1)}, u32[]{:S(2)}) copy-start(f32[288]{0:T(512)S(1)} %get-tuple-element.117) | copy-start | bytes 3460
  18.0 48.7 %copy-start.107 = (f32[288]{0:T(512)}, f32[288]{0:T(512)S(1)}, u32[]{:S(2)}) copy-start(f32[288]{0:T(512)S(1)} %get-tuple-element.118) | copy-start | bytes 3460
  18.0 48.7 %copy-start.109 = (f32[288]{0:T(512)}, f32[288]{0:T(512)S(1)}, u32[]{:S(2)}) copy-start(f32[288]{0:T(512)S(1)} %get-tuple-element.119) | copy-start | bytes 3460
  18.0 48.7 %copy-start.117 = (f32[288]{0:T(512)}, f32[288]{0:T(512)S(1)}, u32[]{:S(2)}) copy-start(f32[288]{0:T(512)S(1)} %get-tuple-element.109) | copy-start | bytes 3460
  20.3 343.2 %copy-start.67 = (f32[288]{0:T(512)}, f32[288]{0:T(512)S(1)}, u32[]{:S(2)}) copy-start(f32[288]{0:T(512)S(1)} %get-tuple-element.90) | copy-start | bytes 3460
  127.8 85.6 %copy-start.208 = (s32[64]{0:T(128)S(1)}, s32[64]{0:T(128)}, u32[]{:S(2)}) copy-start(s32[64]{0:T(128)} %param.22) | copy-start | bytes 772
  132.9 125.0 %all-gather.8.cloned.1.call-start = ((), (), s32[]{:S(2)}) async-start(), calls=%async_computation.6 | async-start | bytes 2621440 | tf_op jit(solution)/shard_map/all_gather | solution.py:193
  211.2 356.5 %all-gather.10.cloned.1.call-start = ((), (), s32[]{:S(2)}) async-start(), calls=%async_computation.8 | async-start | bytes 9461760 | tf_op jit(solution)/shard_map/all_gather | solution.py:240
  213.0 463.9 %reduce-scatter.7.cloned.1.call-start = ((), (), s32[]{:S(2)}) async-start(), calls=%async_computation.7 | async-start | bytes 7864320 | tf_op jit(solution)/shard_map/reduce_scatter | solution.py:205
  220.7 58.5 %copy-start.21 = (bf16[8,192,288]{1,0,2:T(8,128)(2,1)}, bf16[8,192,288]{1,0,2:T(8,128)(2,1)S(1)}, u32[]{:S(2)}) copy-start(bf16[8,192,288]{1,0,2:T(8,128)(2,1)S(1)} %convert_element_type.139) | copy-start | bytes 2654212
  231.7 131.8 %copy-start.69 = (f32[288]{0:T(512)}, f32[288]{0:T(512)S(1)}, u32[]{:S(2)}) copy-start(f32[288]{0:T(512)S(1)} %get-tuple-element.71) | copy-start | bytes 3460
  231.7 131.8 %copy-start.71 = (f32[288]{0:T(512)}, f32[288]{0:T(512)S(1)}, u32[]{:S(2)}) copy-start(f32[288]{0:T(512)S(1)} %get-tuple-element.73) | copy-start | bytes 3460
  231.7 131.8 %copy-start.73 = (f32[288]{0:T(512)}, f32[288]{0:T(512)S(1)}, u32[]{:S(2)}) copy-start(f32[288]{0:T(512)S(1)} %get-tuple-element.74) | copy-start | bytes 3460
  231.7 131.8 %copy-start.75 = (f32[288]{0:T(512)}, f32[288]{0:T(512)S(1)}, u32[]{:S(2)}) copy-start(f32[288]{0:T(512)S(1)} %get-tuple-element.75) | copy-start | bytes 3460
  231.7 131.8 %copy-start.77 = (f32[288]{0:T(512)}, f32[288]{0:T(512)S(1)}, u32[]{:S(2)}) copy-start(f32[288]{0:T(512)S(1)} %get-tuple-element.76) | copy-start | bytes 3460
  231.7 131.8 %copy-start.79 = (f32[288]{0:T(512)}, f32[288]{0:T(512)S(1)}, u32[]{:S(2)}) copy-start(f32[288]{0:T(512)S(1)} %get-tuple-element.77) | copy-start | bytes 3460
  363.7 72.8 %copy-start.210 = (f32[64]{0:T(128)S(1)}, f32[64]{0:T(128)}, u32[]{:S(2)}) copy-start(f32[64]{0:T(128)} %copy-done.209) | copy-start | bytes 772
  567.5 477.0 %all-gather.12.cloned.1.call-start = ((), (), s32[]{:S(2)}) async-start(), calls=%async_computation.9 | async-start | bytes 3932160 | tf_op jit(solution)/shard_map/all_gather | solution.py:199
  576.0 103.7 %copy-start.167 = (f32[512,8]{0,1:T(8,128)S(1)}, f32[512,8]{0,1:T(8,128)}, u32[]{:S(2)}) copy-start(f32[512,8]{0,1:T(8,128)} %param.36) | copy-start | bytes 49156
  576.0 103.7 %copy-start.211 = (f32[64]{0:T(128)S(1)}, f32[64]{0:T(128)}, u32[]{:S(2)}) copy-start(f32[64]{0:T(128)} %copy-done.209) | copy-start | bytes 772
  691.0 263.2 %copy-start.176 = (f32[64,8]{0,1:T(8,128)}, f32[64,8]{0,1:T(8,128)S(1)}, u32[]{:S(2)}) copy-start(f32[64,8]{0,1:T(8,128)S(1)} %psum.93) | copy-start | bytes 6148
  982.5 65.7 %copy-start.63 = (f32[64,8]{0,1:T(8,128)S(1)}, f32[64,8]{0,1:T(8,128)}, u32[]{:S(2)}) copy-start(f32[64,8]{0,1:T(8,128)} %get-tuple-element.213) | copy-start | bytes 6148
  982.6 574.5 %reduce-scatter.9.cloned.1.call-start = ((), (), s32[]{:S(2)}) async-start(), calls=%async_computation.10 | async-start | bytes 2621440 | tf_op jit(solution)/shard_map/reduce_scatter | solution.py:312
  1093.2 73.1 %copy-start.51 = (f32[64,288]{1,0:T(8,128)}, f32[64,288]{1,0:T(8,128)S(1)}, u32[]{:S(2)}) copy-start(f32[64,288]{1,0:T(8,128)S(1)} %get-tuple-element.220) | copy-start | bytes 221188
  1111.5 54.9 %copy-start.65 = (f32[64,48]{0,1:T(8,128)}, f32[64,48]{0,1:T(8,128)S(1)}, u32[]{:S(2)}) copy-start(f32[64,48]{0,1:T(8,128)S(1)} %psum.96) | copy-start | bytes 36868
  1112.9 53.5 %copy-start.68 = (f32[288]{0:T(512)S(1)}, f32[288]{0:T(512)}, u32[]{:S(2)}) copy-start(f32[288]{0:T(512)} %copy-done.67) | copy-start | bytes 3460
  1112.9 53.5 %copy-start.70 = (f32[288]{0:T(512)S(1)}, f32[288]{0:T(512)}, u32[]{:S(2)}) copy-start(f32[288]{0:T(512)} %copy-done.69) | copy-start | bytes 3460
  1112.9 53.5 %copy-start.72 = (f32[288]{0:T(512)S(1)}, f32[288]{0:T(512)}, u32[]{:S(2)}) copy-start(f32[288]{0:T(512)} %copy-done.71) | copy-start | bytes 3460
  1112.9 53.5 %copy-start.74 = (f32[288]{0:T(512)S(1)}, f32[288]{0:T(512)}, u32[]{:S(2)}) copy-start(f32[288]{0:T(512)} %copy-done.73) | copy-start | bytes 3460
  1112.9 53.5 %copy-start.76 = (f32[288]{0:T(512)S(1)}, f32[288]{0:T(512)}, u32[]{:S(2)}) copy-start(f32[288]{0:T(512)} %copy-done.75) | copy-start | bytes 3460
  1112.9 53.5 %copy-start.78 = (f32[288]{0:T(512)S(1)}, f32[288]{0:T(512)}, u32[]{:S(2)}) copy-start(f32[288]{0:T(512)} %copy-done.77) | copy-start | bytes 3460
  1112.9 53.5 %copy-start.80 = (f32[288]{0:T(512)S(1)}, f32[288]{0:T(512)}, u32[]{:S(2)}) copy-start(f32[288]{0:T(512)} %copy-done.79) | copy-start | bytes 3460
  1112.9 53.5 %copy-start.82 = (f32[288]{0:T(512)S(1)}, f32[288]{0:T(512)}, u32[]{:S(2)}) copy-start(f32[288]{0:T(512)} %get-tuple-element.78) | copy-start | bytes 3460
  1112.9 53.5 %copy-start.84 = (f32[288]{0:T(512)S(1)}, f32[288]{0:T(512)}, u32[]{:S(2)}) copy-start(f32[288]{0:T(512)} %get-tuple-element.79) | copy-start | bytes 3460
  1113.0 53.5 %copy-start.86 = (f32[288]{0:T(512)S(1)}, f32[288]{0:T(512)}, u32[]{:S(2)}) copy-start(f32[288]{0:T(512)} %get-tuple-element.80) | copy-start | bytes 3460
  1113.0 53.5 %copy-start.88 = (f32[288]{0:T(512)S(1)}, f32[288]{0:T(512)}, u32[]{:S(2)}) copy-start(f32[288]{0:T(512)} %get-tuple-element.81) | copy-start | bytes 3460
  1113.0 53.5 %copy-start.90 = (f32[288]{0:T(512)S(1)}, f32[288]{0:T(512)}, u32[]{:S(2)}) copy-start(f32[288]{0:T(512)} %get-tuple-element.82) | copy-start | bytes 3460
  1426.6 177.2 %all-gather.14.cloned.1.call-start = ((), (), s32[]{:S(2)}) async-start(), calls=%async_computation.11 | async-start | bytes 2621440 | tf_op jit(solution)/shard_map/all_gather | solution.py:199
  1426.7 130.1 %copy-start.168 = (f32[512,8]{0,1:T(8,128)S(1)}, f32[512,8]{0,1:T(8,128)}, u32[]{:S(2)}) copy-start(f32[512,8]{0,1:T(8,128)} %param.36) | copy-start | bytes 49156
  1426.7 130.1 %copy-start.174 = (f32[64,8]{0,1:T(8,128)S(1)}, f32[64,8]{0,1:T(8,128)}, u32[]{:S(2)}) copy-start(f32[64,8]{0,1:T(8,128)} %copy-done.173) | copy-start | bytes 6148
  1426.7 130.1 %copy-start.212 = (f32[64]{0:T(128)S(1)}, f32[64]{0:T(128)}, u32[]{:S(2)}) copy-start(f32[64]{0:T(128)} %copy-done.209) | copy-start | bytes 772
  1426.7 130.4 %copy-start.46 = (f32[64,16]{1,0:T(8,128)S(1)}, f32[64,16]{1,0:T(8,128)}, u32[]{:S(2)}) copy-start(f32[64,16]{1,0:T(8,128)} %copy-done.45) | copy-start | bytes 12292
  1426.7 132.7 %copy-start.20 = (bf16[64,64,192]{2,1,0:T(8,128)(2,1)S(1)}, bf16[64,64,192]{2,1,0:T(8,128)(2,1)}, u32[]{:S(2)}) copy-start(bf16[64,64,192]{2,1,0:T(8,128)(2,1)} %all-gather.8.cloned.1.call-done) | copy-start | bytes 4718596
  1559.4 344.0 %all-reduce.107.cloned.1.call-start = ((), (), s32[]{:S(2)}) async-start(), calls=%async_computation.13 | async-start | bytes 10911744 | tf_op jit(solution)/shard_map/psum | solution.py:339
  1809.2 493.8 %reduce-scatter.11.cloned.1.call-start = ((), (), s32[]{:S(2)}) async-start(), calls=%async_computation.12 | async-start | bytes 18923520 | tf_op jit(solution)/shard_map/reduce_scatter | solution.py:338
  1861.6 486.2 %copy-start.169 = (f32[512,8]{0,1:T(8,128)S(1)}, f32[512,8]{0,1:T(8,128)}, u32[]{:S(2)}) copy-start(f32[512,8]{0,1:T(8,128)} %param.36) | copy-start | bytes 49156
  1861.6 486.2 %copy-start.170 = (f32[512,8]{0,1:T(8,128)S(1)}, f32[512,8]{0,1:T(8,128)}, u32[]{:S(2)}) copy-start(f32[512,8]{0,1:T(8,128)} %param.38) | copy-start | bytes 49156
  1861.6 486.2 %copy-start.171 = (f32[512,8]{0,1:T(8,128)S(1)}, f32[512,8]{0,1:T(8,128)}, u32[]{:S(2)}) copy-start(f32[512,8]{0,1:T(8,128)} %param.37) | copy-start | bytes 49156
  1861.6 486.8 %copy-start.172 = (f32[512,8]{0,1:T(8,128)S(1)}, f32[512,8]{0,1:T(8,128)}, u32[]{:S(2)}) copy-start(f32[512,8]{0,1:T(8,128)} %param.39) | copy-start | bytes 49156
  1861.6 487.4 %copy-start.32 = (f32[3560,40]{0,1:T(8,128)S(1)}, f32[3560,40]{0,1:T(8,128)}, u32[]{:S(2)}) copy-start(f32[3560,40]{0,1:T(8,128)} %param.32) | copy-start | bytes 1708804
  1861.6 487.4 %copy-start.50 = (f32[3560,40]{0,1:T(8,128)S(1)}, f32[3560,40]{0,1:T(8,128)}, u32[]{:S(2)}) copy-start(f32[3560,40]{0,1:T(8,128)} %param.34) | copy-start | bytes 1708804
  1863.4 490.5 %copy-start.7 = (f32[1826,288]{0,1:T(8,128)S(1)}, f32[1826,288]{0,1:T(8,128)}, u32[]{:S(2)}) copy-start(f32[1826,288]{0,1:T(8,128)} %param.24) | copy-start | bytes 6310660
  (162 other events, 3781.0 us)
Sparse Core Ops, SparseCore 0:
  10.5 48.6 all-gather.5
  133.0 75.4 reduce-scatter.4
  211.3 46.5 all-gather.7
  261.6 79.4 all-gather.9
  567.6 109.2 reduce-scatter.6
  982.7 61.8 all-gather.11
  1426.8 42.6 reduce-scatter.8
  1559.3 44.4 all-gather.13
  1809.3 94.1 all-reduce.106
  1905.6 397.2 reduce-scatter.10
where the time goes:
time: 2390 us; the launch traced here: 2380 us
  matrix products  775 us (32%)
  waiting for transfers between devices  737 us (31%)
  other arithmetic  571 us (24%)
  blocking collectives  136 us (6%)
  local copies, waits for them, and re-layouts  135 us (6%)
  between operations  24.7 us (1%)
    reduce_scatter x1, waiting for transfers between devices, on_device(): lax.psum_scatter(head_grad, ('dp', 'chan'), scatter_dimension=1, tiled=True)  392 us
    dot_general x2, matrix products, second_expand(): mixed = jnp.einsum('bpef,be->bpf', expanded, gating, precision=HIGH)  200 us
    dot_general x2, matrix products, head_block(): jnp.einsum('bpeh,be->bph', expanded, gating, precision=HIGH)  193 us
    reduce_scatter x2, waiting for transfers between devices, spread_rows(): return lax.psum_scatter(values, 'chan', scatter_dimension=1, tiled=True)  167 us
    reduce_sum x4, other arithmetic, depthwise(): padded[:, down_step:down_step + MAP, side_step:side_step + MAP, :]  159 us
    dot_general x2, matrix products, second_project(): return jnp.einsum('bpeo,be->bpo', projected, gating, precision=HIGH)  150 us
    psum x7, blocking collectives, chan_total(): return lax.psum(values, 'chan')  96.7 us
    add_any x2, other arithmetic, depthwise(): padded[:, down_step:down_step + MAP, side_step:side_step + MAP, :]  90.6 us
  transfers between devices with their start and end apart: 10, of which 8 were waited for; matrix products, arithmetic and copies ran while one was open for 23% of the time, Pallas kernels for 0%

commit v1 on v0

v1 whole, which is shorter than its diff:
```python
import functools
import math

import jax
import jax.numpy as jnp
from jax import lax
from jax.experimental import pallas as pl
from jax.experimental.pallas import tpu as pltpu
from jax.sharding import Mesh
from jax.sharding import PartitionSpec as P

C0 = 192
C2 = 320
SE = 48
CLASSES = 1000
NE = 8
HALF = NE // 2
KERNEL = 5
TAPS = KERNEL * KERNEL
MAP = 8
STEP = 10
LANES = 128

HIGH = lax.Precision.HIGHEST
BETA_ONE = 0.9
BETA_TWO = 0.999
EPSILON = 1e-08
DECAY = 0.05
RATE = 0.05
CLIP = 0.02
SMOOTH = 0.9

F32 = jnp.float32
BF16 = jnp.bfloat16
VMEM_BYTES = 60 * 1024 * 1024


def nn(left, right):
    return jnp.dot(left, right, preferred_element_type=F32)


def nt(left, right):
    return lax.dot_general(left, right, (((1,), (1,)), ((), ())), preferred_element_type=F32)


def high_nn(left, right):
    return jnp.dot(left, right, precision=HIGH, preferred_element_type=F32)


def high_nt(left, right):
    return lax.dot_general(
        left, right, (((1,), (1,)), ((), ())), precision=HIGH, preferred_element_type=F32
    )


def high_tn(left, right):
    return lax.dot_general(
        left, right, (((0,), (0,)), ((), ())), precision=HIGH, preferred_element_type=F32
    )


def sig(values):
    return 0.5 * jnp.tanh(0.5 * values) + 0.5


def slope(values, gate):
    return gate * (1.0 + values * (1.0 - gate))


def loop(count, body):
    def step(index, carry):
        body(index)
        return carry

    lax.fori_loop(0, count, step, 0)


def rows_at(index, count):
    return pl.ds(pl.multiple_of(index * count, count), count)


def lanes_at(index):
    return pl.ds(pl.multiple_of(index * LANES, LANES), LANES)


def depthwise(source, taps, lanes, batch, flip, emit):
    parts = batch // 8
    weights = [taps[TAPS - 1 - t if flip else t, :, lanes] for t in range(TAPS)]
    for down in range(MAP):
        total = {}
        for step_y in range(-2, 3):
            line = down + step_y
            if not 0 <= line < MAP:
                continue
            for spot in range(MAP):
                for part in range(parts):
                    value = source[pl.ds((line * MAP + spot) * batch + 8 * part, 8), lanes]
                    for step_x in range(-2, 3):
                        place = spot - step_x
                        if not 0 <= place < MAP:
                            continue
                        term = value * weights[(step_y + 2) * KERNEL + step_x + 2]
                        key = (place, part)
                        total[key] = total[key] + term if key in total else term
        for (place, part), value in total.items():
            emit((down * MAP + place) * batch + 8 * part, value)


def depthwise_weight(source, grad, lanes, batch, store):
    parts = batch // 8
    total = {}
    for down in range(MAP):
        slopes = {
            (spot, part): grad[pl.ds((down * MAP + spot) * batch + 8 * part, 8), lanes]
            for spot in range(MAP)
            for part in range(parts)
        }
        for step_y in range(-2, 3):
            line = down + step_y
            if not 0 <= line < MAP:
                continue
            for spot in range(MAP):
                for part in range(parts):
                    value = source[pl.ds((line * MAP + spot) * batch + 8 * part, 8), lanes]
                    for step_x in range(-2, 3):
                        place = spot - step_x
                        if not 0 <= place < MAP:
                            continue
                        tap = (step_y + 2) * KERNEL + step_x + 2
                        term = value * slopes[(place, part)]
                        total[tap] = total[tap] + term if tap in total else term
    for tap in range(TAPS):
        store(tap, jnp.sum(total[tap], axis=0, keepdims=True))


def pair_gates(gates, width):
    batch = gates.shape[0]
    spots = lax.broadcasted_iota(jnp.int32, (batch, 2 * width), 1)
    out = []
    for pair in range(HALF):
        left = jnp.broadcast_to(gates[:, 2 * pair : 2 * pair + 1], (batch, 2 * width))
        right = jnp.broadcast_to(gates[:, 2 * pair + 1 : 2 * pair + 2], (batch, 2 * width))
        out.append(jnp.where(spots < width, left, right))
    return out


def split_sums(values, width):
    columns = []
    for value in values:
        spots = lax.broadcasted_iota(jnp.int32, value.shape, 1)
        columns.append(jnp.sum(jnp.where(spots < width, value, 0.0), axis=1, keepdims=True))
        columns.append(jnp.sum(jnp.where(spots < width, 0.0, value), axis=1, keepdims=True))
    return jnp.concatenate(columns, axis=1)


def grouped(values, batch):
    return values.reshape(values.shape[0] // batch, batch, values.shape[1])


def flat(values):
    return values.reshape(values.shape[0] * values.shape[1], values.shape[2])


def first_forward(
    x_ref, left_ref, right_ref, taps_ref, mask_ref, count_ref, route_ref,
    conv_ref, wide_ref, twice_ref, mean_ref, gate_ref, small_gates_ref, large_gates_ref,
    act, deep, total,
):
    batch, tile = count_ref.shape[0], act.shape[1]
    line = MAP * batch
    step = pl.program_id(0)

    def expand(index):
        rows = rows_at(index, line)
        value = nt(x_ref[rows, :], left_ref[:, :C0])
        for part in range(tile // LANES):
            here = value[:, part * LANES : (part + 1) * LANES]
            act[rows, part * LANES : (part + 1) * LANES] = here * sig(here) * mask_ref[rows, :]

    loop(MAP, expand)

    def conv(index):
        lanes = lanes_at(index)

        def emit(row, value):
            conv_ref[pl.ds(row, 8), lanes] = value

        depthwise(act, taps_ref, lanes, batch, False, emit)

    loop(tile // LANES, conv)

    def activate(index):
        rows = rows_at(index, line)
        for part in range(tile // LANES):
            lanes = slice(part * LANES, (part + 1) * LANES)
            here = conv_ref[rows, lanes]
            deep[rows, lanes] = (here * sig(here) * mask_ref[rows, :]).astype(BF16)

    loop(MAP, activate)
    part_sum = nn(deep[...], right_ref[:, :C0])

    @pl.when(step == 0)
    def _():
        total[...] = part_sum

    @pl.when(step > 0)
    def _():
        total[...] += part_sum

    @pl.when(step == pl.num_programs(0) - 1)
    def _():
        mean_ref[...] = jnp.zeros_like(mean_ref)

        def finish(index):
            rows = rows_at(index, line)
            value = x_ref[rows, :].astype(F32) + total[rows, :]
            low = value.astype(BF16)
            twice_ref[rows, :C0] = low
            twice_ref[rows, C0:] = low
            for part in range(2):
                lanes = slice(0, LANES) if part == 0 else slice(LANES, C0)
                kept = value[:, lanes] * mask_ref[rows, : lanes.stop - lanes.start]
                mean_ref[:, lanes] += jnp.sum(grouped(kept, batch), axis=0)

        loop(MAP, finish)
        mean_ref[...] = mean_ref[...] / count_ref[:, :1]
        gates = jax.nn.sigmoid(high_nn(mean_ref[...], route_ref[...]))
        gate_ref[...] = gates
        for pair, value in enumerate(pair_gates(gates, C0)):
            small_gates_ref[pair] = value
        for pair, value in enumerate(pair_gates(gates, C2)):
            large_gates_ref[pair] = value

        def widen(index):
            rows = rows_at(index, line)
            value = grouped(twice_ref[rows, :].astype(F32), batch)
            for pair in range(HALF):
                lanes = slice(pair * 2 * C0, (pair + 1) * 2 * C0)
                wide_ref[rows, lanes] = flat(value * small_gates_ref[pair][None]).astype(BF16)

        loop(MAP, widen)


def second_forward(
    wide_ref, own_ref, far_ref, taps_ref, mask_ref, count_ref, squeeze_ref, excite_ref,
    mixed_ref, conv_ref, mean_ref, units_ref, scale_ref,
    act,
):
    batch, tile = count_ref.shape[0], act.shape[1]
    line = MAP * batch
    step = pl.program_id(0)
    half = own_ref.shape[1]

    def expand(index):
        rows = rows_at(index, 2 * line)
        mixed_ref[rows, :] = nt(wide_ref[rows, :half], own_ref[...]) + nt(
            wide_ref[rows, half:], far_ref[...]
        )

    loop(MAP // 2, expand)

    def activate(index):
        rows = rows_at(index, line)
        for part in range(tile // LANES):
            lanes = slice(part * LANES, (part + 1) * LANES)
            here = mixed_ref[rows, lanes]
            act[rows, lanes] = here * sig(here) * mask_ref[rows, :]

    loop(MAP, activate)

    def conv(index):
        lanes = lanes_at(index)

        def emit(row, value):
            conv_ref[pl.ds(row, 8), lanes] = value

        depthwise(act, taps_ref, lanes, batch, False, emit)

    loop(tile // LANES, conv)
    mean_ref[...] = jnp.zeros_like(mean_ref)

    def pool(index):
        rows = rows_at(index, line)
        for part in range(tile // LANES):
            lanes = slice(part * LANES, (part + 1) * LANES)
            here = conv_ref[rows, lanes]
            kept = here * sig(here) * mask_ref[rows, :]
            mean_ref[:, lanes] += jnp.sum(grouped(kept, batch), axis=0)

    loop(MAP, pool)
    mean_ref[...] = mean_ref[...] / count_ref[:, :1]
    units = high_nn(mean_ref[...], squeeze_ref[...])

    @pl.when(step == 0)
    def _():
        units_ref[...] = units

    @pl.when(step > 0)
    def _():
        units_ref[...] += units

    @pl.when(step == pl.num_programs(0) - 1)
    def _():
        value = units_ref[...]
        scale_ref[...] = jax.nn.sigmoid(high_nt(value * jax.nn.sigmoid(value), excite_ref[...]))


def project(
    conv_ref, scale_ref, own_ref, far_ref, mask_ref, count_ref, gates_ref, route_ref,
    each_ref, twice_ref, wide_ref, mean_ref, gate_ref, head_gates_ref,
    scaled,
):
    batch = count_ref.shape[0]
    line = MAP * batch
    width = scaled.shape[1]

    def activate(index):
        rows = rows_at(index, line)
        for part in range(width // LANES):
            lanes = slice(part * LANES, (part + 1) * LANES)
            here = conv_ref[rows, lanes]
            kept = grouped(here * sig(here) * mask_ref[rows, :], batch)
            scaled[rows, lanes] = flat(kept * scale_ref[:, lanes][None]).astype(BF16)

    loop(MAP, activate)
    mean_ref[...] = jnp.zeros_like(mean_ref)
    pairs = HALF // 2

    def mix(index):
        rows = rows_at(index, 2 * line)
        value = scaled[rows, :]
        total = None
        for pair in range(HALF):
            weights = own_ref if pair < pairs else far_ref
            inner = slice((pair % pairs) * 2 * C2, (pair % pairs + 1) * 2 * C2)
            each = nn(value, weights[:, inner])
            each_ref[rows, pair * 2 * C2 : (pair + 1) * 2 * C2] = each.astype(BF16)
            term = grouped(each, batch) * gates_ref[pair][None]
            total = term if total is None else total + term
        total = flat(total)
        value = total[:, :C2] + total[:, C2:]
        low = value.astype(BF16)
        twice_ref[rows, :C2] = low
        twice_ref[rows, C2:] = low
        kept = grouped(value * mask_ref[rows, :1], batch)
        mean_ref[...] += jnp.sum(kept, axis=0)

    loop(MAP // 2, mix)
    mean_ref[...] = mean_ref[...] / count_ref[:, :1]
    gates = jax.nn.sigmoid(high_nn(mean_ref[...], route_ref[...]))
    gate_ref[...] = gates
    for pair, value in enumerate(pair_gates(gates, C2)):
        head_gates_ref[pair] = value

    def widen(index):
        rows = rows_at(index, line)
        value = grouped(twice_ref[rows, :].astype(F32), batch)
        for pair in range(HALF):
            lanes = slice(pair * 2 * C2, (pair + 1) * 2 * C2)
            wide_ref[rows, lanes] = flat(value * head_gates_ref[pair][None]).astype(BF16)

    loop(MAP, widen)


def head(
    wide_ref, twice_ref, own_ref, far_ref, mask_ref, count_ref, label_ref, class_ref,
    gates_ref, gate_ref, mean_ref, route_ref,
    expert_grad_ref, class_grad_ref, loss_ref, hidden_grad_ref, route_grad_ref,
    mixed, slopes, turned, pooled, total,
):
    batch = count_ref.shape[0]
    line = MAP * batch
    step = pl.program_id(0)
    half = own_ref.shape[0]
    experts = NE * C2
    columns = expert_grad_ref.shape[2]
    sides = (own_ref, far_ref)

    @pl.when(step == 0)
    def _():
        pooled[...] = jnp.zeros_like(pooled)
        for side, weights in enumerate(sides):

            def expand(index, side=side, weights=weights):
                rows = rows_at(index, 2 * line)
                mixed[rows, side * half : (side + 1) * half] = nt(
                    wide_ref[rows, :], weights[:, :experts]
                )

            loop(MAP // 2, expand)

        def pool(index):
            rows = rows_at(index, line)
            for part in range(2 * half // LANES):
                lanes = slice(part * LANES, (part + 1) * LANES)
                here = mixed[rows, lanes]
                kept = here * sig(here) * mask_ref[rows, :]
                pooled[:, lanes] += jnp.sum(grouped(kept, batch), axis=0)

        loop(MAP, pool)
        mean = (pooled[...] / count_ref[:, :1]).astype(BF16)
        logits = nn(mean[:, :half], own_ref[:, experts:]) + nn(mean[:, half:], far_ref[:, experts:])
        spots = lax.broadcasted_iota(jnp.int32, logits.shape, 1)
        onehot = (spots == label_ref[...]).astype(F32)
        weight = jnp.sum(onehot * class_ref[...], axis=1, keepdims=True)
        top = jnp.max(logits, axis=1, keepdims=True)
        powers = jnp.exp(logits - top)
        summed = jnp.sum(powers, axis=1, keepdims=True)
        loss = weight * (top + jnp.log(summed) - jnp.sum(logits * onehot, axis=1, keepdims=True))
        loss_ref[...] = jnp.concatenate([loss, weight], axis=1)
        logit_grad = (weight * (powers / summed - onehot)).astype(BF16)
        for side, weights in enumerate(sides):
            place = slice(side * half, (side + 1) * half)
            class_grad_ref[side] = lax.dot_general(
                mean[:, place], logit_grad, (((0,), (0,)), ((), ())), preferred_element_type=F32
            )
            pooled[:, place] = nt(logit_grad, weights[:, experts:]) / count_ref[:, :1]

        def back(index):
            rows = rows_at(index, line)
            for part in range(2 * half // LANES):
                lanes = slice(part * LANES, (part + 1) * LANES)
                here = mixed[rows, lanes]
                value = grouped(mask_ref[rows, :] * slope(here, sig(here)), batch)
                slopes[rows, lanes] = flat(value * pooled[:, lanes][None]).astype(BF16)

        loop(MAP, back)
        for part in range(2 * half // LANES):
            turned[part * LANES : (part + 1) * LANES, :] = slopes[
                :, part * LANES : (part + 1) * LANES
            ].T

    blocks = experts // columns
    side = 1 - step // blocks
    block = step % blocks
    expert_grad_ref[0] = nn(
        turned[pl.ds(pl.multiple_of(side * half, half), half), :],
        wide_ref[:, pl.ds(pl.multiple_of(block * columns, columns), columns)],
    )

    @pl.when(step == pl.num_programs(0) - 1)
    def _():
        sums = [jnp.zeros((batch, 2 * C2), F32)] * HALF

        def pull(index, sums):
            rows = rows_at(index, 2 * line)
            left, right = (slopes[rows, :half], slopes[rows, half:])
            hidden = grouped(twice_ref[rows, :].astype(F32), batch)
            summed = None
            sums = list(sums)
            for pair in range(HALF):
                lanes = slice(pair * 2 * C2, (pair + 1) * 2 * C2)
                each = grouped(nn(left, own_ref[:, lanes]) + nn(right, far_ref[:, lanes]), batch)
                sums[pair] = sums[pair] + jnp.sum(each * hidden, axis=0)
                term = each * gates_ref[pair][None]
                summed = term if summed is None else summed + term
            summed = flat(summed)
            total[rows, :] = summed[:, :C2] + summed[:, C2:]
            return tuple(sums)

        sums = lax.fori_loop(0, MAP // 2, pull, tuple(sums))
        gates = gate_ref[...]
        logit = split_sums(sums, C2) * gates * (1.0 - gates)
        route_grad_ref[...] = high_tn(mean_ref[...], logit)
        back_rows = high_nt(logit, route_ref[...]) / count_ref[:, :1]

        def finish(index):
            rows = rows_at(index, line)
            value = grouped(total[rows, :], batch) + back_rows[None] * grouped(
                jnp.broadcast_to(mask_ref[rows, :1], (line, C2)), batch
            )
            low = flat(value).astype(BF16)
            hidden_grad_ref[rows, :C2] = low
            hidden_grad_ref[rows, C2:] = low

        loop(MAP, finish)


def project_back(
    hidden_ref, gates_ref, each_ref, own_ref, far_ref, conv_ref, scale_ref, mask_ref,
    full_scale_ref, units_ref, mean_ref, excite_ref,
    grad_ref, own_grad_ref, far_grad_ref, gate_sum_ref, unit_grad_ref, small_ref,
    spread, scaled, sums,
):
    batch, tile = scale_ref.shape
    line = MAP * batch
    step = pl.program_id(0)
    half = own_ref.shape[1]

    @pl.when(step == 0)
    def _():
        gate_sum_ref[...] = jnp.zeros_like(gate_sum_ref)

        def widen(index):
            rows = rows_at(index, line)
            value = grouped(hidden_ref[rows, :].astype(F32), batch)
            for pair in range(HALF):
                lanes = slice(pair * 2 * C2, (pair + 1) * 2 * C2)
                spread[rows, lanes] = flat(value * gates_ref[pair][None]).astype(BF16)
                each = grouped(each_ref[rows, lanes].astype(F32), batch)
                gate_sum_ref[pair] += jnp.sum(each * value, axis=0)

        loop(MAP, widen)

    def pull(index):
        rows = rows_at(index, 2 * line)
        grad_ref[rows, :] = nt(spread[rows, :half], own_ref[...]) + nt(
            spread[rows, half:], far_ref[...]
        )

    loop(MAP // 2, pull)
    place = pl.ds(pl.multiple_of(step * tile, tile), tile)
    sums[:, place] = jnp.zeros((batch, tile), F32)

    def activate(index):
        rows = rows_at(index, line)
        for part in range(tile // LANES):
            lanes = slice(part * LANES, (part + 1) * LANES)
            here = conv_ref[rows, lanes]
            kept = here * sig(here) * mask_ref[rows, :]
            scaled[rows, lanes] = flat(grouped(kept, batch) * scale_ref[:, lanes][None]).astype(BF16)
            added = jnp.sum(grouped(grad_ref[rows, lanes] * kept, batch), axis=0)
            sums[:, pl.ds(pl.multiple_of(step * tile + part * LANES, LANES), LANES)] += added

    loop(MAP, activate)
    turned = scaled[...].T
    far_grad_ref[...] = nn(turned, spread[:, half:])
    own_grad_ref[...] = nn(turned, spread[:, :half])

    @pl.when(step == pl.num_programs(0) - 1)
    def _():
        scale = full_scale_ref[...]
        pre = sums[...] * scale * (1.0 - scale)
        units = units_ref[...]
        gate = jax.nn.sigmoid(units)
        unit_grad = high_nn(pre, excite_ref[...]) * slope(units, gate)
        unit_grad_ref[...] = unit_grad
        small_ref[:, :SE] = high_tn(pre, units * gate)
        small_ref[:, SE:] = high_tn(mean_ref[...], unit_grad)


def second_back(
    grad_ref, scale_ref, unit_grad_ref, squeeze_ref, count_ref, mask_ref, conv_ref, mixed_ref,
    taps_ref, wide_ref, own_ref, far_ref, twice_ref, gates_ref, gate_ref, gate_sum_ref,
    route_ref, mean_ref,
    own_grad_ref, far_grad_ref, tap_grad_ref, hidden_grad_ref, route_grad_ref,
    act, inner, slopes, own_all, far_all,
):
    batch, tile = scale_ref.shape
    line = MAP * batch
    step = pl.program_id(0)
    half = own_ref.shape[1]
    place = pl.ds(pl.multiple_of(step * tile, tile), tile)
    own_all[place, :] = own_ref[...]
    far_all[place, :] = far_ref[...]
    pool_grad = high_nt(unit_grad_ref[...], squeeze_ref[...]) / count_ref[:, :1]

    def activate(index):
        rows = rows_at(index, line)
        for part in range(tile // LANES):
            lanes = slice(part * LANES, (part + 1) * LANES)
            mask = mask_ref[rows, :]
            here = mixed_ref[rows, lanes]
            act[rows, lanes] = here * sig(here) * mask
            here = conv_ref[rows, lanes]
            value = grouped(grad_ref[rows, lanes], batch) * scale_ref[:, lanes][None]
            value = flat(value + pool_grad[:, lanes][None])
            inner[rows, lanes] = value * mask * slope(here, sig(here))

    loop(MAP, activate)

    def conv(index):
        lanes = lanes_at(index)

        def store(tap, value):
            tap_grad_ref[tap : tap + 1, lanes] = value

        depthwise_weight(act, inner, lanes, batch, store)

        def emit(row, value):
            act[pl.ds(row, 8), lanes] = value

        depthwise(inner, taps_ref, lanes, batch, True, emit)

    loop(tile // LANES, conv)

    def deactivate(index):
        rows = rows_at(index, line)
        for part in range(tile // LANES):
            lanes = slice(part * LANES, (part + 1) * LANES)
            here = mixed_ref[rows, lanes]
            value = act[rows, lanes] * mask_ref[rows, :] * slope(here, sig(here))
            slopes[rows, pl.ds(pl.multiple_of(step * tile + part * LANES, LANES), LANES)] = (
                value.astype(BF16)
            )

    loop(MAP, deactivate)
    turned = slopes[:, place].T
    far_grad_ref[...] = nn(turned, wide_ref[:, half:])
    own_grad_ref[...] = nn(turned, wide_ref[:, :half])

    @pl.when(step == pl.num_programs(0) - 1)
    def _():
        sums = [jnp.zeros((batch, 2 * C0), F32)] * HALF
        pairs = HALF // 2

        def pull(index, sums):
            rows = rows_at(index, 2 * line)
            value = slopes[rows, :]
            hidden = grouped(twice_ref[rows, :].astype(F32), batch)
            summed = None
            sums = list(sums)
            for pair in range(HALF):
                weights = own_all if pair < pairs else far_all
                lanes = slice((pair % pairs) * 2 * C0, (pair % pairs + 1) * 2 * C0)
                each = grouped(nn(value, weights[:, lanes]), batch)
                sums[pair] = sums[pair] + jnp.sum(each * hidden, axis=0)
                term = each * gates_ref[pair][None]
                summed = term if summed is None else summed + term
            act[rows, : 2 * C0] = flat(summed)
            return tuple(sums)

        sums = lax.fori_loop(0, MAP // 2, pull, tuple(sums))
        gates = gate_ref[...]
        logit = split_sums(sums, C0) + split_sums([gate_sum_ref[k] for k in range(HALF)], C2)
        logit = logit * gates * (1.0 - gates)
        route_grad_ref[...] = high_tn(mean_ref[...], logit)
        back_rows = high_nt(logit, route_ref[...]) / count_ref[:, :1]

        def finish(index):
            rows = rows_at(index, line)
            summed = act[rows, : 2 * C0]
            value = grouped(summed[:, :C0] + summed[:, C0:], batch) + back_rows[None] * grouped(
                jnp.broadcast_to(mask_ref[rows, :1], (line, C0)), batch
            )
            hidden_grad_ref[rows, :] = flat(value).astype(BF16)

        loop(MAP, finish)


def first_back(
    x_ref, left_ref, right_ref, taps_ref, mask_ref, conv_ref, hidden_ref,
    weight_grad_ref, tap_grad_ref,
    act, inner, wide, deep,
):
    tile = act.shape[1]
    batch = x_ref.shape[0] // (MAP * MAP)
    line = MAP * batch

    def expand(index):
        rows = rows_at(index, line)
        value = nt(x_ref[rows, :], left_ref[:, :C0])
        grad = nt(hidden_ref[rows, :], right_ref[:, :C0])
        for part in range(tile // LANES):
            lanes = slice(part * LANES, (part + 1) * LANES)
            mask = mask_ref[rows, :]
            here = value[:, lanes]
            gate = sig(here)
            act[rows, lanes] = here * gate * mask
            wide[rows, lanes] = slope(here, gate) * mask
            here = conv_ref[rows, lanes]
            gate = sig(here)
            deep[rows, lanes] = (here * gate * mask).astype(BF16)
            inner[rows, lanes] = grad[:, lanes] * mask * slope(here, gate)

    loop(MAP, expand)
    weight_grad_ref[:, C0:] = nn(deep[...].T, hidden_ref[...])

    def conv(index):
        lanes = lanes_at(index)

        def store(tap, value):
            tap_grad_ref[tap : tap + 1, lanes] = value

        depthwise_weight(act, inner, lanes, batch, store)

        def emit(row, value):
            act[pl.ds(row, 8), lanes] = value

        depthwise(inner, taps_ref, lanes, batch, True, emit)

    loop(tile // LANES, conv)

    def deactivate(index):
        rows = rows_at(index, line)
        for part in range(tile // LANES):
            lanes = slice(part * LANES, (part + 1) * LANES)
            deep[rows, lanes] = (act[rows, lanes] * wide[rows, lanes]).astype(BF16)

    loop(MAP, deactivate)
    weight_grad_ref[:, :C0] = nn(deep[...].T, x_ref[...])


def adamw_values(master, first, second, average, grad):
    first = BETA_ONE * first + (1.0 - BETA_ONE) * grad
    second = BETA_TWO * second + (1.0 - BETA_TWO) * grad * grad
    ratio = first / (1.0 - BETA_ONE**STEP) / (jnp.sqrt(second / (1.0 - BETA_TWO**STEP)) + EPSILON)
    master = master - RATE * (ratio + DECAY * master)
    average = SMOOTH * average + (1.0 - SMOOTH) * master
    return (first, second, master, average, master.astype(BF16))


def adamw_kernel(widths, factor_ref, *refs):
    pieces = refs[: len(widths)]
    master, first, second, average = refs[len(widths) : len(widths) + 4]
    outs = refs[len(widths) + 4 : len(widths) + 9]
    factor = factor_ref[0]
    if len(widths) == 1:
        grad = pieces[0][...].astype(F32) * factor
    else:
        whole = refs[-1]
        begin = 0
        for piece, width in zip(pieces, widths):
            whole[:, begin : begin + width] = piece[:, :width].astype(F32)
            begin += width
        grad = whole[...] * factor
    values = adamw_values(master[...], first[...], second[...], average[...], grad)
    for out, value in zip(outs, values):
        out[...] = value


def adamw(factor, pieces, widths, master, first, second, average):
    height, width = master.shape
    rows = 72 if height % 72 == 0 else height
    specs = [pl.BlockSpec((rows, piece.shape[1]), lambda i: (i, 0)) for piece in pieces]
    full = pl.BlockSpec((rows, width), lambda i: (i, 0))
    types = (F32, F32, F32, F32, BF16)
    return pl.pallas_call(
        functools.partial(adamw_kernel, tuple(widths)),
        grid=(height // rows,),
        in_specs=[pl.BlockSpec(memory_space=pltpu.SMEM)] + specs + [full] * 4,
        out_specs=[full] * 5,
        out_shape=[jax.ShapeDtypeStruct((height, width), kind) for kind in types],
        scratch_shapes=[pltpu.VMEM((rows, width), F32)] if len(widths) > 1 else [],
        compiler_params=pltpu.CompilerParams(vmem_limit_bytes=VMEM_BYTES),
        name="adamw",
    )(factor, *pieces, master, first, second, average)


def swap(values, axis, distance):
    size = lax.axis_size(axis)
    return lax.ppermute(values, axis, [(i, i ^ distance) for i in range(size)])


def gather(values, axis):
    parts = [values] + [swap(values, axis, k) for k in range(1, lax.axis_size(axis))]
    return jnp.concatenate(parts, axis=0)


def scatter_sum(mine, axis):
    total = mine(0)
    for k in range(1, lax.axis_size(axis)):
        total = total + swap(mine(k).astype(BF16), axis, k).astype(F32)
    return total


def reduce_shard(own, far, rows):
    came = swap(far, "core", 1)
    deep = lax.axis_size("chan")

    def block(k):
        place = slice(k * deep * rows, (k + 1) * deep * rows)
        return own[place] + came[place]

    middle = scatter_sum(block, "xy")
    return scatter_sum(lambda k: middle[k * rows : (k + 1) * rows], "chan")


def total_sum(values):
    for axis in ("core", "xy", "chan"):
        distance = 1
        while distance < lax.axis_size(axis):
            values = values + swap(values, axis, distance)
            distance *= 2
    return values


def own_order(values, rows):
    place = lax.axis_index("xy")
    return [
        lax.dynamic_slice_in_dim(values, (place ^ k) * rows, rows, 0)
        for k in range(lax.axis_size("xy"))
    ]


def spread_back(shard):
    low = shard.astype(BF16)
    place = lax.axis_index("xy")
    size = lax.axis_size("xy")
    stack = gather(low, "xy").reshape(size, *low.shape)
    mine = jnp.concatenate(
        [lax.dynamic_index_in_dim(stack, place ^ k, 0, keepdims=False) for k in range(size)], 0
    )
    return mine, swap(mine, "core", 1)


def two_parts(values):
    upper = lax.reduce_precision(values, 8, 7)
    return [upper.astype(BF16), (values - upper).astype(BF16)]


def call(kernel, grid, ins, outs, scratch, name):
    def spec(shape, block, index):
        if block is None:
            return pl.BlockSpec(memory_space=pltpu.VMEM)
        return pl.BlockSpec(block, index)

    in_specs = []
    arrays = []
    for entry in ins:
        array, block, index, *mode = entry
        arrays.append(array)
        if mode:
            in_specs.append(pl.BlockSpec(block, index, pipeline_mode=mode[0]))
        else:
            in_specs.append(spec(array.shape, block, index))
    return pl.pallas_call(
        kernel,
        grid=grid,
        in_specs=in_specs,
        out_specs=[spec(shape, block, index) for shape, kind, block, index in outs],
        out_shape=[jax.ShapeDtypeStruct(shape, kind) for shape, kind, block, index in outs],
        scratch_shapes=scratch,
        compiler_params=pltpu.CompilerParams(
            vmem_limit_bytes=VMEM_BYTES, dimension_semantics=("arbitrary",) * len(grid)
        ),
        name=name,
    )(*arrays)


def on_device(
    images,
    labels,
    resolution,
    class_weight,
    column_master,
    column_first,
    column_second,
    column_average,
    row_master,
    row_first,
    row_second,
    row_average,
    head_master,
    head_first,
    head_second,
    head_average,
    route_master,
    route_first,
    route_second,
    route_average,
):
    chans, places = lax.axis_size("chan"), lax.axis_size("xy")
    core, place, layer = lax.axis_index("core"), lax.axis_index("xy"), lax.axis_index("chan")
    first_core = core == 0
    batch = images.shape[0] // chans
    slots = MAP * MAP
    rows = slots * batch
    wide = column_master.shape[1] * chans
    height = column_master.shape[1] // places
    begin = C0 + 2 * TAPS + SE
    tile = 3 * LANES
    tiles = wide // tile

    def fixed(array):
        return (array, None, None)

    def whole(array, grid=1):
        zeros = (0,) * array.ndim
        return (array, array.shape, lambda *ids: zeros, pl.Buffered(1))

    column, row = column_master.T, row_master
    column_parts = [column[:, :C0]]
    column_parts += two_parts(column[:, C0 : C0 + 2 * TAPS])
    small_left = jnp.concatenate([part.astype(BF16) for part in column_parts], 1)
    small_left = jnp.pad(small_left, ((0, 0), (0, 2 * C0 - small_left.shape[1])))
    small_right = jnp.concatenate(
        [row[:, :C0].astype(BF16)]
        + two_parts(column[:, C0 + 2 * TAPS : begin])
        + two_parts(row[:, C0 : C0 + SE]),
        1,
    )
    small = jnp.concatenate(own_order(jnp.where(first_core, small_left, small_right), height), 0)
    small = gather(small, "chan").reshape(chans, places, height, 2 * C0)
    small = small.transpose(1, 0, 2, 3).reshape(wide, 2 * C0)
    small_far = swap(small, "core", 1)
    left = jnp.where(first_core, small, small_far)
    right = jnp.where(first_core, small_far, small)

    expand_own = lax.dynamic_slice(
        column, (place * height, begin + core * HALF * C0), (height, HALF * C0)
    ).astype(BF16)
    expand_own = gather(gather(expand_own, "chan"), "xy")
    expand_far = swap(expand_own, "core", 1)
    project_own = lax.dynamic_slice(
        row, (place * height, C0 + SE + core * HALF * C2), (height, HALF * C2)
    ).astype(BF16)
    project_own = gather(gather(project_own, "chan"), "xy")
    project_far = swap(project_own, "core", 1)
    head_own = gather(gather(head_master.T.astype(BF16), "chan"), "xy")
    head_far = swap(head_own, "core", 1)

    def both(values, at, width):
        upper = values[:, at : at + width].astype(F32)
        return upper + values[:, at + width : at + 2 * width].astype(F32)

    def tap_rows(values):
        return jnp.broadcast_to(values.T[:, None, :], (TAPS, 8, wide))

    taps = both(left, C0, 2 * TAPS)
    first_taps, second_taps = tap_rows(taps[:, :TAPS]), tap_rows(taps[:, TAPS:])
    excite_out = both(right, C0, SE)
    excite_in = both(right, C0 + 2 * SE, SE)
    route_in, route_out = route_master[:C0], route_master[C0:]
    route_in = jnp.where(first_core, route_in, jnp.roll(route_in, HALF, axis=1))

    mine = lax.all_to_all(images, "chan", 0, 0, tiled=True)
    mine = mine.reshape(chans, batch, slots // chans, C0).transpose(0, 2, 1, 3)
    label = lax.dynamic_slice_in_dim(labels, layer * batch, batch, 0)
    side = lax.dynamic_slice_in_dim(resolution, layer * batch, batch, 0)
    spots = jnp.arange(slots, dtype=jnp.int32)
    inside = ((spots // MAP)[:, None] < side[None, :]) & ((spots % MAP)[:, None] < side[None, :])
    inside = inside.reshape(rows, 1)
    x = jnp.where(inside, mine.reshape(rows, C0), 0)
    mask = jnp.broadcast_to(inside.astype(F32), (rows, LANES))
    count = jnp.broadcast_to((side * side).astype(F32)[:, None], (batch, LANES))

    def tiled(array):
        return (array, (tile, array.shape[1]), lambda i: (i, 0))

    def across(array):
        return (array, (array.shape[0], tile), lambda i: (0, i))

    def tap_tile(array):
        return (array, (TAPS, 8, tile), lambda i: (0, 0, i))

    def out_full(shape, kind):
        zeros = (0,) * len(shape)
        return (shape, kind, shape, lambda *ids: zeros)

    def out_across(height_, kind):
        return ((height_, wide), kind, (height_, tile), lambda i: (0, i))

    def out_tiled(width, kind):
        return ((wide, width), kind, (tile, width), lambda i: (i, 0))

    conv_one, mixed_in, twice_one, mean_one, gate_one, gates_one, gates_mid = call(
        first_forward,
        (tiles,),
        [
            whole(x), tiled(left), tiled(right), tap_tile(first_taps), whole(mask), whole(count),
            whole(route_in),
        ],
        [
            out_across(rows, F32),
            out_full((rows, NE * C0), BF16),
            out_full((rows, 2 * C0), BF16),
            out_full((batch, C0), F32),
            out_full((batch, NE), F32),
            out_full((HALF, batch, 2 * C0), F32),
            out_full((HALF, batch, 2 * C2), F32),
        ],
        [
            pltpu.VMEM((rows, tile), F32), pltpu.VMEM((rows, tile), BF16),
            pltpu.VMEM((rows, C0), F32),
        ],
        "first_forward",
    )

    mixed_two, conv_two, mean_two, units, scale = call(
        second_forward,
        (tiles,),
        [
            whole(mixed_in), tiled(expand_own), tiled(expand_far), tap_tile(second_taps),
            whole(mask), whole(count), tiled(excite_in), whole(excite_out),
        ],
        [
            out_across(rows, F32),
            out_across(rows, F32),
            out_across(batch, F32),
            out_full((batch, SE), F32),
            out_full((batch, wide), F32),
        ],
        [pltpu.VMEM((rows, tile), F32)],
        "second_forward",
    )

    each, twice_two, mixed_head, mean_three, gate_two, gates_two = call(
        project,
        (),
        [
            fixed(conv_two), fixed(scale), fixed(project_own), fixed(project_far), fixed(mask),
            fixed(count), fixed(gates_mid), fixed(route_out),
        ],
        [
            ((rows, NE * C2), BF16, None, None),
            ((rows, 2 * C2), BF16, None, None),
            ((rows, NE * C2), BF16, None, None),
            ((batch, C2), F32, None, None),
            ((batch, NE), F32, None, None),
            ((HALF, batch, 2 * C2), F32, None, None),
        ],
        [pltpu.VMEM((rows, wide), BF16)],
        "project",
    )

    half = head_own.shape[0]
    blocks = 5
    part = NE * C2 // blocks
    expert_grad, class_grad, losses, hidden_two, route_grad_out = call(
        head,
        (2 * blocks,),
        [
            whole(mixed_head), whole(twice_two), whole(head_own), whole(head_far), whole(mask),
            whole(count), whole(label[:, None]), whole(class_weight[None, :]), whole(gates_two),
            whole(gate_two), whole(mean_three), whole(route_out),
        ],
        [
            (
                (2, half, NE * C2), F32, (1, half, part),
                lambda i: (1 - i // blocks, 0, i % blocks),
            ),
            out_full((2, half, CLASSES), F32),
            out_full((batch, 2), F32),
            out_full((rows, 2 * C2), BF16),
            out_full((C2, NE), F32),
        ],
        [
            pltpu.VMEM((rows, 2 * half), F32), pltpu.VMEM((rows, 2 * half), BF16),
            pltpu.VMEM((2 * half, rows), BF16), pltpu.VMEM((batch, 2 * half), F32),
            pltpu.VMEM((rows, C2), F32),
        ],
        "head",
    )
    rows_head = head_master.shape[1]
    expert_shard = reduce_shard(expert_grad[0], expert_grad[1], rows_head)
    class_shard = reduce_shard(class_grad[0], class_grad[1], rows_head)

    deep_grad, project_grad_own, project_grad_far, gate_sums, unit_grad, excite_grad = call(
        project_back,
        (tiles,),
        [
            whole(hidden_two), whole(gates_mid), whole(each), tiled(project_own),
            tiled(project_far), across(conv_two), across(scale), whole(mask), whole(scale),
            whole(units), whole(mean_two), whole(excite_out),
        ],
        [
            out_across(rows, F32),
            out_tiled(HALF * C2, F32),
            out_tiled(HALF * C2, F32),
            out_full((HALF, batch, 2 * C2), F32),
            out_full((batch, SE), F32),
            out_full((wide, 2 * SE), F32),
        ],
        [
            pltpu.VMEM((rows, NE * C2), BF16), pltpu.VMEM((rows, tile), BF16),
            pltpu.VMEM((batch, wide), F32),
        ],
        "project_back",
    )
    project_shard = reduce_shard(project_grad_own, project_grad_far, height)

    expand_grad_own, expand_grad_far, tap_grad_two, hidden_one, route_grad_in = call(
        second_back,
        (tiles,),
        [
            across(deep_grad), across(scale), whole(unit_grad), tiled(excite_in), whole(count),
            whole(mask), across(conv_two), across(mixed_two), tap_tile(second_taps),
            whole(mixed_in), tiled(expand_own), tiled(expand_far), whole(twice_one),
            whole(gates_one), whole(gate_one), whole(gate_sums), whole(route_in), whole(mean_one),
        ],
        [
            out_tiled(HALF * C0, F32),
            out_tiled(HALF * C0, F32),
            out_across(TAPS, F32),
            out_full((rows, C0), BF16),
            out_full((C0, NE), F32),
        ],
        [
            pltpu.VMEM((rows, tile), F32), pltpu.VMEM((rows, tile), F32),
            pltpu.VMEM((rows, wide), BF16), pltpu.VMEM((wide, HALF * C0), BF16),
            pltpu.VMEM((wide, HALF * C0), BF16),
        ],
        "second_back",
    )
    expand_shard = reduce_shard(expand_grad_own, expand_grad_far, height)

    weight_grad, tap_grad_one = call(
        first_back,
        (tiles,),
        [
            whole(x), tiled(left), tiled(right), tap_tile(first_taps), whole(mask),
            across(conv_one), whole(hidden_one),
        ],
        [out_tiled(2 * C0, F32), out_across(TAPS, F32)],
        [
            pltpu.VMEM((rows, tile), F32), pltpu.VMEM((rows, tile), F32),
            pltpu.VMEM((rows, tile), F32), pltpu.VMEM((rows, tile), BF16),
        ],
        "first_back",
    )
    small_width = C0 + 2 * SE
    tap_grads = jnp.concatenate([tap_grad_one, tap_grad_two], 0).T
    left_grad = jnp.concatenate([weight_grad[:, :C0], tap_grads], 1)
    left_grad = jnp.pad(left_grad, ((0, 0), (0, small_width - left_grad.shape[1])))
    right_grad = jnp.concatenate([weight_grad[:, C0:], excite_grad], 1)
    small_shard = reduce_shard(
        jnp.where(first_core, left_grad, right_grad),
        jnp.where(first_core, right_grad, left_grad),
        height,
    )

    shards = (expert_shard, class_shard, project_shard, expand_shard, small_shard)
    squares = sum(jnp.sum(shard * shard) for shard in shards)
    route_grad_in = jnp.where(first_core, route_grad_in, jnp.roll(route_grad_in, HALF, axis=1))
    route_grad = jnp.concatenate([route_grad_in, route_grad_out], 0)
    scalars = jnp.concatenate([squares[None], jnp.sum(losses, 0)])
    packed = jnp.concatenate([route_grad.reshape(-1, LANES), jnp.pad(scalars, (0, LANES - 3))[None]])
    packed = total_sum(packed)
    route_sum = packed[:-1].reshape(route_grad.shape)
    square_sum, loss_total, weight_total = packed[-1, 0], packed[-1, 1], packed[-1, 2]
    clip_norm = jnp.sqrt(square_sum + jnp.sum(route_sum * route_sum)) / weight_total
    factor = jnp.minimum(1.0, CLIP / (clip_norm + 1e-06)) / weight_total
    scalar = factor[None]

    project_mine, project_other = spread_back(project_shard)
    expand_mine, expand_other = spread_back(expand_shard)
    small_mine, small_other = spread_back(small_shard)

    def ordered(mine_, other):
        return jnp.where(first_core, mine_, other), jnp.where(first_core, other, mine_)

    project_low, project_up = ordered(project_mine, project_other)
    expand_low, expand_up = ordered(expand_mine, expand_other)
    small_low, small_up = ordered(small_mine, small_other)
    squeeze_grad = small_up[:, C0 + SE :]
    column_out = adamw(
        scalar,
        [small_low, small_up[:, C0 : C0 + SE], expand_low, expand_up],
        [C0 + 2 * TAPS, SE, HALF * C0, HALF * C0],
        column,
        column_first.T,
        column_second.T,
        column_average.T,
    )
    row_out = adamw(
        scalar,
        [small_up, squeeze_grad, project_low, project_up],
        [C0, SE, HALF * C2, HALF * C2],
        row_master,
        row_first,
        row_second,
        row_average,
    )
    head_out = adamw(
        scalar,
        [expert_shard, class_shard],
        [NE * C2, CLASSES],
        head_master.T,
        head_first.T,
        head_second.T,
        head_average.T,
    )
    route_out_new = adamw_values(
        route_master, route_first, route_second, route_average, route_sum * factor
    )
    return (
        *[value.T for value in column_out],
        *row_out,
        *[value.T for value in head_out],
        *route_out_new,
        loss_total,
        weight_total,
        clip_norm,
    )


def solution(mesh):
    groups = mesh.devices.shape[0] // 2
    fine = Mesh(
        mesh.devices.reshape(groups, 2, mesh.devices.shape[1]), ("xy", "core", "chan")
    )
    dp = ("xy", "core")
    every = ("xy", "core", "chan")
    column, row, head_spec = P(None, "chan"), P("chan", None), P(None, every)
    return jax.shard_map(
        on_device,
        mesh=fine,
        in_specs=(P(dp, "chan", None), P(dp), P(dp), P())
        + (column,) * 4
        + (row,) * 4
        + (head_spec,) * 4
        + (P(),) * 4,
        out_specs=(column,) * 5 + (row,) * 5 + (head_spec,) * 5 + (P(),) * 8,
        check_vma=False,
    )
```

time: 2390 us -> 758 us (0.32)
  matrix products: 775 us -> 0 us
  other arithmetic: 571 us -> 58.3 us
  waiting for transfers between devices: 737 us -> 274 us
  Pallas kernels: 0 us -> 241 us
  blocking collectives: 136 us -> 0 us
  starting transfers between devices: 0.63 us -> 74.7 us
  local copies, waits for them, and re-layouts: 135 us -> 91.1 us
    dot_general x36 -> x0, matrix products: 775 us -> none  [the longest x2 200 us: second_expand(): mixed = jnp.einsum('bpef,be->bpf', expanded, gating, precision=HIGH)]
    reduce_scatter x4 -> x0, waiting for transfers between devices: 559 us -> none  [the longest x1 392 us: on_device(): lax.psum_scatter(head_grad, ('dp', 'chan'), scatter_dimension=1, tiled=True)]
    ppermute x0 -> x77, waiting for transfers between devices: none -> 274 us  [swap(): return lax.ppermute(values, axis, [(i, i ^ distance) for i in range(size)])]
    reduce_sum x12 -> x3, other arithmetic: 244 us -> 2.8 us  [the longest x2 2.78 us: on_device(): squares = sum((jnp.sum(shard * shard) for shard in shards))]
    pallas_call x0 -> x10, Pallas kernels: none -> 241 us  [the longest x7 218 us: call(): pl.pallas_call(kernel, grid=grid, in_specs=in_specs, out_specs=[spec(shap...]
    all_gather x5 -> x0, waiting for transfers between devices: 138 us -> none  [the longest x2 88.1 us: gather_grads(): lax.all_gather(values.astype(jnp.bfloat16), 'chan', axis=1, tiled=True)]
    psum x8 -> x0, blocking collectives: 136 us -> none  [the longest x7 96.7 us: chan_total(): return lax.psum(values, 'chan')]
    add_any x7 -> x0, other arithmetic: 117 us -> none  [the longest x2 90.6 us: depthwise(): padded[:, down_step:down_step + MAP, side_step:side_step + MAP, :]]
  transfers between devices with their start and end apart: 10 -> 78, of which waited for: 8 -> 37; matrix products, arithmetic and copies ran while one was open for 23% -> 18% of each run, Pallas kernels for 0% -> 10%
where the time goes in v1:
time: 758 us; the launch traced here: 748 us
  waiting for transfers between devices  274 us (36%)
  Pallas kernels  241 us (32%)
  local copies, waits for them, and re-layouts  91.1 us (12%)
  starting transfers between devices  74.7 us (10%)
  other arithmetic  58.3 us (8%)
  between operations  8.93 us (1%)
    ppermute x77, waiting for transfers between devices, swap(): return lax.ppermute(values, axis, [(i, i ^ distance) for i in range(size)])  274 us
    pallas_call x7, Pallas kernels, call(): pl.pallas_call(kernel, grid=grid, in_specs=in_specs, out_specs=[spec(shap...  218 us
    ppermute x77, starting transfers between devices, swap(): return lax.ppermute(values, axis, [(i, i ^ distance) for i in range(size)])  70.5 us
    unnamed x86, local copies, waits for them, and re-layouts  33.2 us
    pallas_call x3, Pallas kernels, adamw(): pl.pallas_call(functools.partial(adamw_kernel, tuple(widths)), grid=(heig...  23.8 us
  transfers between devices with their start and end apart: 78, of which 37 were waited for; matrix products, arithmetic and copies ran while one was open for 18% of the time, Pallas kernels for 10%

profile of v1, /device:TPU:0, one launch (start us, length us, event | category | flops | bytes accessed | tf_op | source)
XLA Modules:
  0.0 747.8 jit_solution(5602418452633460766)
XLA Ops:
  2.5 5.0 collective-permute-start.6
  9.9 3.8 collective-permute-start.13
  13.7 4.2 all-to-all-start
  40.9 2.4 collective-permute-start.20
  45.2 7.1 collective-permute-done.11
  52.3 3.1 collective-permute-start.1
  57.5 16.9 %collective-permute-done.19 = bf16[40,3560]{1,0:T(8,128)(2,1)S(1)} collective-permute-done((bf16[40,3560]{1,0:T(8,128)(2,1)S(1)}, bf16[40,3560]{1,0:T(8,128)(2,1)S(1)}, u32[]{:S(2)}, u32[]{:S(2)}) %collective-permute-start.19) | collective-permute-done | bytes 284832 | tf_op jit(solution)/shard_map/ppermute | solution.py:742
  74.5 2.5 collective-permute-start.23
  80.3 45.2 %collective-permute-done.21 = bf16[160,3560]{1,0:T(8,128)(2,1)S(1)} collective-permute-done((bf16[160,3560]{1,0:T(8,128)(2,1)S(1)}, bf16[160,3560]{1,0:T(8,128)(2,1)S(1)}, u32[]{:S(2)}, u32[]{:S(2)}) %collective-permute-start.21) | collective-permute-done | bytes 1139232 | tf_op jit(solution)/shard_map/ppermute | solution.py:742
  130.8 7.2 copy.169
  139.9 2.4 collective-permute-start.2
  147.1 2.7 collective-permute-done.2
  151.9 2.2 copy.163
  158.5 5.9 collective-permute-done.16
  164.5 18.2 %collective-permute-done.7 = bf16[288,768]{1,0:T(8,128)(2,1)S(1)} collective-permute-done((bf16[288,768]{1,0:T(8,128)(2,1)S(1)}, bf16[288,768]{1,0:T(8,128)(2,1)S(1)}, u32[]{:S(2)}, u32[]{:S(2)}) %collective-permute-start.7) | collective-permute-done | bytes 442400 | tf_op jit(solution)/shard_map/ppermute | solution.py:742
  190.9 2.5 broadcast_select_fusion
  200.1 20.6 %first_forward.1 = (f32[1024,1152]{1,0:T(8,128)}, bf16[1024,1536]{1,0:T(8,128)(2,1)}, bf16[1024,384]{1,0:T(8,128)(2,1)}, f32[16,192]{1,0:T(8,128)}, f32[16,8]{1,...) custom-call(bf16[1024,192]{1,0:T(8,128)(2,1)} %bitcast_select_fusion.x_ref, bf16[1152,384]{1,0:T(8,128)(2,1)} %copy-done.4, ...), custom_call_target="tpu_custom_call" | custom-call | tf_op jit(solution)/shard_map/first_forward/pallas_call | solution.py:817
  223.1 22.3 %second_forward.1 = (f32[1024,1152]{1,0:T(8,128)}, f32[1024,1152]{1,0:T(8,128)}, f32[16,1152]{1,0:T(8,128)}, f32[16,48]{1,0:T(8,128)}, f32[16,1152]{1,0:T(8,128)}) custom-call(bf16[1024,1536]{1,0:T(8,128)(2,1)} %get-tuple-element.74.wide_ref, bf16[1152,768]{1,0:T(8,128)(2,1)} %constant_dynamic-update-slice_fusion.7.own_ref, ...), custom_call_target="tpu_custom_call" | custom-call | tf_op jit(solution)/shard_map/second_forward/pallas_call | solution.py:817
  245.4 20.7 %project.1 = (bf16[1024,2560]{1,0:T(8,128)(2,1)}, bf16[1024,640]{1,0:T(8,128)(2,1)}, bf16[1024,2560]{1,0:T(8,128)(2,1)}, f32[16,320]{1,0:T(8,128)}, f32[16,8]{1,0:T(8,128)}, /*index=5*/f32[4,16,640]{2,1,0:T(8,128)}) custom-call(f32[1024,1152]{1,0:T(8,128)} %get-tuple-element.75.conv_ref, f32[16,1152]{1,0:T(8,128)} %get-tuple-element.76.scale_ref.full_scale_ref, ...), custom_call_target="tpu_custom_call" | custom-call | tf_op jit(solution)/shard_map/project/pallas_call | solution.py:817
  266.1 7.8 %copy.170.far_ref = bf16[640,3560]{1,0:T(8,128)(2,1)} copy(bf16[640,3560]{0,1:T(8,128)(2,1)} %collective-permute-done.24) | data formatting | bytes 9113600 | tf_op jit(solution)/shard_map/ppermute | solution.py:742
  273.9 47.0 %head.1 = (f32[2,640,2560]{2,1,0:T(8,128)}, f32[2,640,1000]{2,1,0:T(8,128)}, f32[16,2]{1,0:T(8,128)}, bf16[1024,640]{1,0:T(8,128)(2,1)}, f32[320,8]{1,0:T(8,128)}) custom-call(bf16[1024,2560]{1,0:T(8,128)(2,1)} %get-tuple-element.78.wide_ref, bf16[1024,640]{1,0:T(8,128)(2,1)} %get-tuple-element.79.twice_ref, ...), custom_call_target="tpu_custom_call" | custom-call | tf_op jit(solution)/shard_map/head/pallas_call | solution.py:817
  320.9 29.3 %project_back.1 = (f32[1024,1152]{1,0:T(8,128)}, f32[1152,1280]{1,0:T(8,128)}, f32[1152,1280]{1,0:T(8,128)}, f32[4,16,640]{2,1,0:T(8,128)}, f32[16,48]{1,0:T(8,128)}, /*index=5*/f32[1152,96]{1,0:T(8,128)}) custom-call(bf16[1024,640]{1,0:T(8,128)(2,1)} %get-tuple-element.83.hidden_ref, f32[4,16,640]{2,1,0:T(8,128)} %get-tuple-element.77.gates_ref, ...), custom_call_target="tpu_custom_call" | custom-call | tf_op jit(solution)/shard_map/project_back/pallas_call | solution.py:817
  350.2 43.6 %second_back.1 = (f32[1152,768]{1,0:T(8,128)}, f32[1152,768]{1,0:T(8,128)}, f32[25,1152]{1,0:T(8,128)}, bf16[1024,192]{1,0:T(8,128)(2,1)}, f32[192,8]{1,0:T(8,128)}) custom-call(f32[1024,1152]{1,0:T(8,128)} %get-tuple-element.87.grad_ref, f32[16,1152]{1,0:T(8,128)} %get-tuple-element.76.scale_ref.full_scale_ref, f32[16,48]{1,0:T(8,128)} %get-tuple-element.88.unit_grad_ref, ...), custom_call_target="tpu_custom_call" | custom-call | tf_op jit(solution)/shard_map/second_back/pallas_call | solution.py:817
  393.8 34.1 %first_back.1 = (f32[1152,384]{1,0:T(8,128)}, f32[25,1152]{1,0:T(8,128)}) custom-call(bf16[1024,192]{1,0:T(8,128)(2,1)} %bitcast_select_fusion.x_ref, bf16[1152,384]{1,0:T(8,128)(2,1)} %copy-done.4, bf16[1152,384]{1,0:T(8,128)(2,1)} %get-tuple-element.259.right_ref, f32[25,8,1152]{2,1,0:T(8,128)} %broadcast_in_dim.56.taps_ref, ...), custom_call_target="tpu_custom_call" | custom-call | tf_op jit(solution)/shard_map/first_back/pallas_call | solution.py:817
  436.4 2.3 copy.172
  439.8 6.0 slice_bitcast_fusion
  445.9 2.7 fusion.76
  452.9 7.2 collective-permute-done.54
  460.6 7.4 collective-permute-done.56
  468.7 5.5 collective-permute-done.55
  475.4 4.1 collective-permute-done.57
  481.1 4.5 collective-permute-done.59
  485.6 5.1 collective-permute-done.58
  491.8 4.9 collective-permute-done.67
  497.0 3.9 collective-permute-done.66
  502.1 2.9 collective-permute-done.65
  505.8 4.5 fusion.74
  510.3 2.4 copy.189
  515.2 2.8 fusion.22
  521.8 3.5 fusion.16
  525.3 3.4 collective-permute-done.33
  529.2 6.1 collective-permute-done.35
  542.0 3.1 collective-permute-done.47
  545.1 8.9 %collective-permute-done.49 = bf16[288,768]{1,0:T(8,128)(2,1)} collective-permute-done((bf16[288,768]{1,0:T(8,128)(2,1)S(1)}, bf16[288,768]{1,0:T(8,128)(2,1)}, u32[]{:S(2)}, u32[]{:S(2)}) %collective-permute-start.49) | collective-permute-done | bytes 442400 | tf_op jit(solution)/shard_map/ppermute | solution.py:742
  554.0 3.9 collective-permute-done.48
  563.4 4.9 collective-permute-done.50
  570.0 5.1 collective-permute-done.51
  585.4 2.9 fusion.8
  591.8 4.5 fusion.2
  597.9 9.7 %collective-permute-done.40 = bf16[288,1280]{1,0:T(8,128)(2,1)S(1)} collective-permute-done((bf16[288,1280]{1,0:T(8,128)(2,1)S(1)}, bf16[288,1280]{1,0:T(8,128)(2,1)S(1)}, u32[]{:S(2)}, u32[]{:S(2)}) %collective-permute-start.40) | collective-permute-done | bytes 737312 | tf_op jit(solution)/shard_map/ppermute | solution.py:742
  609.0 15.0 %collective-permute-done.42 = bf16[288,1280]{1,0:T(8,128)(2,1)S(1)} collective-permute-done((bf16[288,1280]{1,0:T(8,128)(2,1)S(1)}, bf16[288,1280]{1,0:T(8,128)(2,1)S(1)}, u32[]{:S(2)}, u32[]{:S(2)}) %collective-permute-start.42) | collective-permute-done | bytes 737312 | tf_op jit(solution)/shard_map/ppermute | solution.py:742
  626.9 14.1 %collective-permute-done.26 = bf16[160,2560]{1,0:T(8,128)(2,1)S(1)} collective-permute-done((bf16[160,2560]{1,0:T(8,128)(2,1)S(1)}, bf16[160,2560]{1,0:T(8,128)(2,1)S(1)}, u32[]{:S(2)}, u32[]{:S(2)}) %collective-permute-start.26) | collective-permute-done | bytes 819232 | tf_op jit(solution)/shard_map/ppermute | solution.py:742
  641.0 17.8 %collective-permute-done.28 = bf16[160,2560]{1,0:T(8,128)(2,1)S(1)} collective-permute-done((bf16[160,2560]{1,0:T(8,128)(2,1)S(1)}, bf16[160,2560]{1,0:T(8,128)(2,1)S(1)}, u32[]{:S(2)}, u32[]{:S(2)}) %collective-permute-start.28) | collective-permute-done | bytes 819232 | tf_op jit(solution)/shard_map/ppermute | solution.py:742
  661.0 2.6 fusion.71
  663.7 2.2 collective-permute-start.31
  668.7 7.9 %collective-permute-done.29 = bf16[40,2560]{1,0:T(8,128)(2,1)S(1)} collective-permute-done((bf16[40,2560]{1,0:T(8,128)(2,1)S(1)}, bf16[40,2560]{1,0:T(8,128)(2,1)S(1)}, u32[]{:S(2)}, u32[]{:S(2)}) %collective-permute-start.29) | collective-permute-done | bytes 204832 | tf_op jit(solution)/shard_map/ppermute | solution.py:742
  676.6 8.8 %collective-permute-done.30 = bf16[40,2560]{1,0:T(8,128)(2,1)S(1)} collective-permute-done((bf16[40,2560]{1,0:T(8,128)(2,1)S(1)}, bf16[40,2560]{1,0:T(8,128)(2,1)S(1)}, u32[]{:S(2)}, u32[]{:S(2)}) %collective-permute-start.30) | collective-permute-done | bytes 204832 | tf_op jit(solution)/shard_map/ppermute | solution.py:742
  697.1 5.9 collective-permute-done.61
  704.0 2.8 collective-permute-done.62
  707.2 3.7 collective-permute-done.63
  711.0 4.5 collective-permute-done.64
  719.8 3.8 adamw.5
  723.6 8.6 %adamw.3 = (f32[288,1826]{1,0:T(8,128)}, f32[288,1826]{1,0:T(8,128)}, f32[288,1826]{1,0:T(8,128)}, f32[288,1826]{1,0:T(8,128)}, bf16[288,1826]{1,0:T(8,128)(2,1)}) custom-call(f32[1]{0:T(128)} %bitcast.28.factor_ref, bf16[288,288]{1,0:T(8,128)(2,1)} %get-tuple-element.292.refs_0_, bf16[288,48]{1,0:T(8,128)(2,1)} %get-tuple-element.300.refs_1_, ...), custom_call_target="tpu_custom_call" | custom-call | tf_op jit(solution)/shard_map/adamw/pallas_call | solution.py:728
  734.9 11.4 %adamw.4 = (f32[288,2800]{1,0:T(8,128)}, f32[288,2800]{1,0:T(8,128)}, f32[288,2800]{1,0:T(8,128)}, f32[288,2800]{1,0:T(8,128)}, bf16[288,2800]{1,0:T(8,128)(2,1)}) custom-call(f32[1]{0:T(128)} %bitcast.28.factor_ref, bf16[288,288]{1,0:T(8,128)(2,1)} %copy-done.8, bf16[288,48]{1,0:T(8,128)(2,1)} %get-tuple-element.299.refs_1_, ...), custom_call_target="tpu_custom_call" | custom-call | tf_op jit(solution)/shard_map/adamw/pallas_call | solution.py:728
  (297 shorter events, 150.9 us)
Async XLA Ops:
  2.5 38.4 %collective-permute-start.6 = (bf16[72,768]{1,0:T(8,128)(2,1)}, bf16[72,768]{1,0:T(8,128)(2,1)}, u32[]{:S(2)}, u32[]{:S(2)}) collective-permute-start(bf16[72,768]{1,0:T(8,128)(2,1)} %get-tuple-element.217), channel_id=1, source_target_pairs={{0,3},{1,2},{2,1},{3,0},{4,7},{5,6},{6,5},{7,4},{8,11},{9,10},{10,... | collective-permute-start | bytes 331784 | tf_op jit(solution)/shard_map/ppermute | solution.py:742
  7.5 35.7 %collective-permute-start.5 = (bf16[72,768]{1,0:T(8,128)(2,1)}, bf16[72,768]{1,0:T(8,128)(2,1)}, u32[]{:S(2)}, u32[]{:S(2)}) collective-permute-start(bf16[72,768]{1,0:T(8,128)(2,1)} %get-tuple-element.217), channel_id=1, source_target_pairs={{0,2},{1,3},{2,0},{3,1},{4,6},{5,7},{6,4},{7,5},{8,10},{9,11},{10,... | collective-permute-start | bytes 331784 | tf_op jit(solution)/shard_map/ppermute | solution.py:742
  7.6 29.7 %collective-permute-start.4 = (bf16[72,768]{1,0:T(8,128)(2,1)}, bf16[72,768]{1,0:T(8,128)(2,1)}, u32[]{:S(2)}, u32[]{:S(2)}) collective-permute-start(bf16[72,768]{1,0:T(8,128)(2,1)} %get-tuple-element.217), channel_id=1, source_target_pairs={{0,1},{1,0},{2,3},{3,2},{4,5},{5,4},{6,7},{7,6},{8,9},{9,8},{10,11... | collective-permute-start | bytes 331784 | tf_op jit(solution)/shard_map/ppermute | solution.py:742
  9.9 42.4 %collective-permute-start.13 = (bf16[72,1280]{1,0:T(8,128)(2,1)}, bf16[72,1280]{1,0:T(8,128)(2,1)}, u32[]{:S(2)}, u32[]{:S(2)}) collective-permute-start(bf16[72,1280]{1,0:T(8,128)(2,1)} %get-tuple-element.215), channel_id=1, source_target_pairs={{0,3},{1,2},{2,1},{3,0},{4,7},{5,6},{6,5},{7,4},{8,11},{9,10},{10,... | collective-permute-start | bytes 552968 | tf_op jit(solution)/shard_map/ppermute | solution.py:742
  13.7 41.8 %collective-permute-start.12 = (bf16[72,1280]{1,0:T(8,128)(2,1)}, bf16[72,1280]{1,0:T(8,128)(2,1)}, u32[]{:S(2)}, u32[]{:S(2)}) collective-permute-start(bf16[72,1280]{1,0:T(8,128)(2,1)} %get-tuple-element.215), channel_id=1, source_target_pairs={{0,2},{1,3},{2,0},{3,1},{4,6},{5,7},{6,4},{7,5},{8,10},{9,11},{10,... | collective-permute-start | bytes 552968 | tf_op jit(solution)/shard_map/ppermute | solution.py:742
  13.7 175.0 %all-to-all-start = ((bf16[64,16,192]{2,1,0:T(8,128)(2,1)}), bf16[64,16,192]{2,1,0:T(8,128)(2,1)}, u32[]{:S(2)}, u32[]{:S(2)}) async-start(bf16[64,16,192]{2,1,0:T(8,128)(2,1)} %param.20), calls=%async_computation | async-start | bytes 1048576 | tf_op jit(solution)/shard_map/all_to_all | solution.py:917
  37.3 15.1 %collective-permute-start.11 = (bf16[72,1280]{1,0:T(8,128)(2,1)}, bf16[72,1280]{1,0:T(8,128)(2,1)S(1)}, u32[]{:S(2)}, u32[]{:S(2)}) collective-permute-start(bf16[72,1280]{1,0:T(8,128)(2,1)} %get-tuple-element.215), channel_id=1, source_target_pairs={{0,1},{1,0},{2,3},{3,2},{4,5},{5,4},{6,7},{7,6},{8,9},{9,8},{10,11... | collective-permute-start | bytes 552968 | tf_op jit(solution)/shard_map/ppermute | solution.py:742
  40.9 16.6 %collective-permute-start.20 = (bf16[40,3560]{1,0:T(8,128)(2,1)S(1)}, bf16[40,3560]{1,0:T(8,128)(2,1)S(1)}, u32[]{:S(2)}, u32[]{:S(2)}) collective-permute-start(bf16[40,3560]{1,0:T(8,128)(2,1)S(1)} %get-tuple-element.213), channel_id=1, source_target_pairs={{0,3},{1,2},{2,1},{3,0},{4,7},{5,6},{6,5},{7,4},{8,11},{9,10},{10,... | collective-permute-start | bytes 854408 | tf_op jit(solution)/shard_map/ppermute | solution.py:742
  43.2 31.1 %collective-permute-start.19 = (bf16[40,3560]{1,0:T(8,128)(2,1)S(1)}, bf16[40,3560]{1,0:T(8,128)(2,1)S(1)}, u32[]{:S(2)}, u32[]{:S(2)}) collective-permute-start(bf16[40,3560]{1,0:T(8,128)(2,1)S(1)} %get-tuple-element.213), channel_id=1, source_target_pairs={{0,2},{1,3},{2,0},{3,1},{4,6},{5,7},{6,4},{7,5},{8,10},{9,11},{10,... | collective-permute-start | bytes 854408 | tf_op jit(solution)/shard_map/ppermute | solution.py:742
  52.3 22.1 %collective-permute-start.18 = (bf16[40,3560]{1,0:T(8,128)(2,1)S(1)}, bf16[40,3560]{1,0:T(8,128)(2,1)S(1)}, u32[]{:S(2)}, u32[]{:S(2)}) collective-permute-start(bf16[40,3560]{1,0:T(8,128)(2,1)S(1)} %get-tuple-element.213), channel_id=1, source_target_pairs={{0,1},{1,0},{2,3},{3,2},{4,5},{5,4},{6,7},{7,6},{8,9},{9,8},{10,11... | collective-permute-start | bytes 854408 | tf_op jit(solution)/shard_map/ppermute | solution.py:742
  52.3 91.6 %collective-permute-start.1 = (bf16[288,384]{1,0:T(8,128)(2,1)S(1)}, bf16[288,384]{1,0:T(8,128)(2,1)}, u32[]{:S(2)}, u32[]{:S(2)}) collective-permute-start(bf16[288,384]{1,0:T(8,128)(2,1)S(1)} %pad_maximum_fusion.9), channel_id=1, source_target_pairs={{0,2},{1,3},{2,0},{3,1},{4,6},{5,7},{6,4},{7,5},{8,10},{9,11},{10,... | collective-permute-start | bytes 663560 | tf_op jit(solution)/shard_map/ppermute | solution.py:742
  55.5 84.4 %collective-permute-start = (bf16[288,384]{1,0:T(8,128)(2,1)S(1)}, bf16[288,384]{1,0:T(8,128)(2,1)}, u32[]{:S(2)}, u32[]{:S(2)}) collective-permute-start(bf16[288,384]{1,0:T(8,128)(2,1)S(1)} %pad_maximum_fusion.9), channel_id=1, source_target_pairs={{0,1},{1,0},{2,3},{3,2},{4,5},{5,4},{6,7},{7,6},{8,9},{9,8},{10,11... | collective-permute-start | bytes 663560 | tf_op jit(solution)/shard_map/ppermute | solution.py:742
  74.5 55.2 %collective-permute-start.23 = (bf16[160,3560]{1,0:T(8,128)(2,1)S(1)}, bf16[160,3560]{1,0:T(8,128)(2,1)S(1)}, u32[]{:S(2)}, u32[]{:S(2)}) collective-permute-start(bf16[160,3560]{1,0:T(8,128)(2,1)S(1)} %pad_maximum_fusion.1), channel_id=1, source_target_pairs={{0,24},{8,16},{16,8},{24,0},{1,25},{9,17},{17,9},{25,1},{2,26},{10... | collective-permute-start | bytes 3417608 | tf_op jit(solution)/shard_map/ppermute | solution.py:742
  77.0 50.1 %collective-permute-start.22 = (bf16[160,3560]{1,0:T(8,128)(2,1)S(1)}, bf16[160,3560]{1,0:T(8,128)(2,1)S(1)}, u32[]{:S(2)}, u32[]{:S(2)}) collective-permute-start(bf16[160,3560]{1,0:T(8,128)(2,1)S(1)} %pad_maximum_fusion.1), channel_id=1, source_target_pairs={{0,16},{8,24},{16,0},{24,8},{1,17},{9,25},{17,1},{25,9},{2,18},{10... | collective-permute-start | bytes 3417608 | tf_op jit(solution)/shard_map/ppermute | solution.py:742
  77.5 48.0 %collective-permute-start.21 = (bf16[160,3560]{1,0:T(8,128)(2,1)S(1)}, bf16[160,3560]{1,0:T(8,128)(2,1)S(1)}, u32[]{:S(2)}, u32[]{:S(2)}) collective-permute-start(bf16[160,3560]{1,0:T(8,128)(2,1)S(1)} %pad_maximum_fusion.1), channel_id=1, source_target_pairs={{0,8},{8,0},{16,24},{24,16},{1,9},{9,1},{17,25},{25,17},{2,10},{10... | collective-permute-start | bytes 3417608 | tf_op jit(solution)/shard_map/ppermute | solution.py:742
  125.5 30.3 %collective-permute-start.15 = (bf16[288,1280]{1,0:T(8,128)(2,1)}, bf16[288,1280]{1,0:T(8,128)(2,1)}, u32[]{:S(2)}, u32[]{:S(2)}) collective-permute-start(bf16[288,1280]{1,0:T(8,128)(2,1)} %pad_maximum_fusion.2), channel_id=1, source_target_pairs={{0,16},{8,24},{16,0},{24,8},{1,17},{9,25},{17,1},{25,9},{2,18},{10... | collective-permute-start | bytes 2211848 | tf_op jit(solution)/shard_map/ppermute | solution.py:742
  127.1 27.0 %collective-permute-start.14 = (bf16[288,1280]{1,0:T(8,128)(2,1)}, bf16[288,1280]{1,0:T(8,128)(2,1)}, u32[]{:S(2)}, u32[]{:S(2)}) collective-permute-start(bf16[288,1280]{1,0:T(8,128)(2,1)} %pad_maximum_fusion.2), channel_id=1, source_target_pairs={{0,8},{8,0},{16,24},{24,16},{1,9},{9,1},{17,25},{25,17},{2,10},{10... | collective-permute-start | bytes 2211848 | tf_op jit(solution)/shard_map/ppermute | solution.py:742
  138.0 128.1 %collective-permute-start.24 = (bf16[640,3560]{0,1:T(8,128)(2,1)}, bf16[640,3560]{0,1:T(8,128)(2,1)}, u32[]{:S(2)}, u32[]{:S(2)}) collective-permute-start(bf16[640,3560]{0,1:T(8,128)(2,1)} %copy.169), channel_id=1, source_target_pairs={{0,4},{4,0},{1,5},{5,1},{2,6},{6,2},{3,7},{7,3},{8,12},{12,8},{9,1... | collective-permute-start | bytes 13670408 | tf_op jit(solution)/shard_map/ppermute | solution.py:742
  139.9 9.8 %collective-permute-start.2 = (bf16[288,384]{1,0:T(8,128)(2,1)S(1)}, bf16[288,384]{1,0:T(8,128)(2,1)S(1)}, u32[]{:S(2)}, u32[]{:S(2)}) collective-permute-start(bf16[288,384]{1,0:T(8,128)(2,1)S(1)} %pad_maximum_fusion.9), channel_id=1, source_target_pairs={{0,3},{1,2},{2,1},{3,0},{4,7},{5,6},{6,5},{7,4},{8,11},{9,10},{10,... | collective-permute-start | bytes 663560 | tf_op jit(solution)/shard_map/ppermute | solution.py:742
  143.9 20.5 %collective-permute-start.16 = (bf16[288,1280]{1,0:T(8,128)(2,1)}, bf16[288,1280]{1,0:T(8,128)(2,1)S(1)}, u32[]{:S(2)}, u32[]{:S(2)}) collective-permute-start(bf16[288,1280]{1,0:T(8,128)(2,1)} %pad_maximum_fusion.2), channel_id=1, source_target_pairs={{0,24},{8,16},{16,8},{24,0},{1,25},{9,17},{17,9},{25,1},{2,26},{10... | collective-permute-start | bytes 2211848 | tf_op jit(solution)/shard_map/ppermute | solution.py:742
  149.7 37.7 %collective-permute-start.9 = (bf16[288,768]{1,0:T(8,128)(2,1)}, bf16[288,768]{1,0:T(8,128)(2,1)S(1)}, u32[]{:S(2)}, u32[]{:S(2)}) collective-permute-start(bf16[288,768]{1,0:T(8,128)(2,1)} %pad_maximum_fusion.5), channel_id=1, source_target_pairs={{0,24},{8,16},{16,8},{24,0},{1,25},{9,17},{17,9},{25,1},{2,26},{10... | collective-permute-start | bytes 1327112 | tf_op jit(solution)/shard_map/ppermute | solution.py:742
  154.1 32.5 %collective-permute-start.8 = (bf16[288,768]{1,0:T(8,128)(2,1)S(1)}, bf16[288,768]{1,0:T(8,128)(2,1)S(1)}, u32[]{:S(2)}, u32[]{:S(2)}) collective-permute-start(bf16[288,768]{1,0:T(8,128)(2,1)S(1)} %copy-done.13), channel_id=1, source_target_pairs={{0,16},{8,24},{16,0},{24,8},{1,17},{9,25},{17,1},{25,9},{2,18},{10... | collective-permute-start | bytes 1327112 | tf_op jit(solution)/shard_map/ppermute | solution.py:742
  155.8 26.9 %collective-permute-start.7 = (bf16[288,768]{1,0:T(8,128)(2,1)S(1)}, bf16[288,768]{1,0:T(8,128)(2,1)S(1)}, u32[]{:S(2)}, u32[]{:S(2)}) collective-permute-start(bf16[288,768]{1,0:T(8,128)(2,1)S(1)} %copy-done.13), channel_id=1, source_target_pairs={{0,8},{8,0},{16,24},{24,16},{1,9},{9,1},{17,25},{25,17},{2,10},{10... | collective-permute-start | bytes 1327112 | tf_op jit(solution)/shard_map/ppermute | solution.py:742
  164.5 26.5 %collective-permute-start.3 = (bf16[1152,384]{1,0:T(8,128)(2,1)}, bf16[1152,384]{1,0:T(8,128)(2,1)}, u32[]{:S(2)}, u32[]{:S(2)}) collective-permute-start(bf16[1152,384]{1,0:T(8,128)(2,1)} %bitcast.6), channel_id=1, source_target_pairs={{0,4},{4,0},{1,5},{5,1},{2,6},{6,2},{3,7},{7,3},{8,12},{12,8},{9,1... | collective-permute-start | bytes 2654216 | tf_op jit(solution)/shard_map/ppermute | solution.py:742
  182.7 62.7 %collective-permute-start.17 = (bf16[1152,1280]{1,0:T(8,128)(2,1)S(1)}, bf16[1152,1280]{1,0:T(8,128)(2,1)}, u32[]{:S(2)}, u32[]{:S(2)}) collective-permute-start(bf16[1152,1280]{1,0:T(8,128)(2,1)S(1)} %constant_dynamic-update-slice_fusion.14.own_ref), channel_id=1, source_target_pairs={{0,4},{4,0},{1,5},{5,1},{2,6},{6,2},{3,7},{7,3},{8,12},{12,8},{9,1... | collective-permute-start | bytes 8847368 | tf_op jit(solution)/shard_map/ppermute | solution.py:742
  188.2 33.9 %collective-permute-start.10 = (bf16[1152,768]{1,0:T(8,128)(2,1)}, bf16[1152,768]{1,0:T(8,128)(2,1)}, u32[]{:S(2)}, u32[]{:S(2)}) collective-permute-start(bf16[1152,768]{1,0:T(8,128)(2,1)} %constant_dynamic-update-slice_fusion.7.own_ref), channel_id=1, source_target_pairs={{0,4},{4,0},{1,5},{5,1},{2,6},{6,2},{3,7},{7,3},{8,12},{12,8},{9,1... | collective-permute-start | bytes 5308424 | tf_op jit(solution)/shard_map/ppermute | solution.py:742
  434.5 11.4 %collective-permute-start.53 = (f32[1152,288]{0,1:T(8,128)}, f32[1152,288]{0,1:T(8,128)}, u32[]{:S(2)}, u32[]{:S(2)}) collective-permute-start(f32[1152,288]{0,1:T(8,128)} %copy.178), channel_id=1, source_target_pairs={{0,4},{4,0},{1,5},{5,1},{2,6},{6,2},{3,7},{7,3},{8,12},{12,8},{9,1... | collective-permute-start | bytes 3981320 | tf_op jit(solution)/shard_map/ppermute | solution.py:742
  438.7 67.1 %collective-permute-start.32 = (f32[640,1000]{0,1:T(8,128)}, f32[640,1000]{0,1:T(8,128)}, u32[]{:S(2)}, u32[]{:S(2)}) collective-permute-start(f32[640,1000]{0,1:T(8,128)} %copy.172), channel_id=1, source_target_pairs={{0,4},{4,0},{1,5},{5,1},{2,6},{6,2},{3,7},{7,3},{8,12},{12,8},{9,1... | collective-permute-start | bytes 7680008 | tf_op jit(solution)/shard_map/ppermute | solution.py:742
  439.3 80.4 %collective-permute-start.46 = (f32[1152,768]{1,0:T(8,128)}, f32[1152,768]{1,0:T(8,128)}, u32[]{:S(2)}, u32[]{:S(2)}) collective-permute-start(f32[1152,768]{1,0:T(8,128)} %get-tuple-element.102), channel_id=1, source_target_pairs={{0,4},{4,0},{1,5},{5,1},{2,6},{6,2},{3,7},{7,3},{8,12},{12,8},{9,1... | collective-permute-start | bytes 10616840 | tf_op jit(solution)/shard_map/ppermute | solution.py:742
  439.4 146.0 %collective-permute-start.39 = (f32[1152,1280]{1,0:T(8,128)}, f32[1152,1280]{1,0:T(8,128)}, u32[]{:S(2)}, u32[]{:S(2)}) collective-permute-start(f32[1152,1280]{1,0:T(8,128)} %get-tuple-element.100), channel_id=1, source_target_pairs={{0,4},{4,0},{1,5},{5,1},{2,6},{6,2},{3,7},{7,3},{8,12},{12,8},{9,1... | collective-permute-start | bytes 17694728 | tf_op jit(solution)/shard_map/ppermute | solution.py:742
  445.8 146.0 %collective-permute-start.25 = (f32[640,2560]{1,0:T(8,128)}, f32[640,2560]{1,0:T(8,128)}, u32[]{:S(2)}, u32[]{:S(2)}) collective-permute-start(f32[640,2560]{1,0:T(8,128)} %slice_bitcast_fusion), channel_id=1, source_target_pairs={{0,4},{4,0},{1,5},{5,1},{2,6},{6,2},{3,7},{7,3},{8,12},{12,8},{9,1... | collective-permute-start | bytes 19660808 | tf_op jit(solution)/shard_map/ppermute | solution.py:742
  452.3 7.8 %collective-permute-start.54 = (bf16[288,288]{1,0:T(8,128)(2,1)S(1)}, bf16[288,288]{1,0:T(8,128)(2,1)S(1)}, u32[]{:S(2)}, u32[]{:S(2)}) collective-permute-start(bf16[288,288]{1,0:T(8,128)(2,1)S(1)} %get-tuple-element.254), channel_id=1, source_target_pairs={{0,8},{8,0},{16,24},{24,16},{1,9},{9,1},{17,25},{25,17},{2,10},{10... | collective-permute-start | bytes 497672 | tf_op jit(solution)/shard_map/ppermute | solution.py:742
  460.1 7.9 %collective-permute-start.56 = (bf16[288,288]{1,0:T(8,128)(2,1)S(1)}, bf16[288,288]{1,0:T(8,128)(2,1)S(1)}, u32[]{:S(2)}, u32[]{:S(2)}) collective-permute-start(bf16[288,288]{1,0:T(8,128)(2,1)S(1)} %get-tuple-element.255), channel_id=1, source_target_pairs={{0,24},{8,16},{16,8},{24,0},{1,25},{9,17},{17,9},{25,1},{2,26},{10... | collective-permute-start | bytes 497672 | tf_op jit(solution)/shard_map/ppermute | solution.py:742
  505.8 12.8 %collective-permute-start.68 = (bf16[288,288]{1,0:T(8,128)(2,1)}, bf16[288,288]{1,0:T(8,128)(2,1)}, u32[]{:S(2)}, u32[]{:S(2)}) collective-permute-start(bf16[288,288]{1,0:T(8,128)(2,1)} %pad_maximum_fusion.11), channel_id=1, source_target_pairs={{0,4},{4,0},{1,5},{5,1},{2,6},{6,2},{3,7},{7,3},{8,12},{12,8},{9,1... | collective-permute-start | bytes 497672 | tf_op jit(solution)/shard_map/ppermute | solution.py:742
  518.0 10.6 %collective-permute-start.33 = (bf16[160,1000]{1,0:T(8,128)(2,1)S(1)}, bf16[160,1000]{1,0:T(8,128)(2,1)}, u32[]{:S(2)}, u32[]{:S(2)}) collective-permute-start(bf16[160,1000]{1,0:T(8,128)(2,1)S(1)} %get-tuple-element.237), channel_id=1, source_target_pairs={{0,8},{8,0},{16,24},{24,16},{1,9},{9,1},{17,25},{25,17},{2,10},{10... | collective-permute-start | bytes 960008 | tf_op jit(solution)/shard_map/ppermute | solution.py:742
  518.6 16.7 %collective-permute-start.35 = (bf16[160,1000]{1,0:T(8,128)(2,1)}, bf16[160,1000]{1,0:T(8,128)(2,1)}, u32[]{:S(2)}, u32[]{:S(2)}) collective-permute-start(bf16[160,1000]{1,0:T(8,128)(2,1)} %get-tuple-element.238), channel_id=1, source_target_pairs={{0,24},{8,16},{16,8},{24,0},{1,25},{9,17},{17,9},{25,1},{2,26},{10... | collective-permute-start | bytes 960008 | tf_op jit(solution)/shard_map/ppermute | solution.py:742
  519.7 17.5 %collective-permute-start.34 = (bf16[160,1000]{1,0:T(8,128)(2,1)S(1)}, bf16[160,1000]{1,0:T(8,128)(2,1)}, u32[]{:S(2)}, u32[]{:S(2)}) collective-permute-start(bf16[160,1000]{1,0:T(8,128)(2,1)S(1)} %get-tuple-element.239), channel_id=1, source_target_pairs={{0,16},{8,24},{16,0},{24,8},{1,17},{9,25},{17,1},{25,9},{2,18},{10... | collective-permute-start | bytes 960008 | tf_op jit(solution)/shard_map/ppermute | solution.py:742
  528.7 16.4 %collective-permute-start.47 = (bf16[288,768]{1,0:T(8,128)(2,1)}, bf16[288,768]{1,0:T(8,128)(2,1)S(1)}, u32[]{:S(2)}, u32[]{:S(2)}) collective-permute-start(bf16[288,768]{1,0:T(8,128)(2,1)} %get-tuple-element.234), channel_id=1, source_target_pairs={{0,8},{8,0},{16,24},{24,16},{1,9},{9,1},{17,25},{25,17},{2,10},{10... | collective-permute-start | bytes 1327112 | tf_op jit(solution)/shard_map/ppermute | solution.py:742
  535.3 18.7 %collective-permute-start.49 = (bf16[288,768]{1,0:T(8,128)(2,1)S(1)}, bf16[288,768]{1,0:T(8,128)(2,1)}, u32[]{:S(2)}, u32[]{:S(2)}) collective-permute-start(bf16[288,768]{1,0:T(8,128)(2,1)S(1)} %get-tuple-element.235), channel_id=1, source_target_pairs={{0,24},{8,16},{16,8},{24,0},{1,25},{9,17},{17,9},{25,1},{2,26},{10... | collective-permute-start | bytes 1327112 | tf_op jit(solution)/shard_map/ppermute | solution.py:742
  537.2 20.7 %collective-permute-start.48 = (bf16[288,768]{1,0:T(8,128)(2,1)S(1)}, bf16[288,768]{1,0:T(8,128)(2,1)}, u32[]{:S(2)}, u32[]{:S(2)}) collective-permute-start(bf16[288,768]{1,0:T(8,128)(2,1)S(1)} %get-tuple-element.236), channel_id=1, source_target_pairs={{0,16},{8,24},{16,0},{24,8},{1,17},{9,25},{17,1},{25,9},{2,18},{10... | collective-permute-start | bytes 1327112 | tf_op jit(solution)/shard_map/ppermute | solution.py:742
  559.9 8.5 %collective-permute-start.50 = (bf16[72,768]{1,0:T(8,128)(2,1)S(1)}, bf16[72,768]{1,0:T(8,128)(2,1)S(1)}, u32[]{:S(2)}, u32[]{:S(2)}) collective-permute-start(bf16[72,768]{1,0:T(8,128)(2,1)S(1)} %get-tuple-element.293), channel_id=1, source_target_pairs={{0,1},{1,0},{2,3},{3,2},{4,5},{5,4},{6,7},{7,6},{8,9},{9,8},{10,11... | collective-permute-start | bytes 331784 | tf_op jit(solution)/shard_map/ppermute | solution.py:742
  559.9 8.4 %collective-permute-start.52 = (bf16[72,768]{1,0:T(8,128)(2,1)S(1)}, bf16[72,768]{1,0:T(8,128)(2,1)S(1)}, u32[]{:S(2)}, u32[]{:S(2)}) collective-permute-start(bf16[72,768]{1,0:T(8,128)(2,1)S(1)} %get-tuple-element.294), channel_id=1, source_target_pairs={{0,3},{1,2},{2,1},{3,0},{4,7},{5,6},{6,5},{7,4},{8,11},{9,10},{10,... | collective-permute-start | bytes 331784 | tf_op jit(solution)/shard_map/ppermute | solution.py:742
  561.4 13.7 %collective-permute-start.51 = (bf16[72,768]{1,0:T(8,128)(2,1)S(1)}, bf16[72,768]{1,0:T(8,128)(2,1)S(1)}, u32[]{:S(2)}, u32[]{:S(2)}) collective-permute-start(bf16[72,768]{1,0:T(8,128)(2,1)S(1)} %get-tuple-element.295), channel_id=1, source_target_pairs={{0,2},{1,3},{2,0},{3,1},{4,6},{5,7},{6,4},{7,5},{8,10},{9,11},{10,... | collective-permute-start | bytes 331784 | tf_op jit(solution)/shard_map/ppermute | solution.py:742
  568.4 7.4 collective-permute-start.36
  568.4 8.7 %collective-permute-start.38 = (bf16[40,1000]{1,0:T(8,128)(2,1)S(1)}, bf16[40,1000]{1,0:T(8,128)(2,1)S(1)}, u32[]{:S(2)}, u32[]{:S(2)}) collective-permute-start(bf16[40,1000]{1,0:T(8,128)(2,1)S(1)} %get-tuple-element.297), channel_id=1, source_target_pairs={{0,3},{1,2},{2,1},{3,0},{4,7},{5,6},{6,5},{7,4},{8,11},{9,10},{10,... | collective-permute-start | bytes 240008 | tf_op jit(solution)/shard_map/ppermute | solution.py:742
  575.7 7.5 collective-permute-start.71
  585.3 110.8 %collective-permute-start.72 = (bf16[288,768]{1,0:T(8,128)(2,1)S(1)}, bf16[288,768]{1,0:T(8,128)(2,1)S(1)}, u32[]{:S(2)}, u32[]{:S(2)}) collective-permute-start(bf16[288,768]{1,0:T(8,128)(2,1)S(1)} %pad_maximum_fusion.7), channel_id=1, source_target_pairs={{0,4},{4,0},{1,5},{5,1},{2,6},{6,2},{3,7},{7,3},{8,12},{12,8},{9,1... | collective-permute-start | bytes 1327112 | tf_op jit(solution)/shard_map/ppermute | solution.py:742
  588.3 19.4 %collective-permute-start.40 = (bf16[288,1280]{1,0:T(8,128)(2,1)S(1)}, bf16[288,1280]{1,0:T(8,128)(2,1)S(1)}, u32[]{:S(2)}, u32[]{:S(2)}) collective-permute-start(bf16[288,1280]{1,0:T(8,128)(2,1)S(1)} %get-tuple-element.231), channel_id=1, source_target_pairs={{0,8},{8,0},{16,24},{24,16},{1,9},{9,1},{17,25},{25,17},{2,10},{10... | collective-permute-start | bytes 2211848 | tf_op jit(solution)/shard_map/ppermute | solution.py:742
  589.8 34.2 %collective-permute-start.42 = (bf16[288,1280]{1,0:T(8,128)(2,1)S(1)}, bf16[288,1280]{1,0:T(8,128)(2,1)S(1)}, u32[]{:S(2)}, u32[]{:S(2)}) collective-permute-start(bf16[288,1280]{1,0:T(8,128)(2,1)S(1)} %get-tuple-element.232), channel_id=1, source_target_pairs={{0,24},{8,16},{16,8},{24,0},{1,25},{9,17},{17,9},{25,1},{2,26},{10... | collective-permute-start | bytes 2211848 | tf_op jit(solution)/shard_map/ppermute | solution.py:742
  590.9 34.1 %collective-permute-start.41 = (bf16[288,1280]{1,0:T(8,128)(2,1)S(1)}, bf16[288,1280]{1,0:T(8,128)(2,1)S(1)}, u32[]{:S(2)}, u32[]{:S(2)}) collective-permute-start(bf16[288,1280]{1,0:T(8,128)(2,1)S(1)} %get-tuple-element.233), channel_id=1, source_target_pairs={{0,16},{8,24},{16,0},{24,8},{1,17},{9,25},{17,1},{25,9},{2,18},{10... | collective-permute-start | bytes 2211848 | tf_op jit(solution)/shard_map/ppermute | solution.py:742
  596.3 44.7 %collective-permute-start.26 = (bf16[160,2560]{1,0:T(8,128)(2,1)S(1)}, bf16[160,2560]{1,0:T(8,128)(2,1)S(1)}, u32[]{:S(2)}, u32[]{:S(2)}) collective-permute-start(bf16[160,2560]{1,0:T(8,128)(2,1)S(1)} %get-tuple-element.228), channel_id=1, source_target_pairs={{0,8},{8,0},{16,24},{24,16},{1,9},{9,1},{17,25},{25,17},{2,10},{10... | collective-permute-start | bytes 2457608 | tf_op jit(solution)/shard_map/ppermute | solution.py:742
  607.6 51.2 %collective-permute-start.28 = (bf16[160,2560]{1,0:T(8,128)(2,1)S(1)}, bf16[160,2560]{1,0:T(8,128)(2,1)S(1)}, u32[]{:S(2)}, u32[]{:S(2)}) collective-permute-start(bf16[160,2560]{1,0:T(8,128)(2,1)S(1)} %get-tuple-element.229), channel_id=1, source_target_pairs={{0,24},{8,16},{16,8},{24,0},{1,25},{9,17},{17,9},{25,1},{2,26},{10... | collective-permute-start | bytes 2457608 | tf_op jit(solution)/shard_map/ppermute | solution.py:742
  624.0 37.0 %collective-permute-start.27 = (bf16[160,2560]{1,0:T(8,128)(2,1)S(1)}, bf16[160,2560]{1,0:T(8,128)(2,1)S(1)}, u32[]{:S(2)}, u32[]{:S(2)}) collective-permute-start(bf16[160,2560]{1,0:T(8,128)(2,1)S(1)} %get-tuple-element.230), channel_id=1, source_target_pairs={{0,16},{8,24},{16,0},{24,8},{1,17},{9,25},{17,1},{25,9},{2,18},{10... | collective-permute-start | bytes 2457608 | tf_op jit(solution)/shard_map/ppermute | solution.py:742
  626.9 36.8 %collective-permute-start.43 = (bf16[72,1280]{1,0:T(8,128)(2,1)S(1)}, bf16[72,1280]{1,0:T(8,128)(2,1)S(1)}, u32[]{:S(2)}, u32[]{:S(2)}) collective-permute-start(bf16[72,1280]{1,0:T(8,128)(2,1)S(1)} %get-tuple-element.280), channel_id=1, source_target_pairs={{0,1},{1,0},{2,3},{3,2},{4,5},{5,4},{6,7},{7,6},{8,9},{9,8},{10,11... | collective-permute-start | bytes 552968 | tf_op jit(solution)/shard_map/ppermute | solution.py:742
  641.0 24.9 %collective-permute-start.45 = (bf16[72,1280]{1,0:T(8,128)(2,1)S(1)}, bf16[72,1280]{1,0:T(8,128)(2,1)S(1)}, u32[]{:S(2)}, u32[]{:S(2)}) collective-permute-start(bf16[72,1280]{1,0:T(8,128)(2,1)S(1)} %get-tuple-element.281), channel_id=1, source_target_pairs={{0,3},{1,2},{2,1},{3,0},{4,7},{5,6},{6,5},{7,4},{8,11},{9,10},{10,... | collective-permute-start | bytes 552968 | tf_op jit(solution)/shard_map/ppermute | solution.py:742
  658.8 9.2 %collective-permute-start.44 = (bf16[72,1280]{1,0:T(8,128)(2,1)S(1)}, bf16[72,1280]{1,0:T(8,128)(2,1)S(1)}, u32[]{:S(2)}, u32[]{:S(2)}) collective-permute-start(bf16[72,1280]{1,0:T(8,128)(2,1)S(1)} %get-tuple-element.282), channel_id=1, source_target_pairs={{0,2},{1,3},{2,0},{3,1},{4,6},{5,7},{6,4},{7,5},{8,10},{9,11},{10,... | collective-permute-start | bytes 552968 | tf_op jit(solution)/shard_map/ppermute | solution.py:742
  663.6 13.0 %collective-permute-start.29 = (bf16[40,2560]{1,0:T(8,128)(2,1)S(1)}, bf16[40,2560]{1,0:T(8,128)(2,1)S(1)}, u32[]{:S(2)}, u32[]{:S(2)}) collective-permute-start(bf16[40,2560]{1,0:T(8,128)(2,1)S(1)} %get-tuple-element.273), channel_id=1, source_target_pairs={{0,1},{1,0},{2,3},{3,2},{4,5},{5,4},{6,7},{7,6},{8,9},{9,8},{10,11... | collective-permute-start | bytes 614408 | tf_op jit(solution)/shard_map/ppermute | solution.py:742
  663.7 12.9 %collective-permute-start.31 = (bf16[40,2560]{1,0:T(8,128)(2,1)S(1)}, bf16[40,2560]{1,0:T(8,128)(2,1)S(1)}, u32[]{:S(2)}, u32[]{:S(2)}) collective-permute-start(bf16[40,2560]{1,0:T(8,128)(2,1)S(1)} %get-tuple-element.274), channel_id=1, source_target_pairs={{0,3},{1,2},{2,1},{3,0},{4,7},{5,6},{6,5},{7,4},{8,11},{9,10},{10,... | collective-permute-start | bytes 614408 | tf_op jit(solution)/shard_map/ppermute | solution.py:742
  665.9 19.5 %collective-permute-start.30 = (bf16[40,2560]{1,0:T(8,128)(2,1)S(1)}, bf16[40,2560]{1,0:T(8,128)(2,1)S(1)}, u32[]{:S(2)}, u32[]{:S(2)}) collective-permute-start(bf16[40,2560]{1,0:T(8,128)(2,1)S(1)} %get-tuple-element.275), channel_id=1, source_target_pairs={{0,2},{1,3},{2,0},{3,1},{4,6},{5,7},{6,4},{7,5},{8,10},{9,11},{10,... | collective-permute-start | bytes 614408 | tf_op jit(solution)/shard_map/ppermute | solution.py:742
  691.0 12.9 %collective-permute-start.75 = (bf16[72,1280]{1,0:T(8,128)(2,1)S(1)}, bf16[72,1280]{1,0:T(8,128)(2,1)S(1)}, u32[]{:S(2)}, u32[]{:S(2)}) collective-permute-start(bf16[72,1280]{1,0:T(8,128)(2,1)S(1)} %get-tuple-element.252), channel_id=1, source_target_pairs={{0,24},{8,16},{16,8},{24,0},{1,25},{9,17},{17,9},{25,1},{2,26},{10... | collective-permute-start | bytes 552968 | tf_op jit(solution)/shard_map/ppermute | solution.py:742
  692.3 11.6 %collective-permute-start.74 = (bf16[72,1280]{1,0:T(8,128)(2,1)S(1)}, bf16[72,1280]{1,0:T(8,128)(2,1)S(1)}, u32[]{:S(2)}, u32[]{:S(2)}) collective-permute-start(bf16[72,1280]{1,0:T(8,128)(2,1)S(1)} %get-tuple-element.252), channel_id=1, source_target_pairs={{0,16},{8,24},{16,0},{24,8},{1,17},{9,25},{17,1},{25,9},{2,18},{10... | collective-permute-start | bytes 552968 | tf_op jit(solution)/shard_map/ppermute | solution.py:742
  694.0 10.0 %collective-permute-start.73 = (bf16[72,1280]{1,0:T(8,128)(2,1)S(1)}, bf16[72,1280]{1,0:T(8,128)(2,1)S(1)}, u32[]{:S(2)}, u32[]{:S(2)}) collective-permute-start(bf16[72,1280]{1,0:T(8,128)(2,1)S(1)} %get-tuple-element.252), channel_id=1, source_target_pairs={{0,8},{8,0},{16,24},{24,16},{1,9},{9,1},{17,25},{25,17},{2,10},{10... | collective-permute-start | bytes 552968 | tf_op jit(solution)/shard_map/ppermute | solution.py:742
  694.5 8.5 %collective-permute-start.61 = (f32[33,128]{1,0:T(8,128)S(1)}, f32[33,128]{1,0:T(8,128)S(1)}, u32[]{:S(2)}, u32[]{:S(2)}) collective-permute-start(f32[33,128]{1,0:T(8,128)S(1)} %fusion.58), channel_id=1, source_target_pairs={{0,8},{8,0},{16,24},{24,16},{1,9},{9,1},{17,25},{25,17},{2,10},{10... | collective-permute-start | bytes 50696 | tf_op jit(solution)/shard_map/ppermute | solution.py:742
  710.9 22.5 %collective-permute-start.76 = (bf16[288,1280]{1,0:T(8,128)(2,1)S(1)}, bf16[288,1280]{1,0:T(8,128)(2,1)S(1)}, u32[]{:S(2)}, u32[]{:S(2)}) collective-permute-start(bf16[288,1280]{1,0:T(8,128)(2,1)S(1)} %pad_maximum_fusion.4), channel_id=1, source_target_pairs={{0,4},{4,0},{1,5},{5,1},{2,6},{6,2},{3,7},{7,3},{8,12},{12,8},{9,1... | collective-permute-start | bytes 2211848 | tf_op jit(solution)/shard_map/ppermute | solution.py:742
  (42 other events, 629.7 us)

commit v2 on v1

--- a/solution.py
+++ b/solution.py
@@ -32,6 +32,7 @@
 
 F32 = jnp.float32
 BF16 = jnp.bfloat16
+FLOPS_A_MICRO = 1.1e9
 VMEM_BYTES = 60 * 1024 * 1024
 
 
@@ -365,15 +366,15 @@
 def head(
     wide_ref, twice_ref, own_ref, far_ref, mask_ref, count_ref, label_ref, class_ref,
     gates_ref, gate_ref, mean_ref, route_ref,
-    expert_grad_ref, class_grad_ref, loss_ref, hidden_grad_ref, route_grad_ref,
-    mixed, slopes, turned, pooled, total,
+    own_grad_ref, far_grad_ref, loss_ref, hidden_grad_ref, route_grad_ref,
+    mixed, slopes, turned, pooled, total, means, logit_slopes,
 ):
     batch = count_ref.shape[0]
     line = MAP * batch
     step = pl.program_id(0)
     half = own_ref.shape[0]
     experts = NE * C2
-    columns = expert_grad_ref.shape[2]
+    columns = own_grad_ref.shape[1]
     sides = (own_ref, far_ref)
 
     @pl.when(step == 0)
@@ -399,7 +400,7 @@
 
         loop(MAP, pool)
         mean = (pooled[...] / count_ref[:, :1]).astype(BF16)
-        logits = nn(mean[:, :half], own_ref[:, experts:]) + nn(mean[:, half:], far_ref[:, experts:])
+        logits = nn(mean[:, :half], own_ref[:, experts : experts + CLASSES]) + nn(mean[:, half:], far_ref[:, experts : experts + CLASSES])
         spots = lax.broadcasted_iota(jnp.int32, logits.shape, 1)
         onehot = (spots == label_ref[...]).astype(F32)
         weight = jnp.sum(onehot * class_ref[...], axis=1, keepdims=True)
@@ -409,12 +410,12 @@
         loss = weight * (top + jnp.log(summed) - jnp.sum(logits * onehot, axis=1, keepdims=True))
         loss_ref[...] = jnp.concatenate([loss, weight], axis=1)
         logit_grad = (weight * (powers / summed - onehot)).astype(BF16)
+        means[...] = mean
+        logit_slopes[...] = jnp.zeros_like(logit_slopes)
+        logit_slopes[:, :CLASSES] = logit_grad
         for side, weights in enumerate(sides):
             place = slice(side * half, (side + 1) * half)
-            class_grad_ref[side] = lax.dot_general(
-                mean[:, place], logit_grad, (((0,), (0,)), ((), ())), preferred_element_type=F32
-            )
-            pooled[:, place] = nt(logit_grad, weights[:, experts:]) / count_ref[:, :1]
+            pooled[:, place] = nt(logit_grad, weights[:, experts : experts + CLASSES]) / count_ref[:, :1]
 
         def back(index):
             rows = rows_at(index, line)
@@ -430,13 +431,34 @@
                 :, part * LANES : (part + 1) * LANES
             ].T
 
-    blocks = experts // columns
+    blocks = pl.num_programs(0) // 2
     side = 1 - step // blocks
     block = step % blocks
-    expert_grad_ref[0] = nn(
-        turned[pl.ds(pl.multiple_of(side * half, half), half), :],
-        wide_ref[:, pl.ds(pl.multiple_of(block * columns, columns), columns)],
-    )
+    place = pl.ds(pl.multiple_of(side * half, half), half)
+
+    def weight_grad(out):
+        @pl.when(block < experts // columns)
+        def _():
+            out[...] = nn(
+                turned[place, :],
+                wide_ref[:, pl.ds(pl.multiple_of(block * columns, columns), columns)],
+            ).astype(out.dtype)
+
+        @pl.when(block >= experts // columns)
+        def _():
+            begin = pl.multiple_of(block * columns - experts, columns)
+            out[...] = lax.dot_general(
+                means[:, place], logit_slopes[:, pl.ds(begin, columns)],
+                (((0,), (0,)), ((), ())), preferred_element_type=F32,
+            ).astype(out.dtype)
+
+    @pl.when(side == 1)
+    def _():
+        weight_grad(far_grad_ref)
+
+    @pl.when(side == 0)
+    def _():
+        weight_grad(own_grad_ref)
 
     @pl.when(step == pl.num_programs(0) - 1)
     def _():
@@ -700,41 +722,74 @@
     return (first, second, master, average, master.astype(BF16))
 
 
-def adamw_kernel(widths, factor_ref, *refs):
-    pieces = refs[: len(widths)]
-    master, first, second, average = refs[len(widths) : len(widths) + 4]
-    outs = refs[len(widths) + 4 : len(widths) + 9]
-    factor = factor_ref[0]
-    if len(widths) == 1:
-        grad = pieces[0][...].astype(F32) * factor
-    else:
-        whole = refs[-1]
-        begin = 0
-        for piece, width in zip(pieces, widths):
-            whole[:, begin : begin + width] = piece[:, :width].astype(F32)
-            begin += width
-        grad = whole[...] * factor
+def adamw_kernel(segments, arrays, place_ref, factor_ref, *refs):
+    pieces = refs[: 2 * arrays]
+    master, first, second, average = refs[2 * arrays : 2 * arrays + 4]
+    outs = refs[2 * arrays + 4 : 2 * arrays + 9]
+    whole = refs[-1]
+
+    def fill(core):
+        at = 0
+        for side, array, begin, width in segments:
+            source = pieces[2 * array + (side ^ core)]
+            whole[:, at : at + width] = source[:, begin : begin + width].astype(F32)
+            at += width
+
+    for core in range(2):
+
+        @pl.when(place_ref[1] == core)
+        def _(core=core):
+            fill(core)
+
+    grad = whole[...] * factor_ref[0]
     values = adamw_values(master[...], first[...], second[...], average[...], grad)
     for out, value in zip(outs, values):
         out[...] = value
 
 
-def adamw(factor, pieces, widths, master, first, second, average):
+def adamw(factor, spot, rows, pieces, segments, master, first, second, average):
     height, width = master.shape
-    rows = 72 if height % 72 == 0 else height
-    specs = [pl.BlockSpec((rows, piece.shape[1]), lambda i: (i, 0)) for piece in pieces]
-    full = pl.BlockSpec((rows, width), lambda i: (i, 0))
+    specs = [
+        pl.BlockSpec((rows, piece.shape[1]), lambda i, place: (i ^ place[0], 0)) for piece in pieces
+    ]
+    full = pl.BlockSpec((rows, width), lambda i, place: (i, 0))
     types = (F32, F32, F32, F32, BF16)
     return pl.pallas_call(
-        functools.partial(adamw_kernel, tuple(widths)),
-        grid=(height // rows,),
-        in_specs=[pl.BlockSpec(memory_space=pltpu.SMEM)] + specs + [full] * 4,
-        out_specs=[full] * 5,
+        functools.partial(adamw_kernel, segments, len(pieces) // 2),
+        grid_spec=pltpu.PrefetchScalarGridSpec(
+            num_scalar_prefetch=1,
+            grid=(height // rows,),
+            in_specs=[pl.BlockSpec(memory_space=pltpu.SMEM)] + specs + [full] * 4,
+            out_specs=[full] * 5,
+            scratch_shapes=[pltpu.VMEM((rows, width), F32)],
+        ),
         out_shape=[jax.ShapeDtypeStruct((height, width), kind) for kind in types],
-        scratch_shapes=[pltpu.VMEM((rows, width), F32)] if len(widths) > 1 else [],
         compiler_params=pltpu.CompilerParams(vmem_limit_bytes=VMEM_BYTES),
         name="adamw",
-    )(factor, *pieces, master, first, second, average)
+    )(spot, factor, *pieces, master, first, second, average)
+
+
+def adamw_head_kernel(factor_ref, grad, master, first, second, average, *outs):
+    grad = grad[...] * factor_ref[0]
+    values = adamw_values(master[...], first[...], second[...], average[...], grad)
+    for out, value in zip(outs, values):
+        out[...] = value
+
+
+def adamw_head(factor, grad, *state):
+    height, width = state[0].shape
+    part = 4 * LANES
+    block = pl.BlockSpec((height, part), lambda i: (0, i))
+    types = (F32, F32, F32, F32, BF16)
+    return pl.pallas_call(
+        adamw_head_kernel,
+        grid=(pl.cdiv(width, part),),
+        in_specs=[pl.BlockSpec(memory_space=pltpu.SMEM)] + [block] * 5,
+        out_specs=[block] * 5,
+        out_shape=[jax.ShapeDtypeStruct((height, width), kind) for kind in types],
+        compiler_params=pltpu.CompilerParams(vmem_limit_bytes=VMEM_BYTES),
+        name="adamw_head",
+    )(factor, grad, *state)
 
 
 def swap(values, axis, distance):
@@ -742,28 +797,37 @@
     return lax.ppermute(values, axis, [(i, i ^ distance) for i in range(size)])
 
 
-def gather(values, axis):
-    parts = [values] + [swap(values, axis, k) for k in range(1, lax.axis_size(axis))]
+def meet(*values):
+    return lax.optimization_barrier(values)
+
+
+def copies(values, axis):
+    return [values] + [swap(values, axis, k) for k in range(1, lax.axis_size(axis))]
+
+
+def joined(parts):
     return jnp.concatenate(parts, axis=0)
 
 
-def scatter_sum(mine, axis):
-    total = mine(0)
-    for k in range(1, lax.axis_size(axis)):
-        total = total + swap(mine(k).astype(BF16), axis, k).astype(F32)
+def pair_sum(own, came, parts):
+    rows = own.shape[0] // parts
+    return [own[k * rows : (k + 1) * rows] + came[k * rows : (k + 1) * rows] for k in range(parts)]
+
+
+def exchange(blocks, axis):
+    return [blocks[0]] + [swap(block.astype(BF16), axis, k) for k, block in enumerate(blocks) if k]
+
+
+def added(parts):
+    total = parts[0]
+    for value in parts[1:]:
+        total = total + value.astype(F32)
     return total
 
 
-def reduce_shard(own, far, rows):
-    came = swap(far, "core", 1)
-    deep = lax.axis_size("chan")
-
-    def block(k):
-        place = slice(k * deep * rows, (k + 1) * deep * rows)
-        return own[place] + came[place]
-
-    middle = scatter_sum(block, "xy")
-    return scatter_sum(lambda k: middle[k * rows : (k + 1) * rows], "chan")
+def split(values, parts):
+    rows = values.shape[0] // parts
+    return [values[k * rows : (k + 1) * rows] for k in range(parts)]
 
 
 def total_sum(values):
@@ -783,15 +847,12 @@
     ]
 
 
-def spread_back(shard):
-    low = shard.astype(BF16)
+def in_order(parts):
     place = lax.axis_index("xy")
-    size = lax.axis_size("xy")
-    stack = gather(low, "xy").reshape(size, *low.shape)
-    mine = jnp.concatenate(
-        [lax.dynamic_index_in_dim(stack, place ^ k, 0, keepdims=False) for k in range(size)], 0
-    )
-    return mine, swap(mine, "core", 1)
+    stack = jnp.stack(parts)
+    return joined(
+        [lax.dynamic_index_in_dim(stack, place ^ k, 0, keepdims=False) for k in range(len(parts))]
+    )
 
 
 def two_parts(values):
@@ -799,7 +860,7 @@
     return [upper.astype(BF16), (values - upper).astype(BF16)]
 
 
-def call(kernel, grid, ins, outs, scratch, name):
+def call(kernel, grid, ins, outs, scratch, name, micros):
     def spec(shape, block, index):
         if block is None:
             return pl.BlockSpec(memory_space=pltpu.VMEM)
@@ -823,6 +884,9 @@
         scratch_shapes=scratch,
         compiler_params=pltpu.CompilerParams(
             vmem_limit_bytes=VMEM_BYTES, dimension_semantics=("arbitrary",) * len(grid)
+        ),
+        cost_estimate=pl.CostEstimate(
+            flops=int(micros * FLOPS_A_MICRO), bytes_accessed=1 << 20, transcendentals=0
         ),
         name=name,
     )(*arrays)
@@ -880,25 +944,37 @@
         + two_parts(row[:, C0 : C0 + SE]),
         1,
     )
-    small = jnp.concatenate(own_order(jnp.where(first_core, small_left, small_right), height), 0)
-    small = gather(small, "chan").reshape(chans, places, height, 2 * C0)
-    small = small.transpose(1, 0, 2, 3).reshape(wide, 2 * C0)
-    small_far = swap(small, "core", 1)
-    left = jnp.where(first_core, small, small_far)
-    right = jnp.where(first_core, small_far, small)
-
+    small = joined(own_order(jnp.where(first_core, small_left, small_right), height))
     expand_own = lax.dynamic_slice(
         column, (place * height, begin + core * HALF * C0), (height, HALF * C0)
     ).astype(BF16)
-    expand_own = gather(gather(expand_own, "chan"), "xy")
-    expand_far = swap(expand_own, "core", 1)
     project_own = lax.dynamic_slice(
         row, (place * height, C0 + SE + core * HALF * C2), (height, HALF * C2)
     ).astype(BF16)
-    project_own = gather(gather(project_own, "chan"), "xy")
-    project_far = swap(project_own, "core", 1)
-    head_own = gather(gather(head_master.T.astype(BF16), "chan"), "xy")
-    head_far = swap(head_own, "core", 1)
+    part = 4 * LANES
+    blocks = pl.cdiv(NE * C2 + CLASSES, part)
+    lanes = blocks * part
+    head_own = jnp.pad(head_master.T.astype(BF16), ((0, 0), (0, lanes - NE * C2 - CLASSES)))
+    mine = lax.all_to_all(images, "chan", 0, 0, tiled=True)
+    small, expand_own, project_own, head_own, mine = meet(
+        copies(small, "chan"), expand_own, project_own, head_own, mine
+    )
+    small = joined(small).reshape(chans, places, height, 2 * C0)
+    small = small.transpose(1, 0, 2, 3).reshape(wide, 2 * C0)
+    small_far = swap(small, "core", 1)
+    expand_own = copies(expand_own, "chan")
+    project_own = joined([project_own, swap(project_own, "chan", 1)])
+    head_own = lax.all_gather(head_own, "chan", axis=0, tiled=True)
+    expand_own = joined(expand_own)
+    left = jnp.where(first_core, small, small_far)
+    right = jnp.where(first_core, small_far, small)
+    expand_own = copies(expand_own, "xy")
+    distance = 2
+    project_own = [project_own]
+    while distance < chans:
+        held = joined(project_own)
+        project_own = [held, swap(held, "chan", distance)]
+        distance *= 2
 
     def both(values, at, width):
         upper = values[:, at : at + width].astype(F32)
@@ -914,7 +990,6 @@
     route_in, route_out = route_master[:C0], route_master[C0:]
     route_in = jnp.where(first_core, route_in, jnp.roll(route_in, HALF, axis=1))
 
-    mine = lax.all_to_all(images, "chan", 0, 0, tiled=True)
     mine = mine.reshape(chans, batch, slots // chans, C0).transpose(0, 2, 1, 3)
     label = lax.dynamic_slice_in_dim(labels, layer * batch, batch, 0)
     side = lax.dynamic_slice_in_dim(resolution, layer * batch, batch, 0)
@@ -944,7 +1019,7 @@
     def out_tiled(width, kind):
         return ((wide, width), kind, (tile, width), lambda i: (i, 0))
 
-    conv_one, mixed_in, twice_one, mean_one, gate_one, gates_one, gates_mid = call(
+    first_out = call(
         first_forward,
         (tiles,),
         [
@@ -965,7 +1040,15 @@
             pltpu.VMEM((rows, C0), F32),
         ],
         "first_forward",
-    )
+        20,
+    )
+
+    (conv_one, mixed_in, twice_one, mean_one, gate_one, gates_one, gates_mid) = first_out
+    mixed_in, expand_own, project_own, head_own = meet(mixed_in, expand_own, project_own, head_own)
+    expand_own, project_own = joined(expand_own), joined(project_own)
+    head_own = lax.all_gather(head_own, "xy", axis=0, tiled=True)
+    expand_far = swap(expand_own, "core", 1)
+    project_own = copies(project_own, "xy")
 
     mixed_two, conv_two, mean_two, units, scale = call(
         second_forward,
@@ -983,7 +1066,12 @@
         ],
         [pltpu.VMEM((rows, tile), F32)],
         "second_forward",
-    )
+        22,
+    )
+
+    conv_two, project_own = meet(conv_two, project_own)
+    project_own = joined(project_own)
+    project_far = swap(project_own, "core", 1)
 
     each, twice_two, mixed_head, mean_three, gate_two, gates_two = call(
         project,
@@ -1002,12 +1090,13 @@
         ],
         [pltpu.VMEM((rows, wide), BF16)],
         "project",
-    )
-
+        20,
+    )
+
+    mixed_head, head_own = meet(mixed_head, head_own)
+    head_far = swap(head_own, "core", 1)
     half = head_own.shape[0]
-    blocks = 5
-    part = NE * C2 // blocks
-    expert_grad, class_grad, losses, hidden_two, route_grad_out = call(
+    head_grad_own, head_grad_far, losses, hidden_two, route_grad_out = call(
         head,
         (2 * blocks,),
         [
@@ -1016,11 +1105,8 @@
             whole(gate_two), whole(mean_three), whole(route_out),
         ],
         [
-            (
-                (2, half, NE * C2), F32, (1, half, part),
-                lambda i: (1 - i // blocks, 0, i % blocks),
-            ),
-            out_full((2, half, CLASSES), F32),
+            ((half, lanes), BF16, (half, part), lambda i: (0, jnp.maximum(i - blocks, 0))),
+            ((half, lanes), BF16, (half, part), lambda i: (0, jnp.minimum(i, blocks - 1))),
             out_full((batch, 2), F32),
             out_full((rows, 2 * C2), BF16),
             out_full((C2, NE), F32),
@@ -1028,13 +1114,13 @@
         [
             pltpu.VMEM((rows, 2 * half), F32), pltpu.VMEM((rows, 2 * half), BF16),
             pltpu.VMEM((2 * half, rows), BF16), pltpu.VMEM((batch, 2 * half), F32),
-            pltpu.VMEM((rows, C2), F32),
+            pltpu.VMEM((rows, C2), F32), pltpu.VMEM((batch, 2 * half), BF16),
+            pltpu.VMEM((batch, lanes - NE * C2), BF16),
         ],
         "head",
-    )
-    rows_head = head_master.shape[1]
-    expert_shard = reduce_shard(expert_grad[0], expert_grad[1], rows_head)
-    class_shard = reduce_shard(class_grad[0], class_grad[1], rows_head)
+        45,
+    )
+    head_came = swap(head_grad_far, "core", 1)
 
     deep_grad, project_grad_own, project_grad_far, gate_sums, unit_grad, excite_grad = call(
         project_back,
@@ -1057,8 +1143,17 @@
             pltpu.VMEM((batch, wide), F32),
         ],
         "project_back",
-    )
-    project_shard = reduce_shard(project_grad_own, project_grad_far, height)
+        29,
+    )
+    deep_grad, head_came = meet(deep_grad, head_came)
+    high_rows = half // places
+    head_blocks = [
+        lax.dynamic_slice_in_dim(head_grad_own, (place ^ k) * high_rows, high_rows, 0).astype(F32)
+        + lax.dynamic_slice_in_dim(head_came, (place ^ k) * high_rows, high_rows, 0).astype(F32)
+        for k in range(places)
+    ]
+    head_parts = exchange(head_blocks, "xy")
+    project_came = swap(project_grad_far, "core", 1)
 
     expand_grad_own, expand_grad_far, tap_grad_two, hidden_one, route_grad_in = call(
         second_back,
@@ -1082,35 +1177,68 @@
             pltpu.VMEM((wide, HALF * C0), BF16),
         ],
         "second_back",
-    )
-    expand_shard = reduce_shard(expand_grad_own, expand_grad_far, height)
-
-    weight_grad, tap_grad_one = call(
-        first_back,
-        (tiles,),
-        [
-            whole(x), tiled(left), tiled(right), tap_tile(first_taps), whole(mask),
-            across(conv_one), whole(hidden_one),
-        ],
-        [out_tiled(2 * C0, F32), out_across(TAPS, F32)],
-        [
-            pltpu.VMEM((rows, tile), F32), pltpu.VMEM((rows, tile), F32),
-            pltpu.VMEM((rows, tile), F32), pltpu.VMEM((rows, tile), BF16),
-        ],
-        "first_back",
-    )
-    small_width = C0 + 2 * SE
+        43,
+    )
+    hidden_one, project_came, head_parts = meet(hidden_one, project_came, head_parts)
+    head_shard = lax.psum_scatter(added(head_parts), "chan", scatter_dimension=0, tiled=True)
+    project_parts = exchange(pair_sum(project_grad_own, project_came, places), "xy")
+    expand_came = swap(expand_grad_far, "core", 1)
+
+    def first_back_tiles(start, count_, hidden_one):
+        def shifted(array):
+            return (array, (tile, array.shape[1]), lambda i: (i + start, 0))
+
+        return call(
+            first_back,
+            (count_,),
+            [
+                whole(x), shifted(left), shifted(right),
+                (first_taps, (TAPS, 8, tile), lambda i: (0, 0, i + start)), whole(mask),
+                (conv_one, (rows, tile), lambda i: (0, i + start)), whole(hidden_one),
+            ],
+            [
+                ((count_ * tile, 2 * C0), F32, (tile, 2 * C0), lambda i: (i, 0)),
+                ((TAPS, count_ * tile), F32, (TAPS, tile), lambda i: (0, i)),
+            ],
+            [
+                pltpu.VMEM((rows, tile), F32), pltpu.VMEM((rows, tile), F32),
+                pltpu.VMEM((rows, tile), F32), pltpu.VMEM((rows, tile), BF16),
+            ],
+            "first_back",
+            12 * count_,
+        )
+
+    start_grad, tap_grad_start = first_back_tiles(0, tiles - 1, hidden_one)
+    start_grad, hidden_one, project_parts, expand_came = meet(
+        start_grad, hidden_one, project_parts, expand_came
+    )
+    expand_parts = exchange(pair_sum(expand_grad_own, expand_came, places), "xy")
+    project_parts = exchange(split(added(project_parts), chans), "chan")
+    end_grad, tap_grad_end = first_back_tiles(tiles - 1, 1, hidden_one)
+    end_grad, expand_parts, project_parts = meet(end_grad, expand_parts, project_parts)
+    weight_grad = joined([start_grad, end_grad])
+    tap_grad_one = jnp.concatenate([tap_grad_start, tap_grad_end], 1)
+
+    small_width = 3 * LANES
     tap_grads = jnp.concatenate([tap_grad_one, tap_grad_two], 0).T
     left_grad = jnp.concatenate([weight_grad[:, :C0], tap_grads], 1)
     left_grad = jnp.pad(left_grad, ((0, 0), (0, small_width - left_grad.shape[1])))
     right_grad = jnp.concatenate([weight_grad[:, C0:], excite_grad], 1)
-    small_shard = reduce_shard(
-        jnp.where(first_core, left_grad, right_grad),
-        jnp.where(first_core, right_grad, left_grad),
-        height,
-    )
-
-    shards = (expert_shard, class_shard, project_shard, expand_shard, small_shard)
+    right_grad = jnp.pad(right_grad, ((0, 0), (0, small_width - right_grad.shape[1])))
+    small_own = jnp.where(first_core, left_grad, right_grad)
+    small_came = swap(jnp.where(first_core, right_grad, left_grad), "core", 1)
+    small_came, project_parts, head_shard = meet(small_came, project_parts, head_shard)
+    small_parts = exchange(pair_sum(small_own, small_came, places), "xy")
+    project_shard = added(project_parts)
+    small_middle = added(small_parts)
+    mixed_middle = jnp.concatenate([small_middle, added(expand_parts)], 1)
+    mixed_parts = exchange(split(mixed_middle, chans), "chan")
+    project_low = copies(project_shard.astype(BF16), "xy")
+    mixed_parts, project_low = meet(mixed_parts, project_low)
+    mixed_shard = added(mixed_parts)
+    mixed_low = copies(mixed_shard.astype(BF16), "xy")
+
+    shards = (head_shard, project_shard, mixed_shard)
     squares = sum(jnp.sum(shard * shard) for shard in shards)
     route_grad_in = jnp.where(first_core, route_grad_in, jnp.roll(route_grad_in, HALF, axis=1))
     route_grad = jnp.concatenate([route_grad_in, route_grad_out], 0)
@@ -1123,21 +1251,25 @@
     factor = jnp.minimum(1.0, CLIP / (clip_norm + 1e-06)) / weight_total
     scalar = factor[None]
 
-    project_mine, project_other = spread_back(project_shard)
-    expand_mine, expand_other = spread_back(expand_shard)
-    small_mine, small_other = spread_back(small_shard)
-
-    def ordered(mine_, other):
-        return jnp.where(first_core, mine_, other), jnp.where(first_core, other, mine_)
-
-    project_low, project_up = ordered(project_mine, project_other)
-    expand_low, expand_up = ordered(expand_mine, expand_other)
-    small_low, small_up = ordered(small_mine, small_other)
-    squeeze_grad = small_up[:, C0 + SE :]
+    if height % 8 == 0:
+        line, spot = height, jnp.stack([place, core])
+        project_mine, mixed_mine = joined(project_low), joined(mixed_low)
+    else:
+        line, spot = column.shape[0], jnp.stack([jnp.zeros_like(place), core])
+        project_mine, mixed_mine = in_order(project_low), in_order(mixed_low)
+    project_pair = [project_mine, swap(project_mine, "core", 1)]
+    mixed_pair = [mixed_mine, swap(mixed_mine, "core", 1)]
     column_out = adamw(
         scalar,
-        [small_low, small_up[:, C0 : C0 + SE], expand_low, expand_up],
-        [C0 + 2 * TAPS, SE, HALF * C0, HALF * C0],
+        spot,
+        line,
+        mixed_pair,
+        (
+            (0, 0, 0, C0 + 2 * TAPS),
+            (1, 0, C0, SE),
+            (0, 0, small_width, HALF * C0),
+            (1, 0, small_width, HALF * C0),
+        ),
         column,
         column_first.T,
         column_second.T,
@@ -1145,21 +1277,17 @@
     )
     row_out = adamw(
         scalar,
-        [small_up, squeeze_grad, project_low, project_up],
-        [C0, SE, HALF * C2, HALF * C2],
+        spot,
+        line,
+        mixed_pair + project_pair,
+        ((1, 0, 0, C0), (1, 0, C0 + SE, SE), (0, 1, 0, HALF * C2), (1, 1, 0, HALF * C2)),
         row_master,
         row_first,
         row_second,
         row_average,
     )
-    head_out = adamw(
-        scalar,
-        [expert_shard, class_shard],
-        [NE * C2, CLASSES],
-        head_master.T,
-        head_first.T,
-        head_second.T,
-        head_average.T,
+    head_out = adamw_head(
+        scalar, head_shard, head_master.T, head_first.T, head_second.T, head_average.T
     )
     route_out_new = adamw_values(
         route_master, route_first, route_second, route_average, route_sum * factor

time: 758 us -> 524 us (0.69)
  waiting for transfers between devices: 274 us -> 114 us
  local copies, waits for them, and re-layouts: 91.1 us -> 32.1 us
  starting transfers between devices: 74.7 us -> 58.1 us
  other arithmetic: 58.3 us -> 44.5 us
  between operations: 8.93 us -> 20.6 us
    ppermute x77 -> x53, waiting for transfers between devices: 274 us -> 108 us  [swap(): return lax.ppermute(values, axis, [(i, i ^ distance) for i in range(size)])]
    unnamed x86 -> x74, local copies, waits for them, and re-layouts: 33.2 us -> 13.7 us
    ppermute x77 -> x53, starting transfers between devices: 70.5 us -> 53 us  [swap(): return lax.ppermute(values, axis, [(i, i ^ distance) for i in range(size)])]
    squeeze x6 -> x0, local copies, waits for them, and re-layouts: 10.4 us -> none  [the longest x1 6.04 us: on_device(): expert_shard = reduce_shard(expert_grad[0], expert_grad[1], rows_head)]
    ppermute x1 -> x0, local copies, waits for them, and re-layouts: 7.76 us -> none  [swap(): return lax.ppermute(values, axis, [(i, i ^ distance) for i in range(size)])]
    convert_element_type x8 -> x7, other arithmetic: 16.9 us -> 21.8 us  [the longest x4 19.2 us: exchange(): block.astype(BF16)]
    pallas_call x7 -> x8, Pallas kernels: 218 us -> 221 us  [call(): pl.pallas_call(kernel, grid=grid, in_specs=in_specs, out_specs=[spec(shap...]
  transfers between devices with their start and end apart: 78 -> 57, of which waited for: 37 -> 22; matrix products, arithmetic and copies ran while one was open for 18% -> 11% of each run, Pallas kernels for 10% -> 36%
where the time goes in v2:
time: 524 us; the launch traced here: 518 us
  Pallas kernels  248 us (47%)
  waiting for transfers between devices  114 us (22%)
  starting transfers between devices  58.1 us (11%)
  other arithmetic  44.5 us (8%)
  local copies, waits for them, and re-layouts  32.1 us (6%)
  between operations  20.6 us (4%)
    pallas_call x8, Pallas kernels, call(): pl.pallas_call(kernel, grid=grid, in_specs=in_specs, out_specs=[spec(shap...  221 us
    ppermute x53, waiting for transfers between devices, swap(): return lax.ppermute(values, axis, [(i, i ^ distance) for i in range(size)])  108 us
    ppermute x53, starting transfers between devices, swap(): return lax.ppermute(values, axis, [(i, i ^ distance) for i in range(size)])  53 us
    pallas_call x2, Pallas kernels, adamw(): pl.pallas_call(functools.partial(adamw_kernel, segments, len(pieces) // 2...  21.1 us
    convert_element_type x4, other arithmetic, exchange(): block.astype(BF16)  19.2 us
    unnamed x74, local copies, waits for them, and re-layouts  13.7 us
  transfers between devices with their start and end apart: 57, of which 22 were waited for; matrix products, arithmetic and copies ran while one was open for 11% of the time, Pallas kernels for 36%

profile of v2, /device:TPU:0, one launch (start us, length us, event | category | flops | bytes accessed | tf_op | source)
XLA Modules:
  0.0 517.8 jit_solution(6299576290228764803)
XLA Ops:
  11.9 5.1 collective-permute-start.2
  17.7 5.0 all-to-all-start
  26.9 15.5 %collective-permute-done.1 = bf16[288,384]{1,0:T(8,128)(2,1)S(1)} collective-permute-done((bf16[288,384]{1,0:T(8,128)(2,1)S(1)}, bf16[288,384]{1,0:T(8,128)(2,1)S(1)}, u32[]{:S(2)}, u32[]{:S(2)}) %collective-permute-start.1) | collective-permute-done | bytes 221216 | tf_op jit(solution)/shard_map/ppermute | solution.py:797
  42.4 4.7 all-to-all-done
  47.1 2.6 collective-permute-start.6
  49.7 1.7 collective-permute-start.4
  53.4 5.5 %collective-permute-done.4 = bf16[72,768]{1,0:T(8,128)(2,1)S(1)} collective-permute-done((bf16[72,768]{1,0:T(8,128)(2,1)S(1)}, bf16[72,768]{1,0:T(8,128)(2,1)S(1)}, u32[]{:S(2)}, u32[]{:S(2)}) %collective-permute-start.4) | collective-permute-done | bytes 110624 | tf_op jit(solution)/shard_map/ppermute | solution.py:797
  59.0 2.5 collective-permute-start.9
  62.5 1.3 collective-permute-start.11
  68.9 20.5 %first_forward.1 = (f32[1024,1152]{1,0:T(8,128)}, bf16[1024,1536]{1,0:T(8,128)(2,1)}, bf16[1024,384]{1,0:T(8,128)(2,1)}, f32[16,192]{1,0:T(8,128)}, f32[16,8]{1,...) custom-call(bf16[1024,192]{1,0:T(8,128)(2,1)} %bitcast_select_fusion.x_ref, bf16[1152,384]{1,0:T(8,128)(2,1)} %copy-done.6, ...), custom_call_target="tpu_custom_call" | custom-call | flops 22000001024 | bytes 1048576 | tf_op jit(solution)/shard_map/first_forward/pallas_call | solution.py:878
  89.4 7.8 %collective-permute-done.11 = bf16[144,1280]{1,0:T(8,128)(2,1)} collective-permute-done((bf16[144,1280]{1,0:T(8,128)(2,1)S(1)}, bf16[144,1280]{1,0:T(8,128)(2,1)}, u32[]{:S(2)}, u32[]{:S(2)}) %collective-permute-start.11) | collective-permute-done | bytes 368672 | tf_op jit(solution)/shard_map/ppermute | solution.py:797
  99.3 1.9 constant_dynamic-update-slice_fusion.8
  101.2 1.8 constant_dynamic-update-slice_fusion.7
  104.1 1.4 convert_add_fusion.4
  106.5 2.5 collective-permute-start.15
  111.1 22.5 %second_forward.1 = (f32[1024,1152]{1,0:T(8,128)}, f32[1024,1152]{1,0:T(8,128)}, f32[16,1152]{1,0:T(8,128)}, f32[16,48]{1,0:T(8,128)}, f32[16,1152]{1,0:T(8,128)}) custom-call(bf16[1024,1536]{1,0:T(8,128)(2,1)} %get-tuple-element.146.wide_ref, bf16[1152,768]{1,0:T(8,128)(2,1)} %constant_dynamic-update-slice_fusion.6.own_ref, ...), custom_call_target="tpu_custom_call" | custom-call | flops 24199999488 | bytes 1048576 | tf_op jit(solution)/shard_map/second_forward/pallas_call | solution.py:878
  133.6 20.8 %collective-permute-done.14 = bf16[288,1280]{1,0:T(8,128)(2,1)S(1)} collective-permute-done((bf16[288,1280]{1,0:T(8,128)(2,1)S(1)}, bf16[288,1280]{1,0:T(8,128)(2,1)S(1)}, u32[]{:S(2)}, u32[]{:S(2)}) %collective-permute-start.14) | collective-permute-done | bytes 737312 | tf_op jit(solution)/shard_map/ppermute | solution.py:797
  159.0 4.7 collective-permute-done.16.far_ref
  163.7 1.6 copy-done.28
  165.3 20.8 %project.1 = (bf16[1024,2560]{1,0:T(8,128)(2,1)}, bf16[1024,640]{1,0:T(8,128)(2,1)}, bf16[1024,2560]{1,0:T(8,128)(2,1)}, f32[16,320]{1,0:T(8,128)}, f32[16,8]{1,0:T(8,128)}, /*index=5*/f32[4,16,640]{2,1,0:T(8,128)}) custom-call(f32[1024,1152]{1,0:T(8,128)} %get-tuple-element.154.conv_ref, f32[16,1152]{1,0:T(8,128)} %get-tuple-element.155.scale_ref.full_scale_ref, ...), custom_call_target="tpu_custom_call" | custom-call | flops 22000001024 | bytes 1048576 | tf_op jit(solution)/shard_map/project/pallas_call | solution.py:878
  187.1 7.2 %collective-permute-done.17.far_ref = bf16[640,3584]{1,0:T(8,128)(2,1)} collective-permute-done((bf16[640,3584]{1,0:T(8,128)(2,1)}, bf16[640,3584]{1,0:T(8,128)(2,1)}, u32[]{:S(2)}, u32[]{:S(2)}) %collective-permute-start.17) | collective-permute-done | bytes 4587552 | tf_op jit(solution)/shard_map/ppermute | solution.py:797
  194.2 47.3 %head.1 = (bf16[640,3584]{1,0:T(8,128)(2,1)}, bf16[640,3584]{1,0:T(8,128)(2,1)}, f32[16,2]{1,0:T(8,128)}, bf16[1024,640]{1,0:T(8,128)(2,1)}, f32[320,8]{1,0:T(8,128)}) custom-call(bf16[1024,2560]{1,0:T(8,128)(2,1)} %get-tuple-element.163.wide_ref, bf16[1024,640]{1,0:T(8,128)(2,1)} %get-tuple-element.164.twice_ref, ...), custom_call_target="tpu_custom_call" | custom-call | flops 49500000256 | bytes 1048576 | tf_op jit(solution)/shard_map/head/pallas_call | solution.py:878
  241.7 29.5 %project_back.1 = (f32[1024,1152]{1,0:T(8,128)}, f32[1152,1280]{1,0:T(8,128)}, f32[1152,1280]{1,0:T(8,128)}, f32[4,16,640]{2,1,0:T(8,128)}, f32[16,48]{1,0:T(8,128)}, /*index=5*/f32[1152,96]{1,0:T(8,128)}) custom-call(bf16[1024,640]{1,0:T(8,128)(2,1)} %get-tuple-element.169.hidden_ref, f32[4,16,640]{2,1,0:T(8,128)} %get-tuple-element.160.gates_ref, ...), custom_call_target="tpu_custom_call" | custom-call | flops 31900000256 | bytes 1048576 | tf_op jit(solution)/shard_map/project_back/pallas_call | solution.py:878
  271.6 6.1 %add_convert_fusion = (bf16[160,3584]{1,0:T(8,128)(2,1)}, bf16[160,3584]{1,0:T(8,128)(2,1)}, bf16[160,3584]{1,0:T(8,128)(2,1)}, f32[160,3584]{1,0:T(8,128)S(1)}) fusion(bf16[640,3584]{1,0:T(8,128)(2,1)} %collective-permute-done.18, s32[]{:T(128)S(6)} %select_n.127, bf16[640,3584]{1,0:T(8,128)(2,1)} %get-tuple-element.188, s32[]{:T(128)S(6)} %select_n.126, ...), kind=kLoop, calls=%fused_computation.1 | loop fusion | flops 8601600 | bytes 14909456 | tf_op jit(solution)/shard_map/convert_element_type | solution.py:818
  277.7 1.7 collective-permute-start.22
  279.4 1.3 collective-permute-start.21
  281.2 43.4 %second_back.1 = (f32[1152,768]{1,0:T(8,128)}, f32[1152,768]{1,0:T(8,128)}, f32[25,1152]{1,0:T(8,128)}, bf16[1024,192]{1,0:T(8,128)(2,1)}, f32[192,8]{1,0:T(8,128)}) custom-call(f32[1024,1152]{1,0:T(8,128)} %get-tuple-element.175.grad_ref, f32[16,1152]{1,0:T(8,128)} %get-tuple-element.155.scale_ref.full_scale_ref, ...), custom_call_target="tpu_custom_call" | custom-call | flops 47300001792 | bytes 1048576 | tf_op jit(solution)/shard_map/second_back/pallas_call | solution.py:878
  324.7 6.1 %collective-permute-done.21 = bf16[160,3584]{1,0:T(8,128)(2,1)} collective-permute-done((bf16[160,3584]{1,0:T(8,128)(2,1)}, bf16[160,3584]{1,0:T(8,128)(2,1)}, u32[]{:S(2)}, u32[]{:S(2)}) %collective-permute-start.21) | collective-permute-done | bytes 1146912 | tf_op jit(solution)/shard_map/ppermute | solution.py:797
  330.9 6.1 %add_convert_fusion.3 = (bf16[288,1280]{1,0:T(8,128)(2,1)}, bf16[288,1280]{1,0:T(8,128)(2,1)}, bf16[288,1280]{1,0:T(8,128)(2,1)}, f32[288,1280]{1,0:T(8,128)S(1)}) fusion(f32[1152,1280]{1,0:T(8,128)} %collective-permute-done.19, f32[1152,1280]{1,0:T(8,128)} %get-tuple-element.192), kind=kLoop, calls=%fused_computation.12 | loop fusion | flops 2580480 | bytes 15482880 | tf_op jit(solution)/shard_map/convert_element_type | solution.py:818
  337.0 1.7 collective-permute-start.25
  340.5 3.6 convert_add_fusion
  344.1 24.1 %first_back.2 = (f32[768,384]{1,0:T(8,128)}, f32[25,768]{1,0:T(8,128)}) custom-call(bf16[1024,192]{1,0:T(8,128)(2,1)} %bitcast_select_fusion.x_ref, bf16[1152,384]{1,0:T(8,128)(2,1)} %copy-done.6, bf16[1152,384]{1,0:T(8,128)(2,1)} %get-tuple-element.353.right_ref, f32[25,8,1152]{2,1,0:T(8,128)} %broadcast_in_dim.56.taps_ref, ...), custom_call_target="tpu_custom_call" | custom-call | flops 26400000000 | bytes 1048576 | tf_op jit(solution)/shard_map/first_back/pallas_call | solution.py:878
  368.2 4.2 collective-permute-done.24
  372.4 4.6 add_convert_fusion.6
  377.0 1.6 collective-permute-start.29
  378.6 1.3 collective-permute-start.28
  380.5 1.9 fusion.28
  383.2 1.7 collective-permute-start.32
  384.9 13.2 %first_back.3 = (f32[384,384]{1,0:T(8,128)}, f32[25,384]{1,0:T(8,128)}) custom-call(bf16[1024,192]{1,0:T(8,128)(2,1)} %bitcast_select_fusion.x_ref, bf16[1152,384]{1,0:T(8,128)(2,1)} %copy-done.6, bf16[1152,384]{1,0:T(8,128)(2,1)} %get-tuple-element.353.right_ref, f32[25,8,1152]{2,1,0:T(8,128)} %broadcast_in_dim.56.taps_ref, ...), custom_call_target="tpu_custom_call" | custom-call | flops 13200000000 | bytes 1048576 | tf_op jit(solution)/shard_map/first_back/pallas_call | solution.py:878
  398.1 2.7 collective-permute-start.30
  402.8 5.5 %collective-permute-done.31 = bf16[72,1280]{1,0:T(8,128)(2,1)} collective-permute-done((bf16[72,1280]{1,0:T(8,128)(2,1)}, bf16[72,1280]{1,0:T(8,128)(2,1)}, u32[]{:S(2)}, u32[]{:S(2)}) %collective-permute-start.31) | collective-permute-done | bytes 184352 | tf_op jit(solution)/shard_map/ppermute | solution.py:797
  409.6 1.8 fusion.2
  413.4 1.5 convert_add_fusion.3
  415.4 2.3 fusion.5
  417.8 1.5 collective-permute-start.34
  419.3 1.4 collective-permute-start.36
  421.3 1.9 fusion.20
  423.2 1.7 collective-permute-start.42
  428.8 3.3 collective-permute-done.36
  432.1 6.0 %collective-permute-done.35 = bf16[288,384]{1,0:T(8,128)(2,1)} collective-permute-done((bf16[288,384]{1,0:T(8,128)(2,1)}, bf16[288,384]{1,0:T(8,128)(2,1)}, u32[]{:S(2)}, u32[]{:S(2)}) %collective-permute-start.35) | collective-permute-done | bytes 221216 | tf_op jit(solution)/shard_map/ppermute | solution.py:797
  438.0 1.5 fusion.8
  439.7 1.8 collective-permute-start.39
  441.4 2.7 collective-permute-start.37
  444.2 2.9 collective-permute-done.39
  447.1 3.4 collective-permute-done.38
  452.6 1.5 collective-permute-start.50
  457.0 6.2 %collective-permute-done.44 = f32[33,128]{1,0:T(8,128)S(1)} collective-permute-done((f32[33,128]{1,0:T(8,128)S(1)}, f32[33,128]{1,0:T(8,128)S(1)}, u32[]{:S(2)}, u32[]{:S(2)}) %collective-permute-start.44) | collective-permute-done | bytes 16928 | tf_op jit(solution)/shard_map/ppermute | solution.py:797
  463.2 1.5 collective-permute-start.45
  464.8 2.3 collective-permute-done.45
  468.0 2.8 collective-permute-done.46
  472.4 3.1 collective-permute-done.47
  479.9 5.9 %adamw_head.1 = (f32[40,3560]{1,0:T(8,128)}, f32[40,3560]{1,0:T(8,128)}, f32[40,3560]{1,0:T(8,128)}, f32[40,3560]{1,0:T(8,128)}, bf16[40,3560]{1,0:T(8,128)(2,1)}) custom-call(f32[1]{0:T(128)} %bitcast.21.factor_ref, f32[40,3584]{1,0:T(8,128)} %reduce-scatter.2.cloned.1.call-done.grad, f32[40,3560]{1,0:T(8,128)} %bitcast.56, f32[40,3560]{1,0:T(8,128)} %bitcast.61, ...), custom_call_target="tpu_custom_call" | custom-call | tf_op jit(solution)/shard_map/adamw_head/pallas_call | solution.py:784
  487.9 9.1 %adamw.2 = (f32[288,1826]{1,0:T(8,128)}, f32[288,1826]{1,0:T(8,128)}, f32[288,1826]{1,0:T(8,128)}, f32[288,1826]{1,0:T(8,128)}, bf16[288,1826]{1,0:T(8,128)(2,1)}) custom-call(s32[2]{0:T(128)} %pad_add_fusion.place_ref, f32[1]{0:T(128)} %bitcast.21.factor_ref, bf16[288,1152]{1,0:T(8,128)(2,1)} %copy-done.2, bf16[288,1152]{1,0:T(8,128)(2,1)} %copy-done.5, ...), custom_call_target="tpu_custom_call" | custom-call | tf_op jit(solution)/shard_map/adamw/pallas_call | solution.py:757
  497.9 12.0 %adamw.3 = (f32[288,2800]{1,0:T(8,128)}, f32[288,2800]{1,0:T(8,128)}, f32[288,2800]{1,0:T(8,128)}, f32[288,2800]{1,0:T(8,128)}, bf16[288,2800]{1,0:T(8,128)(2,1)}) custom-call(s32[2]{0:T(128)} %pad_add_fusion.place_ref, f32[1]{0:T(128)} %bitcast.21.factor_ref, bf16[288,1152]{1,0:T(8,128)(2,1)} %copy-done.2, bf16[288,1152]{1,0:T(8,128)(2,1)} %copy-done.5, ...), custom_call_target="tpu_custom_call" | custom-call | tf_op jit(solution)/shard_map/adamw/pallas_call | solution.py:757
  (227 shorter events, 54.2 us)
Async XLA Ops:
  7.2 179.1 %copy-start = (s32[64]{0:T(128)S(1)}, s32[64]{0:T(128)}, u32[]{:S(2)}) copy-start(s32[64]{0:T(128)} %param.21) | copy-start | bytes 772
  11.4 11.6 %copy-start.7 = (f32[3560,40]{0,1:T(8,128)S(1)}, f32[3560,40]{0,1:T(8,128)}, u32[]{:S(2)}) copy-start(f32[3560,40]{0,1:T(8,128)} %param.32) | copy-start | bytes 1708804
  11.9 15.0 %collective-permute-start.2 = (bf16[288,384]{1,0:T(8,128)(2,1)S(1)}, bf16[288,384]{1,0:T(8,128)(2,1)S(1)}, u32[]{:S(2)}, u32[]{:S(2)}) collective-permute-start(bf16[288,384]{1,0:T(8,128)(2,1)S(1)} %pad_maximum_fusion.5), channel_id=1, source_target_pairs={{0,3},{1,2},{2,1},{3,0},{4,7},{5,6},{6,5},{7,4},{8,11},{9,10},{10,... | collective-permute-start | bytes 663560 | tf_op jit(solution)/shard_map/ppermute | solution.py:797
  17.0 25.4 %collective-permute-start.1 = (bf16[288,384]{1,0:T(8,128)(2,1)S(1)}, bf16[288,384]{1,0:T(8,128)(2,1)S(1)}, u32[]{:S(2)}, u32[]{:S(2)}) collective-permute-start(bf16[288,384]{1,0:T(8,128)(2,1)S(1)} %pad_maximum_fusion.5), channel_id=1, source_target_pairs={{0,2},{1,3},{2,0},{3,1},{4,6},{5,7},{6,4},{7,5},{8,10},{9,11},{10,... | collective-permute-start | bytes 663560 | tf_op jit(solution)/shard_map/ppermute | solution.py:797
  17.0 25.4 %collective-permute-start = (bf16[288,384]{1,0:T(8,128)(2,1)S(1)}, bf16[288,384]{1,0:T(8,128)(2,1)S(1)}, u32[]{:S(2)}, u32[]{:S(2)}) collective-permute-start(bf16[288,384]{1,0:T(8,128)(2,1)S(1)} %pad_maximum_fusion.5), channel_id=1, source_target_pairs={{0,1},{1,0},{2,3},{3,2},{4,5},{5,4},{6,7},{7,6},{8,9},{9,8},{10,11... | collective-permute-start | bytes 663560 | tf_op jit(solution)/shard_map/ppermute | solution.py:797
  17.7 29.4 %all-to-all-start = ((bf16[64,16,192]{2,1,0:T(8,128)(2,1)}), bf16[64,16,192]{2,1,0:T(8,128)(2,1)S(1)}, u32[]{:S(2)}, u32[]{:S(2)}) async-start(bf16[64,16,192]{2,1,0:T(8,128)(2,1)} %param.20), calls=%async_computation | async-start | bytes 1048576 | tf_op jit(solution)/shard_map/all_to_all | solution.py:958
  22.7 75.8 %all-gather.3.cloned.1.call-start = ((), (), s32[]{:S(2)}) async-start(), calls=%async_computation.2 | async-start | bytes 1433600 | tf_op jit(solution)/shard_map/all_gather | solution.py:967
  47.1 11.9 %collective-permute-start.6 = (bf16[72,768]{1,0:T(8,128)(2,1)S(1)}, bf16[72,768]{1,0:T(8,128)(2,1)S(1)}, u32[]{:S(2)}, u32[]{:S(2)}) collective-permute-start(bf16[72,768]{1,0:T(8,128)(2,1)S(1)} %fusion.19), channel_id=1, source_target_pairs={{0,3},{1,2},{2,1},{3,0},{4,7},{5,6},{6,5},{7,4},{8,11},{9,10},{10,... | collective-permute-start | bytes 331784 | tf_op jit(solution)/shard_map/ppermute | solution.py:797
  49.7 9.2 %collective-permute-start.5 = (bf16[72,768]{1,0:T(8,128)(2,1)S(1)}, bf16[72,768]{1,0:T(8,128)(2,1)S(1)}, u32[]{:S(2)}, u32[]{:S(2)}) collective-permute-start(bf16[72,768]{1,0:T(8,128)(2,1)S(1)} %fusion.19), channel_id=1, source_target_pairs={{0,2},{1,3},{2,0},{3,1},{4,6},{5,7},{6,4},{7,5},{8,10},{9,11},{10,... | collective-permute-start | bytes 331784 | tf_op jit(solution)/shard_map/ppermute | solution.py:797
  49.7 9.2 %collective-permute-start.4 = (bf16[72,768]{1,0:T(8,128)(2,1)S(1)}, bf16[72,768]{1,0:T(8,128)(2,1)S(1)}, u32[]{:S(2)}, u32[]{:S(2)}) collective-permute-start(bf16[72,768]{1,0:T(8,128)(2,1)S(1)} %fusion.19), channel_id=1, source_target_pairs={{0,1},{1,0},{2,3},{3,2},{4,5},{5,4},{6,7},{7,6},{8,9},{9,8},{10,11... | collective-permute-start | bytes 331784 | tf_op jit(solution)/shard_map/ppermute | solution.py:797
  52.6 133.5 %all-gather.5.cloned.1.call-start = ((), (), s32[]{:S(2)}) async-start(), calls=%async_computation.3 | async-start | bytes 5734400 | tf_op jit(solution)/shard_map/all_gather | solution.py:1049
  52.7 9.8 %collective-permute-start.10 = (bf16[72,1280]{1,0:T(8,128)(2,1)S(1)}, bf16[72,1280]{1,0:T(8,128)(2,1)S(1)}, u32[]{:S(2)}, u32[]{:S(2)}) collective-permute-start(bf16[72,1280]{1,0:T(8,128)(2,1)S(1)} %dynamic_slice.81), channel_id=1, source_target_pairs={{0,1},{1,0},{2,3},{3,2},{4,5},{5,4},{6,7},{7,6},{8,9},{9,8},{10,11... | collective-permute-start | bytes 552968 | tf_op jit(solution)/shard_map/ppermute | solution.py:797
  53.2 10.6 %collective-permute-start.3 = (bf16[1152,384]{1,0:T(8,128)(2,1)S(1)}, bf16[1152,384]{1,0:T(8,128)(2,1)S(1)}, u32[]{:S(2)}, u32[]{:S(2)}) collective-permute-start(bf16[1152,384]{1,0:T(8,128)(2,1)S(1)} %bitcast.50), channel_id=1, source_target_pairs={{0,4},{4,0},{1,5},{5,1},{2,6},{6,2},{3,7},{7,3},{8,12},{12,8},{9,1... | collective-permute-start | bytes 2654216 | tf_op jit(solution)/shard_map/ppermute | solution.py:797
  59.0 38.3 %collective-permute-start.9 = (bf16[288,768]{1,0:T(8,128)(2,1)S(1)}, bf16[288,768]{1,0:T(8,128)(2,1)S(1)}, u32[]{:S(2)}, u32[]{:S(2)}) collective-permute-start(bf16[288,768]{1,0:T(8,128)(2,1)S(1)} %constant_dynamic-update-slice_fusion), channel_id=1, source_target_pairs={{0,24},{8,16},{16,8},{24,0},{1,25},{9,17},{17,9},{25,1},{2,26},{10... | collective-permute-start | bytes 1327112 | tf_op jit(solution)/shard_map/ppermute | solution.py:797
  61.5 35.8 %collective-permute-start.8 = (bf16[288,768]{1,0:T(8,128)(2,1)S(1)}, bf16[288,768]{1,0:T(8,128)(2,1)}, u32[]{:S(2)}, u32[]{:S(2)}) collective-permute-start(bf16[288,768]{1,0:T(8,128)(2,1)S(1)} %constant_dynamic-update-slice_fusion), channel_id=1, source_target_pairs={{0,16},{8,24},{16,0},{24,8},{1,17},{9,25},{17,1},{25,9},{2,18},{10... | collective-permute-start | bytes 1327112 | tf_op jit(solution)/shard_map/ppermute | solution.py:797
  62.0 35.3 %collective-permute-start.7 = (bf16[288,768]{1,0:T(8,128)(2,1)S(1)}, bf16[288,768]{1,0:T(8,128)(2,1)}, u32[]{:S(2)}, u32[]{:S(2)}) collective-permute-start(bf16[288,768]{1,0:T(8,128)(2,1)S(1)} %constant_dynamic-update-slice_fusion), channel_id=1, source_target_pairs={{0,8},{8,0},{16,24},{24,16},{1,9},{9,1},{17,25},{25,17},{2,10},{10... | collective-permute-start | bytes 1327112 | tf_op jit(solution)/shard_map/ppermute | solution.py:797
  62.5 34.7 %collective-permute-start.11 = (bf16[144,1280]{1,0:T(8,128)(2,1)S(1)}, bf16[144,1280]{1,0:T(8,128)(2,1)}, u32[]{:S(2)}, u32[]{:S(2)}) collective-permute-start(bf16[144,1280]{1,0:T(8,128)(2,1)S(1)} %constant_dynamic-update-slice_fusion.4), channel_id=1, source_target_pairs={{0,2},{1,3},{2,0},{3,1},{4,6},{5,7},{6,4},{7,5},{8,10},{9,11},{10,... | collective-permute-start | bytes 1105928 | tf_op jit(solution)/shard_map/ppermute | solution.py:797
  103.8 6.3 %collective-permute-start.12 = (bf16[1152,768]{1,0:T(8,128)(2,1)}, bf16[1152,768]{1,0:T(8,128)(2,1)}, u32[]{:S(2)}, u32[]{:S(2)}) collective-permute-start(bf16[1152,768]{1,0:T(8,128)(2,1)} %constant_dynamic-update-slice_fusion.6.own_ref), channel_id=1, source_target_pairs={{0,4},{4,0},{1,5},{5,1},{2,6},{6,2},{3,7},{7,3},{8,12},{12,8},{9,1... | collective-permute-start | bytes 5308424 | tf_op jit(solution)/shard_map/ppermute | solution.py:797
  106.5 27.1 %collective-permute-start.15 = (bf16[288,1280]{1,0:T(8,128)(2,1)S(1)}, bf16[288,1280]{1,0:T(8,128)(2,1)S(1)}, u32[]{:S(2)}, u32[]{:S(2)}) collective-permute-start(bf16[288,1280]{1,0:T(8,128)(2,1)S(1)} %constant_dynamic-update-slice_fusion.10), channel_id=1, source_target_pairs={{0,24},{8,16},{16,8},{24,0},{1,25},{9,17},{17,9},{25,1},{2,26},{10... | collective-permute-start | bytes 2211848 | tf_op jit(solution)/shard_map/ppermute | solution.py:797
  109.0 45.4 %collective-permute-start.14 = (bf16[288,1280]{1,0:T(8,128)(2,1)S(1)}, bf16[288,1280]{1,0:T(8,128)(2,1)S(1)}, u32[]{:S(2)}, u32[]{:S(2)}) collective-permute-start(bf16[288,1280]{1,0:T(8,128)(2,1)S(1)} %constant_dynamic-update-slice_fusion.10), channel_id=1, source_target_pairs={{0,16},{8,24},{16,0},{24,8},{1,17},{9,25},{17,1},{25,9},{2,18},{10... | collective-permute-start | bytes 2211848 | tf_op jit(solution)/shard_map/ppermute | solution.py:797
  109.5 45.0 %collective-permute-start.13 = (bf16[288,1280]{1,0:T(8,128)(2,1)S(1)}, bf16[288,1280]{1,0:T(8,128)(2,1)S(1)}, u32[]{:S(2)}, u32[]{:S(2)}) collective-permute-start(bf16[288,1280]{1,0:T(8,128)(2,1)S(1)} %constant_dynamic-update-slice_fusion.10), channel_id=1, source_target_pairs={{0,8},{8,0},{16,24},{24,16},{1,9},{9,1},{17,25},{25,17},{2,10},{10... | collective-permute-start | bytes 2211848 | tf_op jit(solution)/shard_map/ppermute | solution.py:797
  110.1 305.4 %reduce-scatter.2.cloned.1.call-start = ((), (), s32[]{:S(2)}) async-start(), calls=%async_computation.4 | async-start | bytes 2867200 | tf_op jit(solution)/shard_map/reduce_scatter | solution.py:1183
  158.1 5.6 %collective-permute-start.16 = (bf16[1152,1280]{1,0:T(8,128)(2,1)}, bf16[1152,1280]{1,0:T(8,128)(2,1)S(1)}, u32[]{:S(2)}, u32[]{:S(2)}) collective-permute-start(bf16[1152,1280]{1,0:T(8,128)(2,1)} %constant_dynamic-update-slice_fusion.12.own_ref), channel_id=1, source_target_pairs={{0,4},{4,0},{1,5},{5,1},{2,6},{6,2},{3,7},{7,3},{8,12},{12,8},{9,1... | collective-permute-start | bytes 8847368 | tf_op jit(solution)/shard_map/ppermute | solution.py:797
  186.1 8.1 %collective-permute-start.17 = (bf16[640,3584]{1,0:T(8,128)(2,1)}, bf16[640,3584]{1,0:T(8,128)(2,1)}, u32[]{:S(2)}, u32[]{:S(2)}) collective-permute-start(bf16[640,3584]{1,0:T(8,128)(2,1)} %all-gather.5.cloned.1.call-done.own_ref), channel_id=1, source_target_pairs={{0,4},{4,0},{1,5},{5,1},{2,6},{6,2},{3,7},{7,3},{8,12},{12,8},{9,1... | collective-permute-start | bytes 13762568 | tf_op jit(solution)/shard_map/ppermute | solution.py:797
  241.5 30.1 %collective-permute-start.18 = (bf16[640,3584]{1,0:T(8,128)(2,1)}, bf16[640,3584]{1,0:T(8,128)(2,1)}, u32[]{:S(2)}, u32[]{:S(2)}) collective-permute-start(bf16[640,3584]{1,0:T(8,128)(2,1)} %get-tuple-element.174), channel_id=1, source_target_pairs={{0,4},{4,0},{1,5},{5,1},{2,6},{6,2},{3,7},{7,3},{8,12},{12,8},{9,1... | collective-permute-start | bytes 13762568 | tf_op jit(solution)/shard_map/ppermute | solution.py:797
  271.2 59.6 %collective-permute-start.19 = (f32[1152,1280]{1,0:T(8,128)}, f32[1152,1280]{1,0:T(8,128)}, u32[]{:S(2)}, u32[]{:S(2)}) collective-permute-start(f32[1152,1280]{1,0:T(8,128)} %get-tuple-element.187), channel_id=1, source_target_pairs={{0,4},{4,0},{1,5},{5,1},{2,6},{6,2},{3,7},{7,3},{8,12},{12,8},{9,1... | collective-permute-start | bytes 17694728 | tf_op jit(solution)/shard_map/ppermute | solution.py:797
  277.7 46.9 %collective-permute-start.22 = (bf16[160,3584]{1,0:T(8,128)(2,1)}, bf16[160,3584]{1,0:T(8,128)(2,1)S(1)}, u32[]{:S(2)}, u32[]{:S(2)}) collective-permute-start(bf16[160,3584]{1,0:T(8,128)(2,1)} %get-tuple-element.332), channel_id=1, source_target_pairs={{0,24},{8,16},{16,8},{24,0},{1,25},{9,17},{17,9},{25,1},{2,26},{10... | collective-permute-start | bytes 3440648 | tf_op jit(solution)/shard_map/ppermute | solution.py:797
  279.4 51.4 %collective-permute-start.21 = (bf16[160,3584]{1,0:T(8,128)(2,1)}, bf16[160,3584]{1,0:T(8,128)(2,1)}, u32[]{:S(2)}, u32[]{:S(2)}) collective-permute-start(bf16[160,3584]{1,0:T(8,128)(2,1)} %get-tuple-element.333), channel_id=1, source_target_pairs={{0,16},{8,24},{16,0},{24,8},{1,17},{9,25},{17,1},{25,9},{2,18},{10... | collective-permute-start | bytes 3440648 | tf_op jit(solution)/shard_map/ppermute | solution.py:797
  280.7 50.1 %collective-permute-start.20 = (bf16[160,3584]{1,0:T(8,128)(2,1)}, bf16[160,3584]{1,0:T(8,128)(2,1)}, u32[]{:S(2)}, u32[]{:S(2)}) collective-permute-start(bf16[160,3584]{1,0:T(8,128)(2,1)} %get-tuple-element.334), channel_id=1, source_target_pairs={{0,8},{8,0},{16,24},{24,16},{1,9},{9,1},{17,25},{25,17},{2,10},{10... | collective-permute-start | bytes 3440648 | tf_op jit(solution)/shard_map/ppermute | solution.py:797
  324.6 47.8 %collective-permute-start.26 = (f32[1152,768]{1,0:T(8,128)}, f32[1152,768]{1,0:T(8,128)}, u32[]{:S(2)}, u32[]{:S(2)}) collective-permute-start(f32[1152,768]{1,0:T(8,128)} %get-tuple-element.194), channel_id=1, source_target_pairs={{0,4},{4,0},{1,5},{5,1},{2,6},{6,2},{3,7},{7,3},{8,12},{12,8},{9,1... | collective-permute-start | bytes 10616840 | tf_op jit(solution)/shard_map/ppermute | solution.py:797
  337.0 31.2 %collective-permute-start.25 = (bf16[288,1280]{1,0:T(8,128)(2,1)}, bf16[288,1280]{1,0:T(8,128)(2,1)}, u32[]{:S(2)}, u32[]{:S(2)}) collective-permute-start(bf16[288,1280]{1,0:T(8,128)(2,1)} %get-tuple-element.328), channel_id=1, source_target_pairs={{0,24},{8,16},{16,8},{24,0},{1,25},{9,17},{17,9},{25,1},{2,26},{10... | collective-permute-start | bytes 2211848 | tf_op jit(solution)/shard_map/ppermute | solution.py:797
  338.7 33.8 %collective-permute-start.24 = (bf16[288,1280]{1,0:T(8,128)(2,1)}, bf16[288,1280]{1,0:T(8,128)(2,1)}, u32[]{:S(2)}, u32[]{:S(2)}) collective-permute-start(bf16[288,1280]{1,0:T(8,128)(2,1)} %get-tuple-element.329), channel_id=1, source_target_pairs={{0,16},{8,24},{16,0},{24,8},{1,17},{9,25},{17,1},{25,9},{2,18},{10... | collective-permute-start | bytes 2211848 | tf_op jit(solution)/shard_map/ppermute | solution.py:797
  339.9 32.5 %collective-permute-start.23 = (bf16[288,1280]{1,0:T(8,128)(2,1)}, bf16[288,1280]{1,0:T(8,128)(2,1)}, u32[]{:S(2)}, u32[]{:S(2)}) collective-permute-start(bf16[288,1280]{1,0:T(8,128)(2,1)} %get-tuple-element.330), channel_id=1, source_target_pairs={{0,8},{8,0},{16,24},{24,16},{1,9},{9,1},{17,25},{25,17},{2,10},{10... | collective-permute-start | bytes 2211848 | tf_op jit(solution)/shard_map/ppermute | solution.py:797
  377.0 31.5 %collective-permute-start.29 = (bf16[288,768]{1,0:T(8,128)(2,1)}, bf16[288,768]{1,0:T(8,128)(2,1)}, u32[]{:S(2)}, u32[]{:S(2)}) collective-permute-start(bf16[288,768]{1,0:T(8,128)(2,1)} %get-tuple-element.336), channel_id=1, source_target_pairs={{0,24},{8,16},{16,8},{24,0},{1,25},{9,17},{17,9},{25,1},{2,26},{10... | collective-permute-start | bytes 1327112 | tf_op jit(solution)/shard_map/ppermute | solution.py:797
  378.6 29.8 %collective-permute-start.28 = (bf16[288,768]{1,0:T(8,128)(2,1)}, bf16[288,768]{1,0:T(8,128)(2,1)}, u32[]{:S(2)}, u32[]{:S(2)}) collective-permute-start(bf16[288,768]{1,0:T(8,128)(2,1)} %get-tuple-element.337), channel_id=1, source_target_pairs={{0,16},{8,24},{16,0},{24,8},{1,17},{9,25},{17,1},{25,9},{2,18},{10... | collective-permute-start | bytes 1327112 | tf_op jit(solution)/shard_map/ppermute | solution.py:797
  380.0 28.5 %collective-permute-start.27 = (bf16[288,768]{1,0:T(8,128)(2,1)}, bf16[288,768]{1,0:T(8,128)(2,1)}, u32[]{:S(2)}, u32[]{:S(2)}) collective-permute-start(bf16[288,768]{1,0:T(8,128)(2,1)} %get-tuple-element.338), channel_id=1, source_target_pairs={{0,8},{8,0},{16,24},{24,16},{1,9},{9,1},{17,25},{25,17},{2,10},{10... | collective-permute-start | bytes 1327112 | tf_op jit(solution)/shard_map/ppermute | solution.py:797
  383.2 17.6 %copy-start.18 = (f32[25,1152]{1,0:T(8,128)S(1)}, f32[25,1152]{1,0:T(8,128)}, u32[]{:S(2)}) copy-start(f32[25,1152]{1,0:T(8,128)} %get-tuple-element.208) | copy-start | bytes 345604
  383.2 17.6 %copy-start.21 = (f32[25,768]{1,0:T(8,128)S(1)}, f32[25,768]{1,0:T(8,128)}, u32[]{:S(2)}) copy-start(f32[25,768]{1,0:T(8,128)} %get-tuple-element.206) | copy-start | bytes 230404
  383.2 14.9 %collective-permute-start.32 = (bf16[72,1280]{1,0:T(8,128)(2,1)S(1)}, bf16[72,1280]{1,0:T(8,128)(2,1)}, u32[]{:S(2)}, u32[]{:S(2)}) collective-permute-start(bf16[72,1280]{1,0:T(8,128)(2,1)S(1)} %get-tuple-element.361), channel_id=1, source_target_pairs={{0,3},{1,2},{2,1},{3,0},{4,7},{5,6},{6,5},{7,4},{8,11},{9,10},{10,... | collective-permute-start | bytes 552968 | tf_op jit(solution)/shard_map/ppermute | solution.py:797
  398.1 10.2 %collective-permute-start.31 = (bf16[72,1280]{1,0:T(8,128)(2,1)}, bf16[72,1280]{1,0:T(8,128)(2,1)}, u32[]{:S(2)}, u32[]{:S(2)}) collective-permute-start(bf16[72,1280]{1,0:T(8,128)(2,1)} %get-tuple-element.362), channel_id=1, source_target_pairs={{0,2},{1,3},{2,0},{3,1},{4,6},{5,7},{6,4},{7,5},{8,10},{9,11},{10,... | collective-permute-start | bytes 552968 | tf_op jit(solution)/shard_map/ppermute | solution.py:797
  398.1 10.3 %collective-permute-start.30 = (bf16[72,1280]{1,0:T(8,128)(2,1)}, bf16[72,1280]{1,0:T(8,128)(2,1)}, u32[]{:S(2)}, u32[]{:S(2)}) collective-permute-start(bf16[72,1280]{1,0:T(8,128)(2,1)} %get-tuple-element.363), channel_id=1, source_target_pairs={{0,1},{1,0},{2,3},{3,2},{4,5},{5,4},{6,7},{7,6},{8,9},{9,8},{10,11... | collective-permute-start | bytes 552968 | tf_op jit(solution)/shard_map/ppermute | solution.py:797
  411.4 4.0 collective-permute-start.33
  417.8 10.4 %collective-permute-start.34 = (bf16[288,384]{1,0:T(8,128)(2,1)}, bf16[288,384]{1,0:T(8,128)(2,1)}, u32[]{:S(2)}, u32[]{:S(2)}) collective-permute-start(bf16[288,384]{1,0:T(8,128)(2,1)} %get-tuple-element.340), channel_id=1, source_target_pairs={{0,8},{8,0},{16,24},{24,16},{1,9},{9,1},{17,25},{25,17},{2,10},{10... | collective-permute-start | bytes 663560 | tf_op jit(solution)/shard_map/ppermute | solution.py:797
  419.3 12.8 %collective-permute-start.36 = (bf16[288,384]{1,0:T(8,128)(2,1)}, bf16[288,384]{1,0:T(8,128)(2,1)}, u32[]{:S(2)}, u32[]{:S(2)}) collective-permute-start(bf16[288,384]{1,0:T(8,128)(2,1)} %get-tuple-element.341), channel_id=1, source_target_pairs={{0,24},{8,16},{16,8},{24,0},{1,25},{9,17},{17,9},{25,1},{2,26},{10... | collective-permute-start | bytes 663560 | tf_op jit(solution)/shard_map/ppermute | solution.py:797
  420.7 17.4 %collective-permute-start.35 = (bf16[288,384]{1,0:T(8,128)(2,1)}, bf16[288,384]{1,0:T(8,128)(2,1)}, u32[]{:S(2)}, u32[]{:S(2)}) collective-permute-start(bf16[288,384]{1,0:T(8,128)(2,1)} %get-tuple-element.342), channel_id=1, source_target_pairs={{0,16},{8,24},{16,0},{24,8},{1,17},{9,25},{17,1},{25,9},{2,18},{10... | collective-permute-start | bytes 663560 | tf_op jit(solution)/shard_map/ppermute | solution.py:797
  423.2 18.2 %collective-permute-start.42 = (bf16[72,1280]{1,0:T(8,128)(2,1)S(1)}, bf16[72,1280]{1,0:T(8,128)(2,1)}, u32[]{:S(2)}, u32[]{:S(2)}) collective-permute-start(bf16[72,1280]{1,0:T(8,128)(2,1)S(1)} %get-tuple-element.237), channel_id=1, source_target_pairs={{0,24},{8,16},{16,8},{24,0},{1,25},{9,17},{17,9},{25,1},{2,26},{10... | collective-permute-start | bytes 552968 | tf_op jit(solution)/shard_map/ppermute | solution.py:797
  424.9 19.3 %collective-permute-start.41 = (bf16[72,1280]{1,0:T(8,128)(2,1)S(1)}, bf16[72,1280]{1,0:T(8,128)(2,1)}, u32[]{:S(2)}, u32[]{:S(2)}) collective-permute-start(bf16[72,1280]{1,0:T(8,128)(2,1)S(1)} %get-tuple-element.237), channel_id=1, source_target_pairs={{0,16},{8,24},{16,0},{24,8},{1,17},{9,25},{17,1},{25,9},{2,18},{10... | collective-permute-start | bytes 552968 | tf_op jit(solution)/shard_map/ppermute | solution.py:797
  428.2 15.9 %collective-permute-start.40 = (bf16[72,1280]{1,0:T(8,128)(2,1)S(1)}, bf16[72,1280]{1,0:T(8,128)(2,1)S(1)}, u32[]{:S(2)}, u32[]{:S(2)}) collective-permute-start(bf16[72,1280]{1,0:T(8,128)(2,1)S(1)} %get-tuple-element.237), channel_id=1, source_target_pairs={{0,8},{8,0},{16,24},{24,16},{1,9},{9,1},{17,25},{25,17},{2,10},{10... | collective-permute-start | bytes 552968 | tf_op jit(solution)/shard_map/ppermute | solution.py:797
  439.6 12.3 %copy-start.17 = (f32[32,128]{1,0:T(8,128)S(1)}, f32[32,128]{1,0:T(8,128)}, u32[]{:S(2)}) copy-start(f32[32,128]{1,0:T(8,128)} %reshape.144) | copy-start | bytes 49156
  439.7 7.4 %collective-permute-start.39 = (bf16[72,1152]{1,0:T(8,128)(2,1)S(1)}, bf16[72,1152]{1,0:T(8,128)(2,1)S(1)}, u32[]{:S(2)}, u32[]{:S(2)}) collective-permute-start(bf16[72,1152]{1,0:T(8,128)(2,1)S(1)} %get-tuple-element.364), channel_id=1, source_target_pairs={{0,3},{1,2},{2,1},{3,0},{4,7},{5,6},{6,5},{7,4},{8,11},{9,10},{10,... | collective-permute-start | bytes 497672 | tf_op jit(solution)/shard_map/ppermute | solution.py:797
  441.4 9.0 %collective-permute-start.38 = (bf16[72,1152]{1,0:T(8,128)(2,1)S(1)}, bf16[72,1152]{1,0:T(8,128)(2,1)S(1)}, u32[]{:S(2)}, u32[]{:S(2)}) collective-permute-start(bf16[72,1152]{1,0:T(8,128)(2,1)S(1)} %get-tuple-element.365), channel_id=1, source_target_pairs={{0,2},{1,3},{2,0},{3,1},{4,6},{5,7},{6,4},{7,5},{8,10},{9,11},{10,... | collective-permute-start | bytes 497672 | tf_op jit(solution)/shard_map/ppermute | solution.py:797
  441.4 9.0 %collective-permute-start.37 = (bf16[72,1152]{1,0:T(8,128)(2,1)S(1)}, bf16[72,1152]{1,0:T(8,128)(2,1)S(1)}, u32[]{:S(2)}, u32[]{:S(2)}) collective-permute-start(bf16[72,1152]{1,0:T(8,128)(2,1)S(1)} %get-tuple-element.366), channel_id=1, source_target_pairs={{0,1},{1,0},{2,3},{3,2},{4,5},{5,4},{6,7},{7,6},{8,9},{9,8},{10,11... | collective-permute-start | bytes 497672 | tf_op jit(solution)/shard_map/ppermute | solution.py:797
  451.9 4.2 collective-permute-start.43
  452.6 26.9 %collective-permute-start.50 = (bf16[72,1152]{1,0:T(8,128)(2,1)S(1)}, bf16[72,1152]{1,0:T(8,128)(2,1)S(1)}, u32[]{:S(2)}, u32[]{:S(2)}) collective-permute-start(bf16[72,1152]{1,0:T(8,128)(2,1)S(1)} %get-tuple-element.359), channel_id=1, source_target_pairs={{0,24},{8,16},{16,8},{24,0},{1,25},{9,17},{17,9},{25,1},{2,26},{10... | collective-permute-start | bytes 497672 | tf_op jit(solution)/shard_map/ppermute | solution.py:797
  454.1 25.3 %collective-permute-start.49 = (bf16[72,1152]{1,0:T(8,128)(2,1)S(1)}, bf16[72,1152]{1,0:T(8,128)(2,1)S(1)}, u32[]{:S(2)}, u32[]{:S(2)}) collective-permute-start(bf16[72,1152]{1,0:T(8,128)(2,1)S(1)} %get-tuple-element.359), channel_id=1, source_target_pairs={{0,16},{8,24},{16,0},{24,8},{1,17},{9,25},{17,1},{25,9},{2,18},{10... | collective-permute-start | bytes 497672 | tf_op jit(solution)/shard_map/ppermute | solution.py:797
  454.9 24.6 %collective-permute-start.48 = (bf16[72,1152]{1,0:T(8,128)(2,1)S(1)}, bf16[72,1152]{1,0:T(8,128)(2,1)S(1)}, u32[]{:S(2)}, u32[]{:S(2)}) collective-permute-start(bf16[72,1152]{1,0:T(8,128)(2,1)S(1)} %get-tuple-element.359), channel_id=1, source_target_pairs={{0,8},{8,0},{16,24},{24,16},{1,9},{9,1},{17,25},{25,17},{2,10},{10... | collective-permute-start | bytes 497672 | tf_op jit(solution)/shard_map/ppermute | solution.py:797
  456.1 7.1 %collective-permute-start.44 = (f32[33,128]{1,0:T(8,128)S(1)}, f32[33,128]{1,0:T(8,128)S(1)}, u32[]{:S(2)}, u32[]{:S(2)}) collective-permute-start(f32[33,128]{1,0:T(8,128)S(1)} %fusion.25), channel_id=1, source_target_pairs={{0,8},{8,0},{16,24},{24,16},{1,9},{9,1},{17,25},{25,17},{2,10},{10... | collective-permute-start | bytes 50696 | tf_op jit(solution)/shard_map/ppermute | solution.py:797
  463.2 3.8 collective-permute-start.45
  467.0 3.8 collective-permute-start.46
  470.8 4.7 collective-permute-start.47
  472.3 13.5 %copy-start.10 = (bf16[288,1280]{1,0:T(8,128)(2,1)}, bf16[288,1280]{1,0:T(8,128)(2,1)S(1)}, u32[]{:S(2)}) copy-start(bf16[288,1280]{1,0:T(8,128)(2,1)S(1)} %constant_dynamic-update-slice_fusion.18.refs_2_) | copy-start | bytes 2211844
  472.3 24.7 %collective-permute-start.52 = (bf16[288,1280]{1,0:T(8,128)(2,1)S(1)}, bf16[288,1280]{1,0:T(8,128)(2,1)S(1)}, u32[]{:S(2)}, u32[]{:S(2)}) collective-permute-start(bf16[288,1280]{1,0:T(8,128)(2,1)S(1)} %constant_dynamic-update-slice_fusion.18.refs_2_), channel_id=1, source_target_pairs={{0,4},{4,0},{1,5},{5,1},{2,6},{6,2},{3,7},{7,3},{8,12},{12,8},{9,1... | collective-permute-start | bytes 2211848 | tf_op jit(solution)/shard_map/ppermute | solution.py:797
  479.6 7.5 %collective-permute-start.51 = (bf16[288,1152]{1,0:T(8,128)(2,1)S(1)}, bf16[288,1152]{1,0:T(8,128)(2,1)S(1)}, u32[]{:S(2)}, u32[]{:S(2)}) collective-permute-start(bf16[288,1152]{1,0:T(8,128)(2,1)S(1)} %pad_maximum_fusion.2.refs_0_), channel_id=1, source_target_pairs={{0,4},{4,0},{1,5},{5,1},{2,6},{6,2},{3,7},{7,3},{8,12},{12,8},{9,1... | collective-permute-start | bytes 1990664 | tf_op jit(solution)/shard_map/ppermute | solution.py:797
  497.9 12.0 %copy-start.1 = (s32[64]{0:T(128)S(1)}, s32[64]{0:T(128)}, u32[]{:S(2)}) copy-start(s32[64]{0:T(128)} %param.21) | copy-start | bytes 772
  (23 other events, 130.7 us)
Sparse Core Ops, SparseCore 0:
  52.8 45.7 all-gather.2
  110.2 72.7 all-gather.4
  344.2 46.3 reduce-scatter.1

commit v3 on v2

--- a/solution.py
+++ b/solution.py
@@ -33,6 +33,7 @@
 F32 = jnp.float32
 BF16 = jnp.bfloat16
 FLOPS_A_MICRO = 1.1e9
+HBM = "hbm"
 VMEM_BYTES = 60 * 1024 * 1024
 
 
@@ -58,6 +59,10 @@
     return lax.dot_general(
         left, right, (((0,), (0,)), ((), ())), precision=HIGH, preferred_element_type=F32
     )
+
+
+def turn(values):
+    return values.T
 
 
 def sig(values):
@@ -109,29 +114,29 @@
 
 def depthwise_weight(source, grad, lanes, batch, store):
     parts = batch // 8
-    total = {}
-    for down in range(MAP):
-        slopes = {
-            (spot, part): grad[pl.ds((down * MAP + spot) * batch + 8 * part, 8), lanes]
-            for spot in range(MAP)
-            for part in range(parts)
-        }
-        for step_y in range(-2, 3):
+    for step_y in range(-2, 3):
+        total = {}
+        for down in range(MAP):
             line = down + step_y
             if not 0 <= line < MAP:
                 continue
-            for spot in range(MAP):
-                for part in range(parts):
+            for part in range(parts):
+                slopes = [
+                    grad[pl.ds((down * MAP + spot) * batch + 8 * part, 8), lanes]
+                    for spot in range(MAP)
+                ]
+                for spot in range(MAP):
                     value = source[pl.ds((line * MAP + spot) * batch + 8 * part, 8), lanes]
                     for step_x in range(-2, 3):
                         place = spot - step_x
                         if not 0 <= place < MAP:
                             continue
-                        tap = (step_y + 2) * KERNEL + step_x + 2
-                        term = value * slopes[(place, part)]
-                        total[tap] = total[tap] + term if tap in total else term
-    for tap in range(TAPS):
-        store(tap, jnp.sum(total[tap], axis=0, keepdims=True))
+                        key = (step_x, spot % 2)
+                        term = value * slopes[place]
+                        total[key] = total[key] + term if key in total else term
+        for step_x in range(-2, 3):
+            value = total[(step_x, 0)] + total[(step_x, 1)]
+            store((step_y + 2) * KERNEL + step_x + 2, jnp.sum(value, axis=0, keepdims=True))
 
 
 def pair_gates(gates, width):
@@ -171,12 +176,14 @@
     line = MAP * batch
     step = pl.program_id(0)
 
+    act[...] = nt(x_ref[...], left_ref[:, :C0])
+
     def expand(index):
         rows = rows_at(index, line)
-        value = nt(x_ref[rows, :], left_ref[:, :C0])
         for part in range(tile // LANES):
-            here = value[:, part * LANES : (part + 1) * LANES]
-            act[rows, part * LANES : (part + 1) * LANES] = here * sig(here) * mask_ref[rows, :]
+            lanes = slice(part * LANES, (part + 1) * LANES)
+            here = act[rows, lanes]
+            act[rows, lanes] = here * sig(here) * mask_ref[rows, :]
 
     loop(MAP, expand)
 
@@ -253,12 +260,12 @@
     half = own_ref.shape[1]
 
     def expand(index):
-        rows = rows_at(index, 2 * line)
+        rows = rows_at(index, 4 * line)
         mixed_ref[rows, :] = nt(wide_ref[rows, :half], own_ref[...]) + nt(
             wide_ref[rows, half:], far_ref[...]
         )
 
-    loop(MAP // 2, expand)
+    loop(MAP // 4, expand)
 
     def activate(index):
         rows = rows_at(index, line)
@@ -308,12 +315,13 @@
 
 def project(
     conv_ref, scale_ref, own_ref, far_ref, mask_ref, count_ref, gates_ref, route_ref,
-    each_ref, twice_ref, wide_ref, mean_ref, gate_ref, head_gates_ref,
+    each_ref, twice_ref, mean_ref, gate_ref, head_gates_ref,
     scaled,
 ):
     batch = count_ref.shape[0]
     line = MAP * batch
-    width = scaled.shape[1]
+    block, width = scaled.shape
+    step = pl.program_id(0)
 
     def activate(index):
         rows = rows_at(index, line)
@@ -323,72 +331,80 @@
             kept = grouped(here * sig(here) * mask_ref[rows, :], batch)
             scaled[rows, lanes] = flat(kept * scale_ref[:, lanes][None]).astype(BF16)
 
-    loop(MAP, activate)
-    mean_ref[...] = jnp.zeros_like(mean_ref)
+    loop(block // line, activate)
     pairs = HALF // 2
 
-    def mix(index):
-        rows = rows_at(index, 2 * line)
-        value = scaled[rows, :]
-        total = None
-        for pair in range(HALF):
-            weights = own_ref if pair < pairs else far_ref
-            inner = slice((pair % pairs) * 2 * C2, (pair % pairs + 1) * 2 * C2)
-            each = nn(value, weights[:, inner])
-            each_ref[rows, pair * 2 * C2 : (pair + 1) * 2 * C2] = each.astype(BF16)
-            term = grouped(each, batch) * gates_ref[pair][None]
-            total = term if total is None else total + term
-        total = flat(total)
-        value = total[:, :C2] + total[:, C2:]
-        low = value.astype(BF16)
-        twice_ref[rows, :C2] = low
-        twice_ref[rows, C2:] = low
-        kept = grouped(value * mask_ref[rows, :1], batch)
-        mean_ref[...] += jnp.sum(kept, axis=0)
-
-    loop(MAP // 2, mix)
-    mean_ref[...] = mean_ref[...] / count_ref[:, :1]
-    gates = jax.nn.sigmoid(high_nn(mean_ref[...], route_ref[...]))
-    gate_ref[...] = gates
-    for pair, value in enumerate(pair_gates(gates, C2)):
-        head_gates_ref[pair] = value
-
-    def widen(index):
-        rows = rows_at(index, line)
-        value = grouped(twice_ref[rows, :].astype(F32), batch)
-        for pair in range(HALF):
-            lanes = slice(pair * 2 * C2, (pair + 1) * 2 * C2)
-            wide_ref[rows, lanes] = flat(value * head_gates_ref[pair][None]).astype(BF16)
-
-    loop(MAP, widen)
+    @pl.when(step == 0)
+    def _():
+        mean_ref[...] = jnp.zeros_like(mean_ref)
+
+    value = scaled[...]
+    total = None
+    for pair in range(HALF):
+        weights = own_ref if pair < pairs else far_ref
+        inner = slice((pair % pairs) * 2 * C2, (pair % pairs + 1) * 2 * C2)
+        each = nn(value, weights[:, inner])
+        each_ref[:, pair * 2 * C2 : (pair + 1) * 2 * C2] = each.astype(BF16)
+        term = grouped(each, batch) * gates_ref[pair][None]
+        total = term if total is None else total + term
+    total = flat(total)
+    value = total[:, :C2] + total[:, C2:]
+    low = value.astype(BF16)
+    twice_ref[:, :C2] = low
+    twice_ref[:, C2:] = low
+    kept = grouped(value * mask_ref[:, :1], batch)
+    mean_ref[...] += jnp.sum(kept, axis=0)
+
+    @pl.when(step == pl.num_programs(0) - 1)
+    def _():
+        mean_ref[...] = mean_ref[...] / count_ref[:, :1]
+        gates = jax.nn.sigmoid(high_nn(mean_ref[...], route_ref[...]))
+        gate_ref[...] = gates
+        for pair, value in enumerate(pair_gates(gates, C2)):
+            head_gates_ref[pair] = value
 
 
 def head(
-    wide_ref, twice_ref, own_ref, far_ref, mask_ref, count_ref, label_ref, class_ref,
+    twice_ref, near_ref, distant_ref, mask_ref, count_ref, label_ref, class_ref,
     gates_ref, gate_ref, mean_ref, route_ref,
     own_grad_ref, far_grad_ref, loss_ref, hidden_grad_ref, route_grad_ref,
-    mixed, slopes, turned, pooled, total, means, logit_slopes,
+    weights, wide_ref, mixed, slopes, turned, pooled, total, means, logit_slopes, arrivals,
 ):
     batch = count_ref.shape[0]
     line = MAP * batch
     step = pl.program_id(0)
-    half = own_ref.shape[0]
+    half = near_ref.shape[0]
     experts = NE * C2
     columns = own_grad_ref.shape[1]
-    sides = (own_ref, far_ref)
 
     @pl.when(step == 0)
     def _():
+        loads = [
+            pltpu.make_async_copy(
+                source, weights.at[pl.ds(side * half, half), :], arrivals.at[side]
+            )
+            for side, source in enumerate((near_ref, distant_ref))
+        ]
+        for load in loads:
+            load.start()
         pooled[...] = jnp.zeros_like(pooled)
-        for side, weights in enumerate(sides):
-
-            def expand(index, side=side, weights=weights):
-                rows = rows_at(index, 2 * line)
-                mixed[rows, side * half : (side + 1) * half] = nt(
-                    wide_ref[rows, :], weights[:, :experts]
-                )
-
-            loop(MAP // 2, expand)
+
+        def widen(index):
+            rows = rows_at(index, line)
+            value = grouped(twice_ref[rows, :].astype(F32), batch)
+            for pair in range(HALF):
+                lanes = slice(pair * 2 * C2, (pair + 1) * 2 * C2)
+                wide_ref[rows, lanes] = flat(value * gates_ref[pair][None]).astype(BF16)
+
+        loop(MAP, widen)
+        for load in loads:
+            load.wait()
+
+        def expand(index):
+            rows = rows_at(index, 4 * line)
+            mixed[rows, :] = nt(wide_ref[rows, :], weights[:, :experts])
+
+        loop(MAP // 4, expand)
 
         def pool(index):
             rows = rows_at(index, line)
@@ -400,7 +416,7 @@
 
         loop(MAP, pool)
         mean = (pooled[...] / count_ref[:, :1]).astype(BF16)
-        logits = nn(mean[:, :half], own_ref[:, experts : experts + CLASSES]) + nn(mean[:, half:], far_ref[:, experts : experts + CLASSES])
+        logits = nn(mean, weights[:, experts : experts + CLASSES])
         spots = lax.broadcasted_iota(jnp.int32, logits.shape, 1)
         onehot = (spots == label_ref[...]).astype(F32)
         weight = jnp.sum(onehot * class_ref[...], axis=1, keepdims=True)
@@ -413,9 +429,7 @@
         means[...] = mean
         logit_slopes[...] = jnp.zeros_like(logit_slopes)
         logit_slopes[:, :CLASSES] = logit_grad
-        for side, weights in enumerate(sides):
-            place = slice(side * half, (side + 1) * half)
-            pooled[:, place] = nt(logit_grad, weights[:, experts : experts + CLASSES]) / count_ref[:, :1]
+        pooled[...] = nt(logit_grad, weights[:, experts : experts + CLASSES]) / count_ref[:, :1]
 
         def back(index):
             rows = rows_at(index, line)
@@ -427,9 +441,8 @@
 
         loop(MAP, back)
         for part in range(2 * half // LANES):
-            turned[part * LANES : (part + 1) * LANES, :] = slopes[
-                :, part * LANES : (part + 1) * LANES
-            ].T
+            lanes = slice(part * LANES, (part + 1) * LANES)
+            turned[lanes, :] = turn(slopes[:, lanes])
 
     blocks = pl.num_programs(0) // 2
     side = 1 - step // blocks
@@ -437,20 +450,20 @@
     place = pl.ds(pl.multiple_of(side * half, half), half)
 
     def weight_grad(out):
-        @pl.when(block < experts // columns)
-        def _():
-            out[...] = nn(
-                turned[place, :],
-                wide_ref[:, pl.ds(pl.multiple_of(block * columns, columns), columns)],
-            ).astype(out.dtype)
-
-        @pl.when(block >= experts // columns)
-        def _():
-            begin = pl.multiple_of(block * columns - experts, columns)
-            out[...] = lax.dot_general(
-                means[:, place], logit_slopes[:, pl.ds(begin, columns)],
-                (((0,), (0,)), ((), ())), preferred_element_type=F32,
-            ).astype(out.dtype)
+        for index in range(2):
+
+            @pl.when(block == index)
+            def _(index=index):
+                begin = index * columns
+                width = min(columns, experts - begin)
+                out[:, :width] = nn(turned[place, :], wide_ref[:, begin : begin + width]).astype(
+                    out.dtype
+                )
+                if width < columns:
+                    out[:, width:] = lax.dot_general(
+                        means[:, place], logit_slopes[...],
+                        (((0,), (0,)), ((), ())), preferred_element_type=F32,
+                    ).astype(out.dtype)
 
     @pl.when(side == 1)
     def _():
@@ -466,13 +479,15 @@
 
         def pull(index, sums):
             rows = rows_at(index, 2 * line)
-            left, right = (slopes[rows, :half], slopes[rows, half:])
+            value = slopes[rows, :]
             hidden = grouped(twice_ref[rows, :].astype(F32), batch)
             summed = None
             sums = list(sums)
             for pair in range(HALF):
-                lanes = slice(pair * 2 * C2, (pair + 1) * 2 * C2)
-                each = grouped(nn(left, own_ref[:, lanes]) + nn(right, far_ref[:, lanes]), batch)
+                if pair % 2 == 0:
+                    begin = pair * 2 * C2
+                    both = nn(value, weights[:, begin : begin + 4 * C2])
+                each = grouped(both[:, 2 * C2 * (pair % 2) : 2 * C2 * (pair % 2 + 1)], batch)
                 sums[pair] = sums[pair] + jnp.sum(each * hidden, axis=0)
                 term = each * gates_ref[pair][None]
                 summed = term if summed is None else summed + term
@@ -499,19 +514,20 @@
 
 
 def project_back(
-    hidden_ref, gates_ref, each_ref, own_ref, far_ref, conv_ref, scale_ref, mask_ref,
+    hidden_ref, gates_ref, far_each_ref, own_ref, far_ref, conv_ref, scale_ref, mask_ref,
     full_scale_ref, units_ref, mean_ref, excite_ref,
     grad_ref, own_grad_ref, far_grad_ref, gate_sum_ref, unit_grad_ref, small_ref,
-    spread, scaled, sums,
+    spread, scaled, sums, each_ref, arrival,
 ):
     batch, tile = scale_ref.shape
     line = MAP * batch
     step = pl.program_id(0)
     half = own_ref.shape[1]
+    arriving = pltpu.make_async_copy(far_each_ref, each_ref, arrival)
 
     @pl.when(step == 0)
     def _():
-        gate_sum_ref[...] = jnp.zeros_like(gate_sum_ref)
+        arriving.start()
 
         def widen(index):
             rows = rows_at(index, line)
@@ -519,18 +535,16 @@
             for pair in range(HALF):
                 lanes = slice(pair * 2 * C2, (pair + 1) * 2 * C2)
                 spread[rows, lanes] = flat(value * gates_ref[pair][None]).astype(BF16)
-                each = grouped(each_ref[rows, lanes].astype(F32), batch)
-                gate_sum_ref[pair] += jnp.sum(each * value, axis=0)
 
         loop(MAP, widen)
 
     def pull(index):
-        rows = rows_at(index, 2 * line)
+        rows = rows_at(index, 4 * line)
         grad_ref[rows, :] = nt(spread[rows, :half], own_ref[...]) + nt(
             spread[rows, half:], far_ref[...]
         )
 
-    loop(MAP // 2, pull)
+    loop(MAP // 4, pull)
     place = pl.ds(pl.multiple_of(step * tile, tile), tile)
     sums[:, place] = jnp.zeros((batch, tile), F32)
 
@@ -545,12 +559,24 @@
             sums[:, pl.ds(pl.multiple_of(step * tile + part * LANES, LANES), LANES)] += added
 
     loop(MAP, activate)
-    turned = scaled[...].T
+    turned = turn(scaled[...])
     far_grad_ref[...] = nn(turned, spread[:, half:])
     own_grad_ref[...] = nn(turned, spread[:, :half])
 
     @pl.when(step == pl.num_programs(0) - 1)
     def _():
+        arriving.wait()
+        gate_sum_ref[...] = jnp.zeros_like(gate_sum_ref)
+
+        def weigh(index):
+            rows = rows_at(index, line)
+            value = grouped(hidden_ref[rows, :].astype(F32), batch)
+            for pair in range(HALF):
+                lanes = slice(pair * 2 * C2, (pair + 1) * 2 * C2)
+                each = grouped(each_ref[rows, lanes].astype(F32), batch)
+                gate_sum_ref[pair] += jnp.sum(each * value, axis=0)
+
+        loop(MAP, weigh)
         scale = full_scale_ref[...]
         pre = sums[...] * scale * (1.0 - scale)
         units = units_ref[...]
@@ -617,7 +643,7 @@
             )
 
     loop(MAP, deactivate)
-    turned = slopes[:, place].T
+    turned = turn(slopes[:, place])
     far_grad_ref[...] = nn(turned, wide_ref[:, half:])
     own_grad_ref[...] = nn(turned, wide_ref[:, :half])
 
@@ -671,22 +697,22 @@
 
     def expand(index):
         rows = rows_at(index, line)
-        value = nt(x_ref[rows, :], left_ref[:, :C0])
-        grad = nt(hidden_ref[rows, :], right_ref[:, :C0])
         for part in range(tile // LANES):
             lanes = slice(part * LANES, (part + 1) * LANES)
             mask = mask_ref[rows, :]
-            here = value[:, lanes]
+            here = act[rows, lanes]
             gate = sig(here)
             act[rows, lanes] = here * gate * mask
             wide[rows, lanes] = slope(here, gate) * mask
             here = conv_ref[rows, lanes]
             gate = sig(here)
             deep[rows, lanes] = (here * gate * mask).astype(BF16)
-            inner[rows, lanes] = grad[:, lanes] * mask * slope(here, gate)
-
+            inner[rows, lanes] = inner[rows, lanes] * mask * slope(here, gate)
+
+    act[...] = nt(x_ref[...], left_ref[:, :C0])
+    inner[...] = nt(hidden_ref[...], right_ref[:, :C0])
     loop(MAP, expand)
-    weight_grad_ref[:, C0:] = nn(deep[...].T, hidden_ref[...])
+    weight_grad_ref[:, C0:] = nn(turn(deep[...]), hidden_ref[...])
 
     def conv(index):
         lanes = lanes_at(index)
@@ -710,7 +736,7 @@
             deep[rows, lanes] = (act[rows, lanes] * wide[rows, lanes]).astype(BF16)
 
     loop(MAP, deactivate)
-    weight_grad_ref[:, :C0] = nn(deep[...].T, x_ref[...])
+    weight_grad_ref[:, :C0] = nn(turn(deep[...]), x_ref[...])
 
 
 def adamw_values(master, first, second, average, grad):
@@ -722,6 +748,13 @@
     return (first, second, master, average, master.astype(BF16))
 
 
+def clipped(total):
+    routers = total[: total.shape[0] - 1]
+    squares, weight = total[total.shape[0] - 1 :, :1], total[total.shape[0] - 1 :, 2:3]
+    norm = jnp.sqrt(squares + jnp.sum(routers * routers, keepdims=True)) / weight
+    return norm, jnp.minimum(1.0, CLIP / (norm + 1e-06)) / weight
+
+
 def adamw_kernel(segments, arrays, place_ref, factor_ref, *refs):
     pieces = refs[: 2 * arrays]
     master, first, second, average = refs[2 * arrays : 2 * arrays + 4]
@@ -741,7 +774,7 @@
         def _(core=core):
             fill(core)
 
-    grad = whole[...] * factor_ref[0]
+    grad = whole[...] * factor_ref[0, 1]
     values = adamw_values(master[...], first[...], second[...], average[...], grad)
     for out, value in zip(outs, values):
         out[...] = value
@@ -769,27 +802,29 @@
     )(spot, factor, *pieces, master, first, second, average)
 
 
-def adamw_head_kernel(factor_ref, grad, master, first, second, average, *outs):
-    grad = grad[...] * factor_ref[0]
-    values = adamw_values(master[...], first[...], second[...], average[...], grad)
+def adamw_head_kernel(total_ref, grad, master, first, second, average, *outs):
+    norm, factor = clipped(total_ref[...])
+    outs[5][...] = jnp.concatenate([norm, factor], axis=1)
+    values = adamw_values(master[...], first[...], second[...], average[...], grad[...] * factor)
     for out, value in zip(outs, values):
         out[...] = value
 
 
-def adamw_head(factor, grad, *state):
+def adamw_head(total, grad, *state):
     height, width = state[0].shape
-    part = 4 * LANES
+    part = 14 * LANES
     block = pl.BlockSpec((height, part), lambda i: (0, i))
     types = (F32, F32, F32, F32, BF16)
     return pl.pallas_call(
         adamw_head_kernel,
         grid=(pl.cdiv(width, part),),
-        in_specs=[pl.BlockSpec(memory_space=pltpu.SMEM)] + [block] * 5,
-        out_specs=[block] * 5,
-        out_shape=[jax.ShapeDtypeStruct((height, width), kind) for kind in types],
+        in_specs=[pl.BlockSpec(total.shape, lambda i: (0, 0))] + [block] * 5,
+        out_specs=[block] * 5 + [pl.BlockSpec((1, 2), lambda i: (0, 0))],
+        out_shape=[jax.ShapeDtypeStruct((height, width), kind) for kind in types]
+        + [jax.ShapeDtypeStruct((1, 2), F32)],
         compiler_params=pltpu.CompilerParams(vmem_limit_bytes=VMEM_BYTES),
         name="adamw_head",
-    )(factor, grad, *state)
+    )(total, grad, *state)
 
 
 def swap(values, axis, distance):
@@ -862,6 +897,8 @@
 
 def call(kernel, grid, ins, outs, scratch, name, micros):
     def spec(shape, block, index):
+        if block is HBM:
+            return pl.BlockSpec(memory_space=pl.ANY)
         if block is None:
             return pl.BlockSpec(memory_space=pltpu.VMEM)
         return pl.BlockSpec(block, index)
@@ -951,20 +988,19 @@
     project_own = lax.dynamic_slice(
         row, (place * height, C0 + SE + core * HALF * C2), (height, HALF * C2)
     ).astype(BF16)
-    part = 4 * LANES
-    blocks = pl.cdiv(NE * C2 + CLASSES, part)
+    blocks = 2
+    part = pl.cdiv(NE * C2 + CLASSES, blocks * LANES) * LANES
     lanes = blocks * part
     head_own = jnp.pad(head_master.T.astype(BF16), ((0, 0), (0, lanes - NE * C2 - CLASSES)))
     mine = lax.all_to_all(images, "chan", 0, 0, tiled=True)
-    small, expand_own, project_own, head_own, mine = meet(
-        copies(small, "chan"), expand_own, project_own, head_own, mine
+    small, expand_own, project_own, mine = meet(
+        copies(small, "chan"), expand_own, project_own, mine
     )
     small = joined(small).reshape(chans, places, height, 2 * C0)
     small = small.transpose(1, 0, 2, 3).reshape(wide, 2 * C0)
     small_far = swap(small, "core", 1)
     expand_own = copies(expand_own, "chan")
     project_own = joined([project_own, swap(project_own, "chan", 1)])
-    head_own = lax.all_gather(head_own, "chan", axis=0, tiled=True)
     expand_own = joined(expand_own)
     left = jnp.where(first_core, small, small_far)
     right = jnp.where(first_core, small_far, small)
@@ -997,6 +1033,11 @@
     inside = ((spots // MAP)[:, None] < side[None, :]) & ((spots % MAP)[:, None] < side[None, :])
     inside = inside.reshape(rows, 1)
     x = jnp.where(inside, mine.reshape(rows, C0), 0)
+    x, expand_own, project_own, head_own = meet(x, expand_own, project_own, head_own)
+    expand_own, project_own = joined(expand_own), joined(project_own)
+    head_own = lax.all_gather(head_own, "chan", axis=0, tiled=True)
+    expand_far = swap(expand_own, "core", 1)
+    project_own = copies(project_own, "xy")
     mask = jnp.broadcast_to(inside.astype(F32), (rows, LANES))
     count = jnp.broadcast_to((side * side).astype(F32)[:, None], (batch, LANES))
 
@@ -1040,15 +1081,16 @@
             pltpu.VMEM((rows, C0), F32),
         ],
         "first_forward",
-        20,
+        17,
     )
 
     (conv_one, mixed_in, twice_one, mean_one, gate_one, gates_one, gates_mid) = first_out
-    mixed_in, expand_own, project_own, head_own = meet(mixed_in, expand_own, project_own, head_own)
-    expand_own, project_own = joined(expand_own), joined(project_own)
+    mixed_in, expand_far, project_own, head_own = meet(
+        mixed_in, expand_far, project_own, head_own
+    )
+    project_own = joined(project_own)
+    project_far = swap(project_own, "core", 1)
     head_own = lax.all_gather(head_own, "xy", axis=0, tiled=True)
-    expand_far = swap(expand_own, "core", 1)
-    project_own = copies(project_own, "xy")
 
     mixed_two, conv_two, mean_two, units, scale = call(
         second_forward,
@@ -1066,41 +1108,46 @@
         ],
         [pltpu.VMEM((rows, tile), F32)],
         "second_forward",
-        22,
-    )
-
-    conv_two, project_own = meet(conv_two, project_own)
-    project_own = joined(project_own)
-    project_far = swap(project_own, "core", 1)
-
-    each, twice_two, mixed_head, mean_three, gate_two, gates_two = call(
+        21,
+    )
+
+    conv_two, project_far = meet(conv_two, project_far)
+
+    line = rows // 4
+
+    def out_rows(width, kind):
+        return ((rows, width), kind, (line, width), lambda i: (i, 0))
+
+    def by_rows(array):
+        return (array, (line, array.shape[1]), lambda i: (i, 0))
+
+    each, twice_two, mean_three, gate_two, gates_two = call(
         project,
-        (),
-        [
-            fixed(conv_two), fixed(scale), fixed(project_own), fixed(project_far), fixed(mask),
-            fixed(count), fixed(gates_mid), fixed(route_out),
-        ],
-        [
-            ((rows, NE * C2), BF16, None, None),
-            ((rows, 2 * C2), BF16, None, None),
-            ((rows, NE * C2), BF16, None, None),
-            ((batch, C2), F32, None, None),
-            ((batch, NE), F32, None, None),
-            ((HALF, batch, 2 * C2), F32, None, None),
-        ],
-        [pltpu.VMEM((rows, wide), BF16)],
+        (rows // line,),
+        [
+            by_rows(conv_two), whole(scale), whole(project_own), whole(project_far),
+            by_rows(mask), whole(count), whole(gates_mid), whole(route_out),
+        ],
+        [
+            out_rows(NE * C2, BF16),
+            out_rows(2 * C2, BF16),
+            out_full((batch, C2), F32),
+            out_full((batch, NE), F32),
+            out_full((HALF, batch, 2 * C2), F32),
+        ],
+        [pltpu.VMEM((line, wide), BF16)],
         "project",
-        20,
-    )
-
-    mixed_head, head_own = meet(mixed_head, head_own)
+        16,
+    )
+
+    twice_two, head_own = meet(twice_two, head_own)
     head_far = swap(head_own, "core", 1)
     half = head_own.shape[0]
     head_grad_own, head_grad_far, losses, hidden_two, route_grad_out = call(
         head,
         (2 * blocks,),
         [
-            whole(mixed_head), whole(twice_two), whole(head_own), whole(head_far), whole(mask),
+            whole(twice_two), (head_own, HBM, None), (head_far, HBM, None), whole(mask),
             whole(count), whole(label[:, None]), whole(class_weight[None, :]), whole(gates_two),
             whole(gate_two), whole(mean_three), whole(route_out),
         ],
@@ -1112,13 +1159,14 @@
             out_full((C2, NE), F32),
         ],
         [
+            pltpu.VMEM((2 * half, lanes), BF16), pltpu.VMEM((rows, NE * C2), BF16),
             pltpu.VMEM((rows, 2 * half), F32), pltpu.VMEM((rows, 2 * half), BF16),
             pltpu.VMEM((2 * half, rows), BF16), pltpu.VMEM((batch, 2 * half), F32),
             pltpu.VMEM((rows, C2), F32), pltpu.VMEM((batch, 2 * half), BF16),
-            pltpu.VMEM((batch, lanes - NE * C2), BF16),
+            pltpu.VMEM((batch, lanes - NE * C2), BF16), pltpu.SemaphoreType.DMA((2,)),
         ],
         "head",
-        45,
+        39,
     )
     head_came = swap(head_grad_far, "core", 1)
 
@@ -1126,7 +1174,7 @@
         project_back,
         (tiles,),
         [
-            whole(hidden_two), whole(gates_mid), whole(each), tiled(project_own),
+            whole(hidden_two), whole(gates_mid), (each, HBM, None), tiled(project_own),
             tiled(project_far), across(conv_two), across(scale), whole(mask), whole(scale),
             whole(units), whole(mean_two), whole(excite_out),
         ],
@@ -1140,10 +1188,11 @@
         ],
         [
             pltpu.VMEM((rows, NE * C2), BF16), pltpu.VMEM((rows, tile), BF16),
-            pltpu.VMEM((batch, wide), F32),
+            pltpu.VMEM((batch, wide), F32), pltpu.VMEM((rows, NE * C2), BF16),
+            pltpu.SemaphoreType.DMA(()),
         ],
         "project_back",
-        29,
+        26,
     )
     deep_grad, head_came = meet(deep_grad, head_came)
     high_rows = half // places
@@ -1177,7 +1226,7 @@
             pltpu.VMEM((wide, HALF * C0), BF16),
         ],
         "second_back",
-        43,
+        38,
     )
     hidden_one, project_came, head_parts = meet(hidden_one, project_came, head_parts)
     head_shard = lax.psum_scatter(added(head_parts), "chan", scatter_dimension=0, tiled=True)
@@ -1205,17 +1254,17 @@
                 pltpu.VMEM((rows, tile), F32), pltpu.VMEM((rows, tile), BF16),
             ],
             "first_back",
-            12 * count_,
+            10 * count_,
         )
 
     start_grad, tap_grad_start = first_back_tiles(0, tiles - 1, hidden_one)
-    start_grad, hidden_one, project_parts, expand_came = meet(
-        start_grad, hidden_one, project_parts, expand_came
+    start_grad, tap_grad_start, hidden_one, project_parts, expand_came = meet(
+        start_grad, tap_grad_start, hidden_one, project_parts, expand_came
     )
     expand_parts = exchange(pair_sum(expand_grad_own, expand_came, places), "xy")
-    project_parts = exchange(split(added(project_parts), chans), "chan")
+    project_middle = added(project_parts)
     end_grad, tap_grad_end = first_back_tiles(tiles - 1, 1, hidden_one)
-    end_grad, expand_parts, project_parts = meet(end_grad, expand_parts, project_parts)
+    end_grad, tap_grad_end, expand_parts = meet(end_grad, tap_grad_end, expand_parts)
     weight_grad = joined([start_grad, end_grad])
     tap_grad_one = jnp.concatenate([tap_grad_start, tap_grad_end], 1)
 
@@ -1227,8 +1276,10 @@
     right_grad = jnp.pad(right_grad, ((0, 0), (0, small_width - right_grad.shape[1])))
     small_own = jnp.where(first_core, left_grad, right_grad)
     small_came = swap(jnp.where(first_core, right_grad, left_grad), "core", 1)
-    small_came, project_parts, head_shard = meet(small_came, project_parts, head_shard)
+    small_came, head_shard = meet(small_came, head_shard)
     small_parts = exchange(pair_sum(small_own, small_came, places), "xy")
+    project_parts = exchange(split(project_middle, chans), "chan")
+    small_parts, project_parts = meet(small_parts, project_parts)
     project_shard = added(project_parts)
     small_middle = added(small_parts)
     mixed_middle = jnp.concatenate([small_middle, added(expand_parts)], 1)
@@ -1246,10 +1297,11 @@
     packed = jnp.concatenate([route_grad.reshape(-1, LANES), jnp.pad(scalars, (0, LANES - 3))[None]])
     packed = total_sum(packed)
     route_sum = packed[:-1].reshape(route_grad.shape)
-    square_sum, loss_total, weight_total = packed[-1, 0], packed[-1, 1], packed[-1, 2]
-    clip_norm = jnp.sqrt(square_sum + jnp.sum(route_sum * route_sum)) / weight_total
-    factor = jnp.minimum(1.0, CLIP / (clip_norm + 1e-06)) / weight_total
-    scalar = factor[None]
+    loss_total, weight_total = packed[-1, 1], packed[-1, 2]
+    *head_out, clip_pair = adamw_head(
+        packed, head_shard, head_master.T, head_first.T, head_second.T, head_average.T
+    )
+    clip_norm, factor = clip_pair[0, 0], clip_pair[0, 1]
 
     if height % 8 == 0:
         line, spot = height, jnp.stack([place, core])
@@ -1260,7 +1312,7 @@
     project_pair = [project_mine, swap(project_mine, "core", 1)]
     mixed_pair = [mixed_mine, swap(mixed_mine, "core", 1)]
     column_out = adamw(
-        scalar,
+        clip_pair,
         spot,
         line,
         mixed_pair,
@@ -1276,7 +1328,7 @@
         column_average.T,
     )
     row_out = adamw(
-        scalar,
+        clip_pair,
         spot,
         line,
         mixed_pair + project_pair,
@@ -1285,9 +1337,6 @@
         row_first,
         row_second,
         row_average,
-    )
-    head_out = adamw_head(
-        scalar, head_shard, head_master.T, head_first.T, head_second.T, head_average.T
     )
     route_out_new = adamw_values(
         route_master, route_first, route_second, route_average, route_sum * factor

time: 524 us -> 496 us (0.947)
  Pallas kernels: 248 us -> 216 us
  starting transfers between devices: 58.1 us -> 64 us
    pallas_call x8, Pallas kernels: 221 us -> 191 us  [call(): pl.pallas_call(kernel, grid=grid, in_specs=in_specs, out_specs=[spec(shap...]
    all_gather x1, waiting for transfers between devices: 0.01 us -> 7.09 us  [on_device(): head_own = lax.all_gather(head_own, 'xy', axis=0, tiled=True)]
    ppermute x53, starting transfers between devices: 53 us -> 58.6 us  [swap(): return lax.ppermute(values, axis, [(i, i ^ distance) for i in range(size)])]
    unnamed x74 -> x98, local copies, waits for them, and re-layouts: 13.7 us -> 14.7 us
  transfers between devices with their start and end apart: 57 -> 57, of which waited for: 22 -> 20; matrix products, arithmetic and copies ran while one was open for 11% -> 14% of each run, Pallas kernels for 36% -> 34%
where the time goes in v3:
time: 496 us; the launch traced here: 490 us
  Pallas kernels  216 us (44%)
  waiting for transfers between devices  117 us (24%)
  starting transfers between devices  64 us (13%)
  other arithmetic  42.6 us (9%)
  local copies, waits for them, and re-layouts  33.5 us (7%)
  between operations  16.8 us (3%)
    pallas_call x8, Pallas kernels, call(): pl.pallas_call(kernel, grid=grid, in_specs=in_specs, out_specs=[spec(shap...  191 us
    ppermute x53, waiting for transfers between devices, swap(): return lax.ppermute(values, axis, [(i, i ^ distance) for i in range(size)])  105 us
    ppermute x53, starting transfers between devices, swap(): return lax.ppermute(values, axis, [(i, i ^ distance) for i in range(size)])  58.6 us
    pallas_call x2, Pallas kernels, adamw(): pl.pallas_call(functools.partial(adamw_kernel, segments, len(pieces) // 2...  21.2 us
    convert_element_type x4, other arithmetic, exchange(): block.astype(BF16)  18.6 us
    unnamed x98, local copies, waits for them, and re-layouts  14.7 us
  transfers between devices with their start and end apart: 57, of which 20 were waited for; matrix products, arithmetic and copies ran while one was open for 14% of the time, Pallas kernels for 34%

profile of v3, /device:TPU:0, one launch (start us, length us, event | category | flops | bytes accessed | tf_op | source)
XLA Modules:
  0.0 489.9 jit_solution(4387053247548970718)
XLA Ops:
  11.9 5.1 %collective-permute-start.2 = (bf16[288,384]{1,0:T(8,128)(2,1)S(1)}, bf16[288,384]{1,0:T(8,128)(2,1)S(1)}, u32[]{:S(2)}, u32[]{:S(2)}) collective-permute-start(bf16[288,384]{1,0:T(8,128)(2,1)S(1)} %pad_maximum_fusion.5), channel_id=1, source_target_pairs={{0,3},{1,2},{2,1},{3,0},{4,7},{5,6},{6,5},{7,4},{8,11},{9,10},{10,... | collective-permute-start | bytes 663560 | tf_op jit(solution)/shard_map/ppermute | solution.py:832
  17.7 5.0 %all-to-all-start = ((bf16[64,16,192]{2,1,0:T(8,128)(2,1)}), bf16[64,16,192]{2,1,0:T(8,128)(2,1)S(1)}, u32[]{:S(2)}, u32[]{:S(2)}) async-start(bf16[64,16,192]{2,1,0:T(8,128)(2,1)} %param.20), calls=%async_computation | async-start | bytes 1048576 | tf_op jit(solution)/shard_map/all_to_all | solution.py:995
  27.4 15.0 %collective-permute-done.1 = bf16[288,384]{1,0:T(8,128)(2,1)S(1)} collective-permute-done((bf16[288,384]{1,0:T(8,128)(2,1)S(1)}, bf16[288,384]{1,0:T(8,128)(2,1)S(1)}, u32[]{:S(2)}, u32[]{:S(2)}) %collective-permute-start.1) | collective-permute-done | bytes 221216 | tf_op jit(solution)/shard_map/ppermute | solution.py:832
  42.4 4.6 all-to-all-done
  47.1 2.6 collective-permute-start.5
  49.7 1.7 collective-permute-start.3
  51.8 7.1 %collective-permute-done.3 = bf16[72,768]{1,0:T(8,128)(2,1)S(1)} collective-permute-done((bf16[72,768]{1,0:T(8,128)(2,1)S(1)}, bf16[72,768]{1,0:T(8,128)(2,1)S(1)}, u32[]{:S(2)}, u32[]{:S(2)}) %collective-permute-start.3) | collective-permute-done | bytes 110624 | tf_op jit(solution)/shard_map/ppermute | solution.py:832
  59.0 2.5 collective-permute-start.8
  65.3 14.3 %collective-permute-done.10 = bf16[144,1280]{1,0:T(8,128)(2,1)S(1)} collective-permute-done((bf16[144,1280]{1,0:T(8,128)(2,1)S(1)}, bf16[144,1280]{1,0:T(8,128)(2,1)S(1)}, u32[]{:S(2)}, u32[]{:S(2)}) %collective-permute-start.10) | collective-permute-done | bytes 368672 | tf_op jit(solution)/shard_map/ppermute | solution.py:832
  81.4 2.3 collective-permute-start.15
  85.8 1.8 constant_dynamic-update-slice_fusion.8
  89.2 2.2 broadcast_select_fusion
  95.3 17.8 %first_forward.1 = (f32[1024,1152]{1,0:T(8,128)}, bf16[1024,1536]{1,0:T(8,128)(2,1)}, bf16[1024,384]{1,0:T(8,128)(2,1)}, f32[16,192]{1,0:T(8,128)}, f32[16,8]{1,...) custom-call(bf16[1024,192]{1,0:T(8,128)(2,1)} %bitcast_select_fusion.x_ref, bf16[1152,384]{1,0:T(8,128)(2,1)} %copy-done.6, ...), custom_call_target="tpu_custom_call" | custom-call | flops 18699999232 | bytes 1048576 | tf_op jit(solution)/shard_map/first_forward/pallas_call | solution.py:915
  113.1 3.6 collective-permute-done.14
  118.1 2.0 constant_dynamic-update-slice_fusion.14
  120.1 2.1 constant_dynamic-update-slice_fusion.13
  122.2 2.1 constant_dynamic-update-slice_fusion.12.own_ref
  125.4 1.4 convert_add_fusion.4
  127.9 21.2 %second_forward.1 = (f32[1024,1152]{1,0:T(8,128)}, f32[1024,1152]{1,0:T(8,128)}, f32[16,1152]{1,0:T(8,128)}, f32[16,48]{1,0:T(8,128)}, f32[16,1152]{1,0:T(8,128)}) custom-call(bf16[1024,1536]{1,0:T(8,128)(2,1)} %get-tuple-element.158.wide_ref, bf16[1152,768]{1,0:T(8,128)(2,1)} %constant_dynamic-update-slice_fusion.6.own_ref, ...), custom_call_target="tpu_custom_call" | custom-call | flops 23100000256 | bytes 1048576 | tf_op jit(solution)/shard_map/second_forward/pallas_call | solution.py:915
  149.1 15.7 %project.1 = (bf16[1024,2560]{1,0:T(8,128)(2,1)}, bf16[1024,640]{1,0:T(8,128)(2,1)}, f32[16,320]{1,0:T(8,128)}, f32[16,8]{1,0:T(8,128)}, f32[4,16,640]{2,1,0:T(8,128)}) custom-call(f32[1024,1152]{1,0:T(8,128)} %get-tuple-element.165.conv_ref, f32[16,1152]{1,0:T(8,128)} %get-tuple-element.166.scale_ref.full_scale_ref, ...), custom_call_target="tpu_custom_call" | custom-call | flops 17600000000 | bytes 1048576 | tf_op jit(solution)/shard_map/project/pallas_call | solution.py:915
  164.8 7.1 %all-gather.5.cloned.1.call-done.near_ref = bf16[640,3584]{1,0:T(8,128)(2,1)} async-done(((bf16[160,3584]{1,0:T(8,128)(2,1)}), bf16[640,3584]{1,0:T(8,128)(2,1)}) %all-gather.5.cloned.1.call-update) | async-done | bytes 4587536 | tf_op jit(solution)/shard_map/all_gather | solution.py:1093
  172.7 7.3 %collective-permute-done.17.distant_ref = bf16[640,3584]{1,0:T(8,128)(2,1)} collective-permute-done((bf16[640,3584]{1,0:T(8,128)(2,1)}, bf16[640,3584]{1,0:T(8,128)(2,1)}, u32[]{:S(2)}, u32[]{:S(2)}) %collective-permute-start.17) | collective-permute-done | bytes 4587552 | tf_op jit(solution)/shard_map/ppermute | solution.py:832
  180.0 39.8 %head.1 = (bf16[640,3584]{1,0:T(8,128)(2,1)}, bf16[640,3584]{1,0:T(8,128)(2,1)}, f32[16,2]{1,0:T(8,128)}, bf16[1024,640]{1,0:T(8,128)(2,1)}, f32[320,8]{1,0:T(8,128)}) custom-call(bf16[1024,640]{1,0:T(8,128)(2,1)} %get-tuple-element.171.twice_ref, bf16[640,3584]{1,0:T(8,128)(2,1)} %all-gather.5.cloned.1.call-done.near_ref, ...), custom_call_target="tpu_custom_call" | custom-call | flops 42900000768 | bytes 1048576 | tf_op jit(solution)/shard_map/head/pallas_call | solution.py:915
  220.0 26.9 %project_back.1 = (f32[1024,1152]{1,0:T(8,128)}, f32[1152,1280]{1,0:T(8,128)}, f32[1152,1280]{1,0:T(8,128)}, f32[4,16,640]{2,1,0:T(8,128)}, f32[16,48]{1,0:T(8,128)}, /*index=5*/f32[1152,96]{1,0:T(8,128)}) custom-call(bf16[1024,640]{1,0:T(8,128)(2,1)} %get-tuple-element.176.hidden_ref, f32[4,16,640]{2,1,0:T(8,128)} %get-tuple-element.168.gates_ref, ...), custom_call_target="tpu_custom_call" | custom-call | flops 28600000512 | bytes 1048576 | tf_op jit(solution)/shard_map/project_back/pallas_call | solution.py:915
  247.3 6.1 %add_convert_fusion = (bf16[160,3584]{1,0:T(8,128)(2,1)}, bf16[160,3584]{1,0:T(8,128)(2,1)}, bf16[160,3584]{1,0:T(8,128)(2,1)}, f32[160,3584]{1,0:T(8,128)S(1)}) fusion(bf16[640,3584]{1,0:T(8,128)(2,1)} %collective-permute-done.18, s32[]{:T(128)S(6)} %select_n.127, bf16[640,3584]{1,0:T(8,128)(2,1)} %get-tuple-element.195, s32[]{:T(128)S(6)} %select_n.126, ...), kind=kLoop, calls=%fused_computation.1 | loop fusion | flops 8601600 | bytes 14909456 | tf_op jit(solution)/shard_map/convert_element_type | solution.py:853
  253.4 1.4 collective-permute-start.22
  254.8 1.5 collective-permute-start.21
  256.9 38.7 %second_back.1 = (f32[1152,768]{1,0:T(8,128)}, f32[1152,768]{1,0:T(8,128)}, f32[25,1152]{1,0:T(8,128)}, bf16[1024,192]{1,0:T(8,128)(2,1)}, f32[192,8]{1,0:T(8,128)}) custom-call(f32[1024,1152]{1,0:T(8,128)} %get-tuple-element.182.grad_ref, f32[16,1152]{1,0:T(8,128)} %get-tuple-element.166.scale_ref.full_scale_ref, ...), custom_call_target="tpu_custom_call" | custom-call | flops 41799999488 | bytes 1048576 | tf_op jit(solution)/shard_map/second_back/pallas_call | solution.py:915
  295.7 10.8 %collective-permute-done.21 = bf16[160,3584]{1,0:T(8,128)(2,1)} collective-permute-done((bf16[160,3584]{1,0:T(8,128)(2,1)}, bf16[160,3584]{1,0:T(8,128)(2,1)}, u32[]{:S(2)}, u32[]{:S(2)}) %collective-permute-start.21) | collective-permute-done | bytes 1146912 | tf_op jit(solution)/shard_map/ppermute | solution.py:832
  306.5 6.1 %add_convert_fusion.3 = (bf16[288,1280]{1,0:T(8,128)(2,1)}, bf16[288,1280]{1,0:T(8,128)(2,1)}, bf16[288,1280]{1,0:T(8,128)(2,1)}, f32[288,1280]{1,0:T(8,128)S(1)}) fusion(f32[1152,1280]{1,0:T(8,128)} %collective-permute-done.19, f32[1152,1280]{1,0:T(8,128)} %get-tuple-element.200), kind=kLoop, calls=%fused_computation.12 | loop fusion | flops 2580480 | bytes 15482880 | tf_op jit(solution)/shard_map/convert_element_type | solution.py:853
  312.7 1.5 collective-permute-start.25
  314.1 1.4 collective-permute-start.24
  316.2 3.6 convert_add_fusion
  319.7 19.7 %first_back.2 = (f32[768,384]{1,0:T(8,128)}, f32[25,768]{1,0:T(8,128)}) custom-call(bf16[1024,192]{1,0:T(8,128)(2,1)} %bitcast_select_fusion.x_ref, bf16[1152,384]{1,0:T(8,128)(2,1)} %copy-done.6, bf16[1152,384]{1,0:T(8,128)(2,1)} %get-tuple-element.364.right_ref, f32[25,8,1152]{2,1,0:T(8,128)} %broadcast_in_dim.30.taps_ref, ...), custom_call_target="tpu_custom_call" | custom-call | flops 22000001024 | bytes 1048576 | tf_op jit(solution)/shard_map/first_back/pallas_call | solution.py:915
  339.5 8.6 %collective-permute-done.24 = bf16[288,1280]{1,0:T(8,128)(2,1)} collective-permute-done((bf16[288,1280]{1,0:T(8,128)(2,1)}, bf16[288,1280]{1,0:T(8,128)(2,1)}, u32[]{:S(2)}, u32[]{:S(2)}) %collective-permute-start.24) | collective-permute-done | bytes 737312 | tf_op jit(solution)/shard_map/ppermute | solution.py:832
  348.1 4.6 add_convert_fusion.6
  352.7 1.5 collective-permute-start.29
  354.2 1.4 collective-permute-start.28
  356.1 11.1 %first_back.3 = (f32[384,384]{1,0:T(8,128)}, f32[25,384]{1,0:T(8,128)}) custom-call(bf16[1024,192]{1,0:T(8,128)(2,1)} %bitcast_select_fusion.x_ref, bf16[1152,384]{1,0:T(8,128)(2,1)} %copy-done.6, bf16[1152,384]{1,0:T(8,128)(2,1)} %get-tuple-element.364.right_ref, f32[25,8,1152]{2,1,0:T(8,128)} %broadcast_in_dim.30.taps_ref, ...), custom_call_target="tpu_custom_call" | custom-call | flops 11000000512 | bytes 1048576 | tf_op jit(solution)/shard_map/first_back/pallas_call | solution.py:915
  367.3 1.4 constant_dynamic-update-slice_fusion.17
  368.7 6.7 %collective-permute-done.28 = bf16[288,768]{1,0:T(8,128)(2,1)} collective-permute-done((bf16[288,768]{1,0:T(8,128)(2,1)}, bf16[288,768]{1,0:T(8,128)(2,1)}, u32[]{:S(2)}, u32[]{:S(2)}) %collective-permute-start.28) | collective-permute-done | bytes 442400 | tf_op jit(solution)/shard_map/ppermute | solution.py:832
  378.9 1.8 fusion.2
  382.0 1.9 fusion.25
  384.0 3.4 collective-permute-start.36
  388.5 1.8 fusion.3
  390.4 1.5 collective-permute-start.33
  391.9 1.4 collective-permute-start.32
  393.4 1.4 collective-permute-start.31
  397.0 7.1 %collective-permute-done.35 = bf16[72,1280]{1,0:T(8,128)(2,1)S(1)} collective-permute-done((bf16[72,1280]{1,0:T(8,128)(2,1)S(1)}, bf16[72,1280]{1,0:T(8,128)(2,1)S(1)}, u32[]{:S(2)}, u32[]{:S(2)}) %collective-permute-start.35) | collective-permute-done | bytes 184352 | tf_op jit(solution)/shard_map/ppermute | solution.py:832
  404.3 2.4 collective-permute-start.39
  407.4 1.5 collective-permute-start.42
  408.9 1.4 collective-permute-start.41
  410.9 2.7 collective-permute-start.38
  415.0 4.2 collective-permute-start.37
  419.2 3.6 collective-permute-done.38
  422.8 2.8 collective-permute-done.37
  428.9 1.3 collective-permute-start.49
  432.4 6.5 %collective-permute-done.44 = f32[33,128]{1,0:T(8,128)S(1)} collective-permute-done((f32[33,128]{1,0:T(8,128)S(1)}, f32[33,128]{1,0:T(8,128)S(1)}, u32[]{:S(2)}, u32[]{:S(2)}) %collective-permute-start.44) | collective-permute-done | bytes 16928 | tf_op jit(solution)/shard_map/ppermute | solution.py:832
  439.8 2.9 collective-permute-done.45
  442.7 3.8 collective-permute-done.46
  447.7 3.5 collective-permute-done.47
  451.8 4.0 adamw_head.1
  460.9 9.1 %adamw.2 = (f32[288,1826]{1,0:T(8,128)}, f32[288,1826]{1,0:T(8,128)}, f32[288,1826]{1,0:T(8,128)}, f32[288,1826]{1,0:T(8,128)}, bf16[288,1826]{1,0:T(8,128)(2,1)}) custom-call(s32[2]{0:T(128)} %pad_add_fusion.place_ref, f32[1,2]{1,0:T(1,128)} %get-tuple-element.241.factor_ref, bf16[288,1152]{1,0:T(8,128)(2,1)} %copy-done.2, bf16[288,1152]{1,0:T(8,128)(2,1)} %copy-done.5, ...), custom_call_target="tpu_custom_call" | custom-call | tf_op jit(solution)/shard_map/adamw/pallas_call | solution.py:790
  471.0 12.1 %adamw.3 = (f32[288,2800]{1,0:T(8,128)}, f32[288,2800]{1,0:T(8,128)}, f32[288,2800]{1,0:T(8,128)}, f32[288,2800]{1,0:T(8,128)}, bf16[288,2800]{1,0:T(8,128)(2,1)}) custom-call(s32[2]{0:T(128)} %pad_add_fusion.place_ref, f32[1,2]{1,0:T(1,128)} %get-tuple-element.241.factor_ref, bf16[288,1152]{1,0:T(8,128)(2,1)} %copy-done.2, bf16[288,1152]{1,0:T(8,128)(2,1)} %copy-done.5, ...), custom_call_target="tpu_custom_call" | custom-call | tf_op jit(solution)/shard_map/adamw/pallas_call | solution.py:790
  (251 shorter events, 53.1 us)
Async XLA Ops:
  7.2 164.7 %copy-start = (s32[64]{0:T(128)S(1)}, s32[64]{0:T(128)}, u32[]{:S(2)}) copy-start(s32[64]{0:T(128)} %param.21) | copy-start | bytes 772
  11.4 12.1 %copy-start.8 = (f32[3560,40]{0,1:T(8,128)S(1)}, f32[3560,40]{0,1:T(8,128)}, u32[]{:S(2)}) copy-start(f32[3560,40]{0,1:T(8,128)} %param.32) | copy-start | bytes 1708804
  11.6 11.9 %copy-start.29 = (f32[512,8]{0,1:T(8,128)S(1)}, f32[512,8]{0,1:T(8,128)}, u32[]{:S(2)}) copy-start(f32[512,8]{0,1:T(8,128)} %param.36) | copy-start | bytes 49156
  11.7 12.0 %slice-start = ((f32[512,8]{0,1:T(8,128)}), f32[192,8]{0,1:T(8,128)S(1)}, s32[]{:S(2)}) async-start(f32[512,8]{0,1:T(8,128)} %param.36), calls=%async_computation.5 | async-start | bytes 16384 | tf_op jit(solution)/shard_map/slice | solution.py:1026
  11.9 15.5 %collective-permute-start.2 = (bf16[288,384]{1,0:T(8,128)(2,1)S(1)}, bf16[288,384]{1,0:T(8,128)(2,1)S(1)}, u32[]{:S(2)}, u32[]{:S(2)}) collective-permute-start(bf16[288,384]{1,0:T(8,128)(2,1)S(1)} %pad_maximum_fusion.5), channel_id=1, source_target_pairs={{0,3},{1,2},{2,1},{3,0},{4,7},{5,6},{6,5},{7,4},{8,11},{9,10},{10,... | collective-permute-start | bytes 663560 | tf_op jit(solution)/shard_map/ppermute | solution.py:832
  17.0 25.4 %collective-permute-start.1 = (bf16[288,384]{1,0:T(8,128)(2,1)S(1)}, bf16[288,384]{1,0:T(8,128)(2,1)S(1)}, u32[]{:S(2)}, u32[]{:S(2)}) collective-permute-start(bf16[288,384]{1,0:T(8,128)(2,1)S(1)} %pad_maximum_fusion.5), channel_id=1, source_target_pairs={{0,2},{1,3},{2,0},{3,1},{4,6},{5,7},{6,4},{7,5},{8,10},{9,11},{10,... | collective-permute-start | bytes 663560 | tf_op jit(solution)/shard_map/ppermute | solution.py:832
  17.0 25.4 %collective-permute-start = (bf16[288,384]{1,0:T(8,128)(2,1)S(1)}, bf16[288,384]{1,0:T(8,128)(2,1)S(1)}, u32[]{:S(2)}, u32[]{:S(2)}) collective-permute-start(bf16[288,384]{1,0:T(8,128)(2,1)S(1)} %pad_maximum_fusion.5), channel_id=1, source_target_pairs={{0,1},{1,0},{2,3},{3,2},{4,5},{5,4},{6,7},{7,6},{8,9},{9,8},{10,11... | collective-permute-start | bytes 663560 | tf_op jit(solution)/shard_map/ppermute | solution.py:832
  17.7 29.4 %all-to-all-start = ((bf16[64,16,192]{2,1,0:T(8,128)(2,1)}), bf16[64,16,192]{2,1,0:T(8,128)(2,1)S(1)}, u32[]{:S(2)}, u32[]{:S(2)}) async-start(bf16[64,16,192]{2,1,0:T(8,128)(2,1)} %param.20), calls=%async_computation | async-start | bytes 1048576 | tf_op jit(solution)/shard_map/all_to_all | solution.py:995
  22.7 94.1 %all-gather.3.cloned.1.call-start = ((), (), s32[]{:S(2)}) async-start(), calls=%async_computation.2 | async-start | bytes 1433600 | tf_op jit(solution)/shard_map/all_gather | solution.py:1038
  47.1 11.9 %collective-permute-start.5 = (bf16[72,768]{1,0:T(8,128)(2,1)S(1)}, bf16[72,768]{1,0:T(8,128)(2,1)S(1)}, u32[]{:S(2)}, u32[]{:S(2)}) collective-permute-start(bf16[72,768]{1,0:T(8,128)(2,1)S(1)} %fusion.16), channel_id=1, source_target_pairs={{0,3},{1,2},{2,1},{3,0},{4,7},{5,6},{6,5},{7,4},{8,11},{9,10},{10,... | collective-permute-start | bytes 331784 | tf_op jit(solution)/shard_map/ppermute | solution.py:832
  49.7 9.2 %collective-permute-start.4 = (bf16[72,768]{1,0:T(8,128)(2,1)S(1)}, bf16[72,768]{1,0:T(8,128)(2,1)S(1)}, u32[]{:S(2)}, u32[]{:S(2)}) collective-permute-start(bf16[72,768]{1,0:T(8,128)(2,1)S(1)} %fusion.16), channel_id=1, source_target_pairs={{0,2},{1,3},{2,0},{3,1},{4,6},{5,7},{6,4},{7,5},{8,10},{9,11},{10,... | collective-permute-start | bytes 331784 | tf_op jit(solution)/shard_map/ppermute | solution.py:832
  49.7 9.2 %collective-permute-start.3 = (bf16[72,768]{1,0:T(8,128)(2,1)S(1)}, bf16[72,768]{1,0:T(8,128)(2,1)S(1)}, u32[]{:S(2)}, u32[]{:S(2)}) collective-permute-start(bf16[72,768]{1,0:T(8,128)(2,1)S(1)} %fusion.16), channel_id=1, source_target_pairs={{0,1},{1,0},{2,3},{3,2},{4,5},{5,4},{6,7},{7,6},{8,9},{9,8},{10,11... | collective-permute-start | bytes 331784 | tf_op jit(solution)/shard_map/ppermute | solution.py:832
  51.5 11.1 %collective-permute-start.9 = (bf16[72,1280]{1,0:T(8,128)(2,1)S(1)}, bf16[72,1280]{1,0:T(8,128)(2,1)S(1)}, u32[]{:S(2)}, u32[]{:S(2)}) collective-permute-start(bf16[72,1280]{1,0:T(8,128)(2,1)S(1)} %dynamic_slice.81), channel_id=1, source_target_pairs={{0,1},{1,0},{2,3},{3,2},{4,5},{5,4},{6,7},{7,6},{8,9},{9,8},{10,11... | collective-permute-start | bytes 552968 | tf_op jit(solution)/shard_map/ppermute | solution.py:832
  51.7 12.1 %copy-start.24 = (bf16[288,384]{1,0:T(8,128)(2,1)S(1)}, bf16[288,384]{1,0:T(8,128)(2,1)}, u32[]{:S(2)}) copy-start(bf16[288,384]{1,0:T(8,128)(2,1)} %copy-done.23) | copy-start | bytes 663556
  51.7 12.1 %copy-start.26 = (bf16[288,384]{1,0:T(8,128)(2,1)S(1)}, bf16[288,384]{1,0:T(8,128)(2,1)}, u32[]{:S(2)}) copy-start(bf16[288,384]{1,0:T(8,128)(2,1)} %copy-done.25) | copy-start | bytes 663556
  59.0 20.6 %collective-permute-start.8 = (bf16[288,768]{1,0:T(8,128)(2,1)S(1)}, bf16[288,768]{1,0:T(8,128)(2,1)S(1)}, u32[]{:S(2)}, u32[]{:S(2)}) collective-permute-start(bf16[288,768]{1,0:T(8,128)(2,1)S(1)} %constant_dynamic-update-slice_fusion), channel_id=1, source_target_pairs={{0,24},{8,16},{16,8},{24,0},{1,25},{9,17},{17,9},{25,1},{2,26},{10... | collective-permute-start | bytes 1327112 | tf_op jit(solution)/shard_map/ppermute | solution.py:832
  61.5 19.1 %collective-permute-start.7 = (bf16[288,768]{1,0:T(8,128)(2,1)S(1)}, bf16[288,768]{1,0:T(8,128)(2,1)S(1)}, u32[]{:S(2)}, u32[]{:S(2)}) collective-permute-start(bf16[288,768]{1,0:T(8,128)(2,1)S(1)} %constant_dynamic-update-slice_fusion), channel_id=1, source_target_pairs={{0,16},{8,24},{16,0},{24,8},{1,17},{9,25},{17,1},{25,9},{2,18},{10... | collective-permute-start | bytes 1327112 | tf_op jit(solution)/shard_map/ppermute | solution.py:832
  62.0 19.3 %collective-permute-start.6 = (bf16[288,768]{1,0:T(8,128)(2,1)S(1)}, bf16[288,768]{1,0:T(8,128)(2,1)S(1)}, u32[]{:S(2)}, u32[]{:S(2)}) collective-permute-start(bf16[288,768]{1,0:T(8,128)(2,1)S(1)} %constant_dynamic-update-slice_fusion), channel_id=1, source_target_pairs={{0,8},{8,0},{16,24},{24,16},{1,9},{9,1},{17,25},{25,17},{2,10},{10... | collective-permute-start | bytes 1327112 | tf_op jit(solution)/shard_map/ppermute | solution.py:832
  62.5 17.0 %collective-permute-start.10 = (bf16[144,1280]{1,0:T(8,128)(2,1)S(1)}, bf16[144,1280]{1,0:T(8,128)(2,1)S(1)}, u32[]{:S(2)}, u32[]{:S(2)}) collective-permute-start(bf16[144,1280]{1,0:T(8,128)(2,1)S(1)} %constant_dynamic-update-slice_fusion.4), channel_id=1, source_target_pairs={{0,2},{1,3},{2,0},{3,1},{4,6},{5,7},{6,4},{7,5},{8,10},{9,11},{10,... | collective-permute-start | bytes 1105928 | tf_op jit(solution)/shard_map/ppermute | solution.py:832
  64.2 25.0 %collective-permute-start.11 = (bf16[1152,384]{1,0:T(8,128)(2,1)S(1)}, bf16[1152,384]{1,0:T(8,128)(2,1)}, u32[]{:S(2)}, u32[]{:S(2)}) collective-permute-start(bf16[1152,384]{1,0:T(8,128)(2,1)S(1)} %bitcast.50), channel_id=1, source_target_pairs={{0,4},{4,0},{1,5},{5,1},{2,6},{6,2},{3,7},{7,3},{8,12},{12,8},{9,1... | collective-permute-start | bytes 2654216 | tf_op jit(solution)/shard_map/ppermute | solution.py:832
  81.4 31.6 %collective-permute-start.15 = (bf16[288,1280]{1,0:T(8,128)(2,1)S(1)}, bf16[288,1280]{1,0:T(8,128)(2,1)}, u32[]{:S(2)}, u32[]{:S(2)}) collective-permute-start(bf16[288,1280]{1,0:T(8,128)(2,1)S(1)} %constant_dynamic-update-slice_fusion.10), channel_id=1, source_target_pairs={{0,24},{8,16},{16,8},{24,0},{1,25},{9,17},{17,9},{25,1},{2,26},{10... | collective-permute-start | bytes 2211848 | tf_op jit(solution)/shard_map/ppermute | solution.py:832
  83.7 33.0 %collective-permute-start.14 = (bf16[288,1280]{1,0:T(8,128)(2,1)S(1)}, bf16[288,1280]{1,0:T(8,128)(2,1)}, u32[]{:S(2)}, u32[]{:S(2)}) collective-permute-start(bf16[288,1280]{1,0:T(8,128)(2,1)S(1)} %constant_dynamic-update-slice_fusion.10), channel_id=1, source_target_pairs={{0,16},{8,24},{16,0},{24,8},{1,17},{9,25},{17,1},{25,9},{2,18},{10... | collective-permute-start | bytes 2211848 | tf_op jit(solution)/shard_map/ppermute | solution.py:832
  84.4 32.4 %collective-permute-start.13 = (bf16[288,1280]{1,0:T(8,128)(2,1)S(1)}, bf16[288,1280]{1,0:T(8,128)(2,1)}, u32[]{:S(2)}, u32[]{:S(2)}) collective-permute-start(bf16[288,1280]{1,0:T(8,128)(2,1)S(1)} %constant_dynamic-update-slice_fusion.10), channel_id=1, source_target_pairs={{0,8},{8,0},{16,24},{24,16},{1,9},{9,1},{17,25},{25,17},{2,10},{10... | collective-permute-start | bytes 2211848 | tf_op jit(solution)/shard_map/ppermute | solution.py:832
  85.0 86.9 %all-gather.5.cloned.1.call-start = ((), (), s32[]{:S(2)}) async-start(), calls=%async_computation.3 | async-start | bytes 5734400 | tf_op jit(solution)/shard_map/all_gather | solution.py:1093
  89.2 27.6 %collective-permute-start.12 = (bf16[1152,768]{1,0:T(8,128)(2,1)}, bf16[1152,768]{1,0:T(8,128)(2,1)}, u32[]{:S(2)}, u32[]{:S(2)}) collective-permute-start(bf16[1152,768]{1,0:T(8,128)(2,1)} %constant_dynamic-update-slice_fusion.6.own_ref), channel_id=1, source_target_pairs={{0,4},{4,0},{1,5},{5,1},{2,6},{6,2},{3,7},{7,3},{8,12},{12,8},{9,1... | collective-permute-start | bytes 5308424 | tf_op jit(solution)/shard_map/ppermute | solution.py:832
  116.8 271.7 %reduce-scatter.2.cloned.1.call-start = ((), (), s32[]{:S(2)}) async-start(), calls=%async_computation.4 | async-start | bytes 2867200 | tf_op jit(solution)/shard_map/reduce_scatter | solution.py:1232
  124.3 24.8 %collective-permute-start.16 = (bf16[1152,1280]{1,0:T(8,128)(2,1)}, bf16[1152,1280]{1,0:T(8,128)(2,1)}, u32[]{:S(2)}, u32[]{:S(2)}) collective-permute-start(bf16[1152,1280]{1,0:T(8,128)(2,1)} %constant_dynamic-update-slice_fusion.12.own_ref), channel_id=1, source_target_pairs={{0,4},{4,0},{1,5},{5,1},{2,6},{6,2},{3,7},{7,3},{8,12},{12,8},{9,1... | collective-permute-start | bytes 8847368 | tf_op jit(solution)/shard_map/ppermute | solution.py:832
  171.9 8.1 %collective-permute-start.17 = (bf16[640,3584]{1,0:T(8,128)(2,1)}, bf16[640,3584]{1,0:T(8,128)(2,1)}, u32[]{:S(2)}, u32[]{:S(2)}) collective-permute-start(bf16[640,3584]{1,0:T(8,128)(2,1)} %all-gather.5.cloned.1.call-done.near_ref), channel_id=1, source_target_pairs={{0,4},{4,0},{1,5},{5,1},{2,6},{6,2},{3,7},{7,3},{8,12},{12,8},{9,1... | collective-permute-start | bytes 13762568 | tf_op jit(solution)/shard_map/ppermute | solution.py:832
  219.8 27.5 %collective-permute-start.18 = (bf16[640,3584]{1,0:T(8,128)(2,1)}, bf16[640,3584]{1,0:T(8,128)(2,1)}, u32[]{:S(2)}, u32[]{:S(2)}) collective-permute-start(bf16[640,3584]{1,0:T(8,128)(2,1)} %get-tuple-element.181), channel_id=1, source_target_pairs={{0,4},{4,0},{1,5},{5,1},{2,6},{6,2},{3,7},{7,3},{8,12},{12,8},{9,1... | collective-permute-start | bytes 13762568 | tf_op jit(solution)/shard_map/ppermute | solution.py:832
  246.8 59.7 %collective-permute-start.19 = (f32[1152,1280]{1,0:T(8,128)}, f32[1152,1280]{1,0:T(8,128)}, u32[]{:S(2)}, u32[]{:S(2)}) collective-permute-start(f32[1152,1280]{1,0:T(8,128)} %get-tuple-element.194), channel_id=1, source_target_pairs={{0,4},{4,0},{1,5},{5,1},{2,6},{6,2},{3,7},{7,3},{8,12},{12,8},{9,1... | collective-permute-start | bytes 17694728 | tf_op jit(solution)/shard_map/ppermute | solution.py:832
  253.4 42.3 %collective-permute-start.22 = (bf16[160,3584]{1,0:T(8,128)(2,1)}, bf16[160,3584]{1,0:T(8,128)(2,1)S(1)}, u32[]{:S(2)}, u32[]{:S(2)}) collective-permute-start(bf16[160,3584]{1,0:T(8,128)(2,1)} %get-tuple-element.342), channel_id=1, source_target_pairs={{0,24},{8,16},{16,8},{24,0},{1,25},{9,17},{17,9},{25,1},{2,26},{10... | collective-permute-start | bytes 3440648 | tf_op jit(solution)/shard_map/ppermute | solution.py:832
  254.8 51.7 %collective-permute-start.21 = (bf16[160,3584]{1,0:T(8,128)(2,1)}, bf16[160,3584]{1,0:T(8,128)(2,1)}, u32[]{:S(2)}, u32[]{:S(2)}) collective-permute-start(bf16[160,3584]{1,0:T(8,128)(2,1)} %get-tuple-element.343), channel_id=1, source_target_pairs={{0,16},{8,24},{16,0},{24,8},{1,17},{9,25},{17,1},{25,9},{2,18},{10... | collective-permute-start | bytes 3440648 | tf_op jit(solution)/shard_map/ppermute | solution.py:832
  256.3 50.2 %collective-permute-start.20 = (bf16[160,3584]{1,0:T(8,128)(2,1)}, bf16[160,3584]{1,0:T(8,128)(2,1)}, u32[]{:S(2)}, u32[]{:S(2)}) collective-permute-start(bf16[160,3584]{1,0:T(8,128)(2,1)} %get-tuple-element.344), channel_id=1, source_target_pairs={{0,8},{8,0},{16,24},{24,16},{1,9},{9,1},{17,25},{25,17},{2,10},{10... | collective-permute-start | bytes 3440648 | tf_op jit(solution)/shard_map/ppermute | solution.py:832
  295.6 52.5 %collective-permute-start.26 = (f32[1152,768]{1,0:T(8,128)}, f32[1152,768]{1,0:T(8,128)}, u32[]{:S(2)}, u32[]{:S(2)}) collective-permute-start(f32[1152,768]{1,0:T(8,128)} %get-tuple-element.202), channel_id=1, source_target_pairs={{0,4},{4,0},{1,5},{5,1},{2,6},{6,2},{3,7},{7,3},{8,12},{12,8},{9,1... | collective-permute-start | bytes 10616840 | tf_op jit(solution)/shard_map/ppermute | solution.py:832
  312.7 26.8 %collective-permute-start.25 = (bf16[288,1280]{1,0:T(8,128)(2,1)}, bf16[288,1280]{1,0:T(8,128)(2,1)}, u32[]{:S(2)}, u32[]{:S(2)}) collective-permute-start(bf16[288,1280]{1,0:T(8,128)(2,1)} %get-tuple-element.338), channel_id=1, source_target_pairs={{0,24},{8,16},{16,8},{24,0},{1,25},{9,17},{17,9},{25,1},{2,26},{10... | collective-permute-start | bytes 2211848 | tf_op jit(solution)/shard_map/ppermute | solution.py:832
  314.1 33.9 %collective-permute-start.24 = (bf16[288,1280]{1,0:T(8,128)(2,1)}, bf16[288,1280]{1,0:T(8,128)(2,1)}, u32[]{:S(2)}, u32[]{:S(2)}) collective-permute-start(bf16[288,1280]{1,0:T(8,128)(2,1)} %get-tuple-element.339), channel_id=1, source_target_pairs={{0,16},{8,24},{16,0},{24,8},{1,17},{9,25},{17,1},{25,9},{2,18},{10... | collective-permute-start | bytes 2211848 | tf_op jit(solution)/shard_map/ppermute | solution.py:832
  315.6 32.5 %collective-permute-start.23 = (bf16[288,1280]{1,0:T(8,128)(2,1)}, bf16[288,1280]{1,0:T(8,128)(2,1)}, u32[]{:S(2)}, u32[]{:S(2)}) collective-permute-start(bf16[288,1280]{1,0:T(8,128)(2,1)} %get-tuple-element.340), channel_id=1, source_target_pairs={{0,8},{8,0},{16,24},{24,16},{1,9},{9,1},{17,25},{25,17},{2,10},{10... | collective-permute-start | bytes 2211848 | tf_op jit(solution)/shard_map/ppermute | solution.py:832
  352.7 16.0 %collective-permute-start.29 = (bf16[288,768]{1,0:T(8,128)(2,1)}, bf16[288,768]{1,0:T(8,128)(2,1)S(1)}, u32[]{:S(2)}, u32[]{:S(2)}) collective-permute-start(bf16[288,768]{1,0:T(8,128)(2,1)} %get-tuple-element.346), channel_id=1, source_target_pairs={{0,24},{8,16},{16,8},{24,0},{1,25},{9,17},{17,9},{25,1},{2,26},{10... | collective-permute-start | bytes 1327112 | tf_op jit(solution)/shard_map/ppermute | solution.py:832
  354.2 21.3 %collective-permute-start.28 = (bf16[288,768]{1,0:T(8,128)(2,1)}, bf16[288,768]{1,0:T(8,128)(2,1)}, u32[]{:S(2)}, u32[]{:S(2)}) collective-permute-start(bf16[288,768]{1,0:T(8,128)(2,1)} %get-tuple-element.347), channel_id=1, source_target_pairs={{0,16},{8,24},{16,0},{24,8},{1,17},{9,25},{17,1},{25,9},{2,18},{10... | collective-permute-start | bytes 1327112 | tf_op jit(solution)/shard_map/ppermute | solution.py:832
  355.6 19.9 %collective-permute-start.27 = (bf16[288,768]{1,0:T(8,128)(2,1)}, bf16[288,768]{1,0:T(8,128)(2,1)}, u32[]{:S(2)}, u32[]{:S(2)}) collective-permute-start(bf16[288,768]{1,0:T(8,128)(2,1)} %get-tuple-element.348), channel_id=1, source_target_pairs={{0,8},{8,0},{16,24},{24,16},{1,9},{9,1},{17,25},{25,17},{2,10},{10... | collective-permute-start | bytes 1327112 | tf_op jit(solution)/shard_map/ppermute | solution.py:832
  380.7 7.8 %collective-permute-start.30 = (f32[1152,384]{1,0:T(8,128)}, f32[1152,384]{1,0:T(8,128)}, u32[]{:S(2)}, u32[]{:S(2)}) collective-permute-start(f32[1152,384]{1,0:T(8,128)} %get-tuple-element.355), channel_id=1, source_target_pairs={{0,4},{4,0},{1,5},{5,1},{2,6},{6,2},{3,7},{7,3},{8,12},{12,8},{9,1... | collective-permute-start | bytes 5308424 | tf_op jit(solution)/shard_map/ppermute | solution.py:832
  384.0 9.4 %collective-permute-start.36 = (bf16[72,1280]{1,0:T(8,128)(2,1)S(1)}, bf16[72,1280]{1,0:T(8,128)(2,1)S(1)}, u32[]{:S(2)}, u32[]{:S(2)}) collective-permute-start(bf16[72,1280]{1,0:T(8,128)(2,1)S(1)} %get-tuple-element.372), channel_id=1, source_target_pairs={{0,3},{1,2},{2,1},{3,0},{4,7},{5,6},{6,5},{7,4},{8,11},{9,10},{10,... | collective-permute-start | bytes 552968 | tf_op jit(solution)/shard_map/ppermute | solution.py:832
  387.4 16.6 %collective-permute-start.35 = (bf16[72,1280]{1,0:T(8,128)(2,1)S(1)}, bf16[72,1280]{1,0:T(8,128)(2,1)S(1)}, u32[]{:S(2)}, u32[]{:S(2)}) collective-permute-start(bf16[72,1280]{1,0:T(8,128)(2,1)S(1)} %get-tuple-element.373), channel_id=1, source_target_pairs={{0,2},{1,3},{2,0},{3,1},{4,6},{5,7},{6,4},{7,5},{8,10},{9,11},{10,... | collective-permute-start | bytes 552968 | tf_op jit(solution)/shard_map/ppermute | solution.py:832
  387.4 16.6 %collective-permute-start.34 = (bf16[72,1280]{1,0:T(8,128)(2,1)S(1)}, bf16[72,1280]{1,0:T(8,128)(2,1)S(1)}, u32[]{:S(2)}, u32[]{:S(2)}) collective-permute-start(bf16[72,1280]{1,0:T(8,128)(2,1)S(1)} %get-tuple-element.374), channel_id=1, source_target_pairs={{0,1},{1,0},{2,3},{3,2},{4,5},{5,4},{6,7},{7,6},{8,9},{9,8},{10,11... | collective-permute-start | bytes 552968 | tf_op jit(solution)/shard_map/ppermute | solution.py:832
  390.4 13.7 %collective-permute-start.33 = (bf16[288,384]{1,0:T(8,128)(2,1)S(1)}, bf16[288,384]{1,0:T(8,128)(2,1)S(1)}, u32[]{:S(2)}, u32[]{:S(2)}) collective-permute-start(bf16[288,384]{1,0:T(8,128)(2,1)S(1)} %get-tuple-element.350), channel_id=1, source_target_pairs={{0,24},{8,16},{16,8},{24,0},{1,25},{9,17},{17,9},{25,1},{2,26},{10... | collective-permute-start | bytes 663560 | tf_op jit(solution)/shard_map/ppermute | solution.py:832
  391.9 12.1 %collective-permute-start.32 = (bf16[288,384]{1,0:T(8,128)(2,1)S(1)}, bf16[288,384]{1,0:T(8,128)(2,1)S(1)}, u32[]{:S(2)}, u32[]{:S(2)}) collective-permute-start(bf16[288,384]{1,0:T(8,128)(2,1)S(1)} %get-tuple-element.351), channel_id=1, source_target_pairs={{0,16},{8,24},{16,0},{24,8},{1,17},{9,25},{17,1},{25,9},{2,18},{10... | collective-permute-start | bytes 663560 | tf_op jit(solution)/shard_map/ppermute | solution.py:832
  393.4 10.6 %collective-permute-start.31 = (bf16[288,384]{1,0:T(8,128)(2,1)S(1)}, bf16[288,384]{1,0:T(8,128)(2,1)S(1)}, u32[]{:S(2)}, u32[]{:S(2)}) collective-permute-start(bf16[288,384]{1,0:T(8,128)(2,1)S(1)} %get-tuple-element.352), channel_id=1, source_target_pairs={{0,8},{8,0},{16,24},{24,16},{1,9},{9,1},{17,25},{25,17},{2,10},{10... | collective-permute-start | bytes 663560 | tf_op jit(solution)/shard_map/ppermute | solution.py:832
  404.3 10.7 %collective-permute-start.39 = (bf16[72,1152]{1,0:T(8,128)(2,1)S(1)}, bf16[72,1152]{1,0:T(8,128)(2,1)S(1)}, u32[]{:S(2)}, u32[]{:S(2)}) collective-permute-start(bf16[72,1152]{1,0:T(8,128)(2,1)S(1)} %get-tuple-element.375), channel_id=1, source_target_pairs={{0,3},{1,2},{2,1},{3,0},{4,7},{5,6},{6,5},{7,4},{8,11},{9,10},{10,... | collective-permute-start | bytes 497672 | tf_op jit(solution)/shard_map/ppermute | solution.py:832
  407.4 18.2 %collective-permute-start.42 = (bf16[72,1280]{1,0:T(8,128)(2,1)S(1)}, bf16[72,1280]{1,0:T(8,128)(2,1)S(1)}, u32[]{:S(2)}, u32[]{:S(2)}) collective-permute-start(bf16[72,1280]{1,0:T(8,128)(2,1)S(1)} %get-tuple-element.247), channel_id=1, source_target_pairs={{0,24},{8,16},{16,8},{24,0},{1,25},{9,17},{17,9},{25,1},{2,26},{10... | collective-permute-start | bytes 552968 | tf_op jit(solution)/shard_map/ppermute | solution.py:832
  408.9 16.7 %collective-permute-start.41 = (bf16[72,1280]{1,0:T(8,128)(2,1)S(1)}, bf16[72,1280]{1,0:T(8,128)(2,1)S(1)}, u32[]{:S(2)}, u32[]{:S(2)}) collective-permute-start(bf16[72,1280]{1,0:T(8,128)(2,1)S(1)} %get-tuple-element.247), channel_id=1, source_target_pairs={{0,16},{8,24},{16,0},{24,8},{1,17},{9,25},{17,1},{25,9},{2,18},{10... | collective-permute-start | bytes 552968 | tf_op jit(solution)/shard_map/ppermute | solution.py:832
  410.3 15.3 %collective-permute-start.40 = (bf16[72,1280]{1,0:T(8,128)(2,1)S(1)}, bf16[72,1280]{1,0:T(8,128)(2,1)S(1)}, u32[]{:S(2)}, u32[]{:S(2)}) collective-permute-start(bf16[72,1280]{1,0:T(8,128)(2,1)S(1)} %get-tuple-element.247), channel_id=1, source_target_pairs={{0,8},{8,0},{16,24},{24,16},{1,9},{9,1},{17,25},{25,17},{2,10},{10... | collective-permute-start | bytes 552968 | tf_op jit(solution)/shard_map/ppermute | solution.py:832
  410.9 11.8 %collective-permute-start.38 = (bf16[72,1152]{1,0:T(8,128)(2,1)S(1)}, bf16[72,1152]{1,0:T(8,128)(2,1)S(1)}, u32[]{:S(2)}, u32[]{:S(2)}) collective-permute-start(bf16[72,1152]{1,0:T(8,128)(2,1)S(1)} %get-tuple-element.376), channel_id=1, source_target_pairs={{0,2},{1,3},{2,0},{3,1},{4,6},{5,7},{6,4},{7,5},{8,10},{9,11},{10,... | collective-permute-start | bytes 497672 | tf_op jit(solution)/shard_map/ppermute | solution.py:832
  415.0 10.6 %collective-permute-start.37 = (bf16[72,1152]{1,0:T(8,128)(2,1)S(1)}, bf16[72,1152]{1,0:T(8,128)(2,1)S(1)}, u32[]{:S(2)}, u32[]{:S(2)}) collective-permute-start(bf16[72,1152]{1,0:T(8,128)(2,1)S(1)} %get-tuple-element.377), channel_id=1, source_target_pairs={{0,1},{1,0},{2,3},{3,2},{4,5},{5,4},{6,7},{7,6},{8,9},{9,8},{10,11... | collective-permute-start | bytes 497672 | tf_op jit(solution)/shard_map/ppermute | solution.py:832
  427.0 4.1 collective-permute-start.43
  427.6 29.5 %collective-permute-start.50 = (bf16[72,1152]{1,0:T(8,128)(2,1)S(1)}, bf16[72,1152]{1,0:T(8,128)(2,1)S(1)}, u32[]{:S(2)}, u32[]{:S(2)}) collective-permute-start(bf16[72,1152]{1,0:T(8,128)(2,1)S(1)} %get-tuple-element.370), channel_id=1, source_target_pairs={{0,24},{8,16},{16,8},{24,0},{1,25},{9,17},{17,9},{25,1},{2,26},{10... | collective-permute-start | bytes 497672 | tf_op jit(solution)/shard_map/ppermute | solution.py:832
  428.9 28.2 %collective-permute-start.49 = (bf16[72,1152]{1,0:T(8,128)(2,1)S(1)}, bf16[72,1152]{1,0:T(8,128)(2,1)S(1)}, u32[]{:S(2)}, u32[]{:S(2)}) collective-permute-start(bf16[72,1152]{1,0:T(8,128)(2,1)S(1)} %get-tuple-element.370), channel_id=1, source_target_pairs={{0,16},{8,24},{16,0},{24,8},{1,17},{9,25},{17,1},{25,9},{2,18},{10... | collective-permute-start | bytes 497672 | tf_op jit(solution)/shard_map/ppermute | solution.py:832
  430.3 26.9 %collective-permute-start.48 = (bf16[72,1152]{1,0:T(8,128)(2,1)S(1)}, bf16[72,1152]{1,0:T(8,128)(2,1)S(1)}, u32[]{:S(2)}, u32[]{:S(2)}) collective-permute-start(bf16[72,1152]{1,0:T(8,128)(2,1)S(1)} %get-tuple-element.370), channel_id=1, source_target_pairs={{0,8},{8,0},{16,24},{24,16},{1,9},{9,1},{17,25},{25,17},{2,10},{10... | collective-permute-start | bytes 497672 | tf_op jit(solution)/shard_map/ppermute | solution.py:832
  431.1 7.8 %collective-permute-start.44 = (f32[33,128]{1,0:T(8,128)S(1)}, f32[33,128]{1,0:T(8,128)S(1)}, u32[]{:S(2)}, u32[]{:S(2)}) collective-permute-start(f32[33,128]{1,0:T(8,128)S(1)} %fusion.22), channel_id=1, source_target_pairs={{0,8},{8,0},{16,24},{24,16},{1,9},{9,1},{17,25},{25,17},{2,10},{10... | collective-permute-start | bytes 50696 | tf_op jit(solution)/shard_map/ppermute | solution.py:832
  438.9 3.8 collective-permute-start.45
  442.7 3.8 collective-permute-start.46
  446.5 4.7 collective-permute-start.47
  447.6 22.5 %collective-permute-start.52 = (bf16[288,1280]{1,0:T(8,128)(2,1)S(1)}, bf16[288,1280]{1,0:T(8,128)(2,1)S(1)}, u32[]{:S(2)}, u32[]{:S(2)}) collective-permute-start(bf16[288,1280]{1,0:T(8,128)(2,1)S(1)} %constant_dynamic-update-slice_fusion.18.refs_2_), channel_id=1, source_target_pairs={{0,4},{4,0},{1,5},{5,1},{2,6},{6,2},{3,7},{7,3},{8,12},{12,8},{9,1... | collective-permute-start | bytes 2211848 | tf_op jit(solution)/shard_map/ppermute | solution.py:832
  457.2 2.9 collective-permute-start.51
  471.0 12.1 %copy-start.1 = (s32[64]{0:T(128)S(1)}, s32[64]{0:T(128)}, u32[]{:S(2)}) copy-start(s32[64]{0:T(128)} %param.21) | copy-start | bytes 772
  (35 other events, 193.8 us)
Sparse Core Ops, SparseCore 0:
  85.1 28.7 all-gather.2
  116.9 54.9 all-gather.4
  319.9 46.9 reduce-scatter.1

commit v4 on v3

--- a/solution.py
+++ b/solution.py
@@ -872,14 +872,6 @@
             values = values + swap(values, axis, distance)
             distance *= 2
     return values
-
-
-def own_order(values, rows):
-    place = lax.axis_index("xy")
-    return [
-        lax.dynamic_slice_in_dim(values, (place ^ k) * rows, rows, 0)
-        for k in range(lax.axis_size("xy"))
-    ]
 
 
 def in_order(parts):
@@ -981,10 +973,13 @@
         + two_parts(row[:, C0 : C0 + SE]),
         1,
     )
-    small = joined(own_order(jnp.where(first_core, small_left, small_right), height))
+    small = lax.dynamic_slice_in_dim(
+        jnp.where(first_core, small_left, small_right), place * height, height, 0
+    )
     expand_own = lax.dynamic_slice(
         column, (place * height, begin + core * HALF * C0), (height, HALF * C0)
     ).astype(BF16)
+    first_own = jnp.concatenate([expand_own, small], 1)
     project_own = lax.dynamic_slice(
         row, (place * height, C0 + SE + core * HALF * C2), (height, HALF * C2)
     ).astype(BF16)
@@ -993,24 +988,25 @@
     lanes = blocks * part
     head_own = jnp.pad(head_master.T.astype(BF16), ((0, 0), (0, lanes - NE * C2 - CLASSES)))
     mine = lax.all_to_all(images, "chan", 0, 0, tiled=True)
-    small, expand_own, project_own, mine = meet(
-        copies(small, "chan"), expand_own, project_own, mine
-    )
-    small = joined(small).reshape(chans, places, height, 2 * C0)
-    small = small.transpose(1, 0, 2, 3).reshape(wide, 2 * C0)
-    small_far = swap(small, "core", 1)
-    expand_own = copies(expand_own, "chan")
-    project_own = joined([project_own, swap(project_own, "chan", 1)])
-    expand_own = joined(expand_own)
-    left = jnp.where(first_core, small, small_far)
-    right = jnp.where(first_core, small_far, small)
-    expand_own = copies(expand_own, "xy")
+    first_own, project_own, head_own = meet(
+        copies(first_own, "chan"), [project_own, swap(project_own, "chan", 1)], head_own
+    )
+    first_own = copies(joined(first_own), "xy")
+    head_own = lax.all_gather(head_own, "chan", axis=0, tiled=True)
     distance = 2
-    project_own = [project_own]
     while distance < chans:
         held = joined(project_own)
         project_own = [held, swap(held, "chan", distance)]
         distance *= 2
+    mine = mine.reshape(chans, batch, slots // chans, C0).transpose(0, 2, 1, 3)
+    mine, first_own, project_own, head_own = meet(mine, first_own, project_own, head_own)
+    head_own = lax.all_gather(head_own, "xy", axis=0, tiled=True)
+    first_own, project_own = joined(first_own), joined(project_own)
+    first_far = swap(first_own, "core", 1)
+    project_own = copies(project_own, "xy")
+    small, small_far = first_own[:, HALF * C0 :], first_far[:, HALF * C0 :]
+    left = jnp.where(first_core, small, small_far)
+    right = jnp.where(first_core, small_far, small)
 
     def both(values, at, width):
         upper = values[:, at : at + width].astype(F32)
@@ -1026,23 +1022,20 @@
     route_in, route_out = route_master[:C0], route_master[C0:]
     route_in = jnp.where(first_core, route_in, jnp.roll(route_in, HALF, axis=1))
 
-    mine = mine.reshape(chans, batch, slots // chans, C0).transpose(0, 2, 1, 3)
     label = lax.dynamic_slice_in_dim(labels, layer * batch, batch, 0)
     side = lax.dynamic_slice_in_dim(resolution, layer * batch, batch, 0)
     spots = jnp.arange(slots, dtype=jnp.int32)
     inside = ((spots // MAP)[:, None] < side[None, :]) & ((spots % MAP)[:, None] < side[None, :])
     inside = inside.reshape(rows, 1)
     x = jnp.where(inside, mine.reshape(rows, C0), 0)
-    x, expand_own, project_own, head_own = meet(x, expand_own, project_own, head_own)
-    expand_own, project_own = joined(expand_own), joined(project_own)
-    head_own = lax.all_gather(head_own, "chan", axis=0, tiled=True)
-    expand_far = swap(expand_own, "core", 1)
-    project_own = copies(project_own, "xy")
     mask = jnp.broadcast_to(inside.astype(F32), (rows, LANES))
     count = jnp.broadcast_to((side * side).astype(F32)[:, None], (batch, LANES))
 
     def tiled(array):
         return (array, (tile, array.shape[1]), lambda i: (i, 0))
+
+    def experts(array):
+        return (array, (tile, HALF * C0), lambda i: (i, 0))
 
     def across(array):
         return (array, (array.shape[0], tile), lambda i: (0, i))
@@ -1085,18 +1078,12 @@
     )
 
     (conv_one, mixed_in, twice_one, mean_one, gate_one, gates_one, gates_mid) = first_out
-    mixed_in, expand_far, project_own, head_own = meet(
-        mixed_in, expand_far, project_own, head_own
-    )
-    project_own = joined(project_own)
-    project_far = swap(project_own, "core", 1)
-    head_own = lax.all_gather(head_own, "xy", axis=0, tiled=True)
 
     mixed_two, conv_two, mean_two, units, scale = call(
         second_forward,
         (tiles,),
         [
-            whole(mixed_in), tiled(expand_own), tiled(expand_far), tap_tile(second_taps),
+            whole(mixed_in), experts(first_own), experts(first_far), tap_tile(second_taps),
             whole(mask), whole(count), tiled(excite_in), whole(excite_out),
         ],
         [
@@ -1111,7 +1098,9 @@
         21,
     )
 
-    conv_two, project_far = meet(conv_two, project_far)
+    conv_two, project_own = meet(conv_two, project_own)
+    project_own = joined(project_own)
+    project_far = swap(project_own, "core", 1)
 
     line = rows // 4
 
@@ -1210,7 +1199,7 @@
         [
             across(deep_grad), across(scale), whole(unit_grad), tiled(excite_in), whole(count),
             whole(mask), across(conv_two), across(mixed_two), tap_tile(second_taps),
-            whole(mixed_in), tiled(expand_own), tiled(expand_far), whole(twice_one),
+            whole(mixed_in), experts(first_own), experts(first_far), whole(twice_one),
             whole(gates_one), whole(gate_one), whole(gate_sums), whole(route_in), whole(mean_one),
         ],
         [

time: 496 us -> 491 us (0.990)
  waiting for transfers between devices: 117 us -> 109 us
    all_gather x1, waiting for transfers between devices: 7.09 us -> 1.19 us  [on_device(): head_own = lax.all_gather(head_own, 'xy', axis=0, tiled=True)]
    ppermute x53 -> x49, waiting for transfers between devices: 105 us -> 106 us  [swap(): return lax.ppermute(values, axis, [(i, i ^ distance) for i in range(size)])]
    unnamed x98 -> x78, local copies, waits for them, and re-layouts: 14.7 us -> 13.9 us
    ppermute x53 -> x49, starting transfers between devices: 58.6 us -> 58.7 us  [swap(): return lax.ppermute(values, axis, [(i, i ^ distance) for i in range(size)])]
  transfers between devices with their start and end apart: 57 -> 53, of which waited for: 20 -> 18; matrix products, arithmetic and copies ran while one was open for 14% -> 12% of each run, Pallas kernels for 34% -> 34%
where the time goes in v4:
time: 491 us; the launch traced here: 482 us
  Pallas kernels  216 us (44%)
  waiting for transfers between devices  109 us (22%)
  starting transfers between devices  63.9 us (13%)
  other arithmetic  42.4 us (9%)
  local copies, waits for them, and re-layouts  33.6 us (7%)
  between operations  16.9 us (3%)
    pallas_call x8, Pallas kernels, call(): pl.pallas_call(kernel, grid=grid, in_specs=in_specs, out_specs=[spec(shap...  191 us
    ppermute x49, waiting for transfers between devices, swap(): return lax.ppermute(values, axis, [(i, i ^ distance) for i in range(size)])  106 us
    ppermute x49, starting transfers between devices, swap(): return lax.ppermute(values, axis, [(i, i ^ distance) for i in range(size)])  58.7 us
    pallas_call x2, Pallas kernels, adamw(): pl.pallas_call(functools.partial(adamw_kernel, segments, len(pieces) // 2...  21.2 us
    convert_element_type x4, other arithmetic, exchange(): block.astype(BF16)  18.6 us
    unnamed x78, local copies, waits for them, and re-layouts  13.9 us
  transfers between devices with their start and end apart: 53, of which 18 were waited for; matrix products, arithmetic and copies ran while one was open for 12% of the time, Pallas kernels for 34%

profile of v4, /device:TPU:0, one launch (start us, length us, event | category | flops | bytes accessed | tf_op | source)
XLA Modules:
  0.0 482.3 jit_solution(479507652733113808)
XLA Ops:
  13.8 3.1 collective-permute-start
  16.9 2.6 collective-permute-start.1
  19.5 5.1 %all-to-all-start = ((bf16[64,16,192]{2,1,0:T(8,128)(2,1)}), bf16[64,16,192]{2,1,0:T(8,128)(2,1)S(1)}, u32[]{:S(2)}, u32[]{:S(2)}) async-start(bf16[64,16,192]{2,1,0:T(8,128)(2,1)} %param.20), calls=%async_computation | async-start | bytes 1048576 | tf_op jit(solution)/shard_map/all_to_all | solution.py:990
  25.7 2.1 collective-permute-start.3
  28.6 6.4 %collective-permute-done.1 = bf16[72,1152]{1,0:T(8,128)(2,1)S(1)} collective-permute-done((bf16[72,1152]{1,0:T(8,128)(2,1)S(1)}, bf16[72,1152]{1,0:T(8,128)(2,1)S(1)}, u32[]{:S(2)}, u32[]{:S(2)}) %collective-permute-start.1) | collective-permute-done | bytes 165920 | tf_op jit(solution)/shard_map/ppermute | solution.py:832
  34.9 5.0 %collective-permute-done.3 = bf16[72,1280]{1,0:T(8,128)(2,1)S(1)} collective-permute-done((bf16[72,1280]{1,0:T(8,128)(2,1)S(1)}, bf16[72,1280]{1,0:T(8,128)(2,1)S(1)}, u32[]{:S(2)}, u32[]{:S(2)}) %collective-permute-start.3) | collective-permute-done | bytes 184352 | tf_op jit(solution)/shard_map/ppermute | solution.py:832
  40.2 1.6 collective-permute-start.4
  41.7 1.5 collective-permute-start.5
  43.7 3.6 collective-permute-start.7
  47.5 31.8 %collective-permute-done.7 = bf16[144,1280]{1,0:T(8,128)(2,1)S(1)} collective-permute-done((bf16[144,1280]{1,0:T(8,128)(2,1)S(1)}, bf16[144,1280]{1,0:T(8,128)(2,1)S(1)}, u32[]{:S(2)}, u32[]{:S(2)}) %collective-permute-start.7) | collective-permute-done | bytes 368672 | tf_op jit(solution)/shard_map/ppermute | solution.py:832
  79.2 1.7 all-gather.3.cloned.1.call-done
  82.7 2.0 constant_dynamic-update-slice_fusion.7
  84.7 2.0 constant_dynamic-update-slice_fusion.6.own_ref
  89.5 1.5 collective-permute-start.9
  91.0 1.5 collective-permute-start.10
  94.0 1.6 broadcast_select_fusion
  97.0 1.4 convert_add_fusion.4
  101.1 18.1 %first_forward.1 = (f32[1024,1152]{1,0:T(8,128)}, bf16[1024,1536]{1,0:T(8,128)(2,1)}, bf16[1024,384]{1,0:T(8,128)(2,1)}, f32[16,192]{1,0:T(8,128)}, f32[16,8]{1,...) custom-call(bf16[1024,192]{1,0:T(8,128)(2,1)} %bitcast_select_fusion.x_ref, bf16[1152,384]{1,0:T(8,128)(2,1)} %copy-done.6, ...), custom_call_target="tpu_custom_call" | custom-call | flops 18699999232 | bytes 1048576 | tf_op jit(solution)/shard_map/first_forward/pallas_call | solution.py:907
  120.2 21.3 %second_forward.1 = (f32[1024,1152]{1,0:T(8,128)}, f32[1024,1152]{1,0:T(8,128)}, f32[16,1152]{1,0:T(8,128)}, f32[16,48]{1,0:T(8,128)}, f32[16,1152]{1,0:T(8,128)}) custom-call(bf16[1024,1536]{1,0:T(8,128)(2,1)} %get-tuple-element.150.wide_ref, bf16[1152,1152]{1,0:T(8,128)(2,1)} %constant_dynamic-update-slice_fusion.6.own_ref, ...), custom_call_target="tpu_custom_call" | custom-call | flops 23100000256 | bytes 1048576 | tf_op jit(solution)/shard_map/second_forward/pallas_call | solution.py:907
  147.7 4.3 collective-permute-done.12.far_ref
  152.0 15.7 %project.1 = (bf16[1024,2560]{1,0:T(8,128)(2,1)}, bf16[1024,640]{1,0:T(8,128)(2,1)}, f32[16,320]{1,0:T(8,128)}, f32[16,8]{1,0:T(8,128)}, f32[4,16,640]{2,1,0:T(8,128)}) custom-call(f32[1024,1152]{1,0:T(8,128)} %get-tuple-element.154.conv_ref, f32[16,1152]{1,0:T(8,128)} %get-tuple-element.155.scale_ref.full_scale_ref, bf16[1152,1280]{1,0:T(8,128)(2,1)} %copy-done.18, ...), custom_call_target="tpu_custom_call" | custom-call | flops 17600000000 | bytes 1048576 | tf_op jit(solution)/shard_map/project/pallas_call | solution.py:907
  169.6 7.3 %collective-permute-done.13.distant_ref = bf16[640,3584]{1,0:T(8,128)(2,1)} collective-permute-done((bf16[640,3584]{1,0:T(8,128)(2,1)}, bf16[640,3584]{1,0:T(8,128)(2,1)}, u32[]{:S(2)}, u32[]{:S(2)}) %collective-permute-start.13) | collective-permute-done | bytes 4587552 | tf_op jit(solution)/shard_map/ppermute | solution.py:832
  176.9 39.7 %head.1 = (bf16[640,3584]{1,0:T(8,128)(2,1)}, bf16[640,3584]{1,0:T(8,128)(2,1)}, f32[16,2]{1,0:T(8,128)}, bf16[1024,640]{1,0:T(8,128)(2,1)}, f32[320,8]{1,0:T(8,128)}) custom-call(bf16[1024,640]{1,0:T(8,128)(2,1)} %get-tuple-element.163.twice_ref, bf16[640,3584]{1,0:T(8,128)(2,1)} %all-gather.5.cloned.1.call-done.near_ref, ...), custom_call_target="tpu_custom_call" | custom-call | flops 42900000768 | bytes 1048576 | tf_op jit(solution)/shard_map/head/pallas_call | solution.py:907
  216.9 26.9 %project_back.1 = (f32[1024,1152]{1,0:T(8,128)}, f32[1152,1280]{1,0:T(8,128)}, f32[1152,1280]{1,0:T(8,128)}, f32[4,16,640]{2,1,0:T(8,128)}, f32[16,48]{1,0:T(8,128)}, /*index=5*/f32[1152,96]{1,0:T(8,128)}) custom-call(bf16[1024,640]{1,0:T(8,128)(2,1)} %get-tuple-element.168.hidden_ref, f32[4,16,640]{2,1,0:T(8,128)} %get-tuple-element.160.gates_ref, ...), custom_call_target="tpu_custom_call" | custom-call | flops 28600000512 | bytes 1048576 | tf_op jit(solution)/shard_map/project_back/pallas_call | solution.py:907
  244.2 6.1 %add_convert_fusion = (bf16[160,3584]{1,0:T(8,128)(2,1)}, bf16[160,3584]{1,0:T(8,128)(2,1)}, bf16[160,3584]{1,0:T(8,128)(2,1)}, f32[160,3584]{1,0:T(8,128)S(1)}) fusion(bf16[640,3584]{1,0:T(8,128)(2,1)} %collective-permute-done.14, s32[]{:T(128)S(6)} %select_n.115, bf16[640,3584]{1,0:T(8,128)(2,1)} %get-tuple-element.187, s32[]{:T(128)S(6)} %select_n.114, ...), kind=kLoop, calls=%fused_computation.1 | loop fusion | flops 8601600 | bytes 14909456 | tf_op jit(solution)/shard_map/convert_element_type | solution.py:853
  250.3 1.4 collective-permute-start.16
  252.3 1.5 collective-permute-start.18
  253.8 38.7 %second_back.1 = (f32[1152,768]{1,0:T(8,128)}, f32[1152,768]{1,0:T(8,128)}, f32[25,1152]{1,0:T(8,128)}, bf16[1024,192]{1,0:T(8,128)(2,1)}, f32[192,8]{1,0:T(8,128)}) custom-call(f32[1024,1152]{1,0:T(8,128)} %get-tuple-element.174.grad_ref, f32[16,1152]{1,0:T(8,128)} %get-tuple-element.155.scale_ref.full_scale_ref, ...), custom_call_target="tpu_custom_call" | custom-call | flops 41799999488 | bytes 1048576 | tf_op jit(solution)/shard_map/second_back/pallas_call | solution.py:907
  292.6 11.1 %collective-permute-done.17 = bf16[160,3584]{1,0:T(8,128)(2,1)} collective-permute-done((bf16[160,3584]{1,0:T(8,128)(2,1)}, bf16[160,3584]{1,0:T(8,128)(2,1)}, u32[]{:S(2)}, u32[]{:S(2)}) %collective-permute-start.17) | collective-permute-done | bytes 1146912 | tf_op jit(solution)/shard_map/ppermute | solution.py:832
  303.7 6.1 %add_convert_fusion.3 = (bf16[288,1280]{1,0:T(8,128)(2,1)}, bf16[288,1280]{1,0:T(8,128)(2,1)}, bf16[288,1280]{1,0:T(8,128)(2,1)}, f32[288,1280]{1,0:T(8,128)S(1)}) fusion(f32[1152,1280]{1,0:T(8,128)} %collective-permute-done.15, f32[1152,1280]{1,0:T(8,128)} %get-tuple-element.192), kind=kLoop, calls=%fused_computation.12 | loop fusion | flops 2580480 | bytes 15482880 | tf_op jit(solution)/shard_map/convert_element_type | solution.py:853
  310.4 1.5 collective-permute-start.20
  311.9 1.5 collective-permute-start.21
  313.3 3.6 convert_add_fusion
  316.9 19.7 %first_back.2 = (f32[768,384]{1,0:T(8,128)}, f32[25,768]{1,0:T(8,128)}) custom-call(bf16[1024,192]{1,0:T(8,128)(2,1)} %bitcast_select_fusion.x_ref, bf16[1152,384]{1,0:T(8,128)(2,1)} %copy-done.6, bf16[1152,384]{1,0:T(8,128)(2,1)} %copy-done.3, f32[25,8,1152]{2,1,0:T(8,128)} %broadcast_in_dim.30.taps_ref, f32[1024,128]{1,0:T(8,128)} %broadcast_in_dim.54.mask_ref, ...), custom_call_target="tpu_custom_call" | custom-call | flops 22000001024 | bytes 1048576 | tf_op jit(solution)/shard_map/first_back/pallas_call | solution.py:907
  336.7 7.0 %collective-permute-done.20 = bf16[288,1280]{1,0:T(8,128)(2,1)} collective-permute-done((bf16[288,1280]{1,0:T(8,128)(2,1)}, bf16[288,1280]{1,0:T(8,128)(2,1)}, u32[]{:S(2)}, u32[]{:S(2)}) %collective-permute-start.20) | collective-permute-done | bytes 737312 | tf_op jit(solution)/shard_map/ppermute | solution.py:832
  343.7 4.6 add_convert_fusion.6
  348.3 1.5 collective-permute-start.23
  350.3 1.5 collective-permute-start.25
  351.8 11.1 %first_back.3 = (f32[384,384]{1,0:T(8,128)}, f32[25,384]{1,0:T(8,128)}) custom-call(bf16[1024,192]{1,0:T(8,128)(2,1)} %bitcast_select_fusion.x_ref, bf16[1152,384]{1,0:T(8,128)(2,1)} %copy-done.6, bf16[1152,384]{1,0:T(8,128)(2,1)} %copy-done.3, f32[25,8,1152]{2,1,0:T(8,128)} %broadcast_in_dim.30.taps_ref, f32[1024,128]{1,0:T(8,128)} %broadcast_in_dim.54.mask_ref, ...), custom_call_target="tpu_custom_call" | custom-call | flops 11000000512 | bytes 1048576 | tf_op jit(solution)/shard_map/first_back/pallas_call | solution.py:907
  364.3 5.0 %collective-permute-done.24 = bf16[288,768]{1,0:T(8,128)(2,1)} collective-permute-done((bf16[288,768]{1,0:T(8,128)(2,1)}, bf16[288,768]{1,0:T(8,128)(2,1)}, u32[]{:S(2)}, u32[]{:S(2)}) %collective-permute-start.24) | collective-permute-done | bytes 442400 | tf_op jit(solution)/shard_map/ppermute | solution.py:832
  372.8 1.8 fusion.2
  375.9 1.9 fusion.25
  377.9 1.4 collective-permute-start.30
  379.3 2.4 collective-permute-start.31
  382.3 1.8 fusion.3
  384.8 1.5 collective-permute-start.28
  386.2 2.2 collective-permute-done.30
  388.5 1.4 collective-permute-start.29
  392.0 3.6 collective-permute-done.31
  396.7 3.1 collective-permute-start.33
  401.0 1.5 collective-permute-start.37
  406.2 1.5 collective-permute-start.35
  407.8 9.1 %collective-permute-done.34 = bf16[72,1152]{1,0:T(8,128)(2,1)S(1)} collective-permute-done((bf16[72,1152]{1,0:T(8,128)(2,1)S(1)}, bf16[72,1152]{1,0:T(8,128)(2,1)S(1)}, u32[]{:S(2)}, u32[]{:S(2)}) %collective-permute-start.34) | collective-permute-done | bytes 165920 | tf_op jit(solution)/shard_map/ppermute | solution.py:832
  419.0 1.5 collective-permute-start.46
  421.0 1.5 collective-permute-start.44
  423.2 6.6 %collective-permute-done.40 = f32[33,128]{1,0:T(8,128)S(1)} collective-permute-done((f32[33,128]{1,0:T(8,128)S(1)}, f32[33,128]{1,0:T(8,128)S(1)}, u32[]{:S(2)}, u32[]{:S(2)}) %collective-permute-start.40) | collective-permute-done | bytes 16928 | tf_op jit(solution)/shard_map/ppermute | solution.py:832
  431.2 2.4 collective-permute-done.41
  433.6 3.6 collective-permute-start.42
  437.1 1.7 collective-permute-done.42
  438.9 2.8 collective-permute-start.43
  441.8 1.8 collective-permute-done.43
  444.2 3.9 adamw_head.1
  453.2 9.1 %adamw.2 = (f32[288,1826]{1,0:T(8,128)}, f32[288,1826]{1,0:T(8,128)}, f32[288,1826]{1,0:T(8,128)}, f32[288,1826]{1,0:T(8,128)}, bf16[288,1826]{1,0:T(8,128)(2,1)}) custom-call(s32[2]{0:T(128)} %pad_add_fusion.place_ref, f32[1,2]{1,0:T(1,128)} %get-tuple-element.233.factor_ref, bf16[288,1152]{1,0:T(8,128)(2,1)} %copy-done.2, bf16[288,1152]{1,0:T(8,128)(2,1)} %copy-done.5, ...), custom_call_target="tpu_custom_call" | custom-call | tf_op jit(solution)/shard_map/adamw/pallas_call | solution.py:790
  463.2 12.1 %adamw.3 = (f32[288,2800]{1,0:T(8,128)}, f32[288,2800]{1,0:T(8,128)}, f32[288,2800]{1,0:T(8,128)}, f32[288,2800]{1,0:T(8,128)}, bf16[288,2800]{1,0:T(8,128)(2,1)}) custom-call(s32[2]{0:T(128)} %pad_add_fusion.place_ref, f32[1,2]{1,0:T(1,128)} %get-tuple-element.233.factor_ref, bf16[288,1152]{1,0:T(8,128)(2,1)} %copy-done.2, bf16[288,1152]{1,0:T(8,128)(2,1)} %copy-done.5, ...), custom_call_target="tpu_custom_call" | custom-call | tf_op jit(solution)/shard_map/adamw/pallas_call | solution.py:790
  (221 shorter events, 55.5 us)
Async XLA Ops:
  7.2 161.7 %copy-start = (s32[64]{0:T(128)S(1)}, s32[64]{0:T(128)}, u32[]{:S(2)}) copy-start(s32[64]{0:T(128)} %param.21) | copy-start | bytes 772
  10.3 17.5 %copy-start.8 = (f32[3560,40]{0,1:T(8,128)S(1)}, f32[3560,40]{0,1:T(8,128)}, u32[]{:S(2)}) copy-start(f32[3560,40]{0,1:T(8,128)} %param.32) | copy-start | bytes 1708804
  13.8 14.8 %collective-permute-start = (bf16[72,1152]{1,0:T(8,128)(2,1)S(1)}, bf16[72,1152]{1,0:T(8,128)(2,1)S(1)}, u32[]{:S(2)}, u32[]{:S(2)}) collective-permute-start(bf16[72,1152]{1,0:T(8,128)(2,1)S(1)} %pad_maximum_fusion.4), channel_id=1, source_target_pairs={{0,1},{1,0},{2,3},{3,2},{4,5},{5,4},{6,7},{7,6},{8,9},{9,8},{10,11... | collective-permute-start | bytes 497672 | tf_op jit(solution)/shard_map/ppermute | solution.py:832
  16.9 18.0 %collective-permute-start.1 = (bf16[72,1152]{1,0:T(8,128)(2,1)S(1)}, bf16[72,1152]{1,0:T(8,128)(2,1)S(1)}, u32[]{:S(2)}, u32[]{:S(2)}) collective-permute-start(bf16[72,1152]{1,0:T(8,128)(2,1)S(1)} %pad_maximum_fusion.4), channel_id=1, source_target_pairs={{0,2},{1,3},{2,0},{3,1},{4,6},{5,7},{6,4},{7,5},{8,10},{9,11},{10,... | collective-permute-start | bytes 497672 | tf_op jit(solution)/shard_map/ppermute | solution.py:832
  19.5 15.4 %collective-permute-start.2 = (bf16[72,1152]{1,0:T(8,128)(2,1)S(1)}, bf16[72,1152]{1,0:T(8,128)(2,1)S(1)}, u32[]{:S(2)}, u32[]{:S(2)}) collective-permute-start(bf16[72,1152]{1,0:T(8,128)(2,1)S(1)} %pad_maximum_fusion.4), channel_id=1, source_target_pairs={{0,3},{1,2},{2,1},{3,0},{4,7},{5,6},{6,5},{7,4},{8,11},{9,10},{10,... | collective-permute-start | bytes 497672 | tf_op jit(solution)/shard_map/ppermute | solution.py:832
  19.5 27.8 %all-to-all-start = ((bf16[64,16,192]{2,1,0:T(8,128)(2,1)}), bf16[64,16,192]{2,1,0:T(8,128)(2,1)S(1)}, u32[]{:S(2)}, u32[]{:S(2)}) async-start(bf16[64,16,192]{2,1,0:T(8,128)(2,1)} %param.20), calls=%async_computation | async-start | bytes 1048576 | tf_op jit(solution)/shard_map/all_to_all | solution.py:990
  24.6 56.4 %all-gather.3.cloned.1.call-start = ((), (), s32[]{:S(2)}) async-start(), calls=%async_computation.2 | async-start | bytes 1433600 | tf_op jit(solution)/shard_map/all_gather | solution.py:995
  25.7 14.3 %collective-permute-start.3 = (bf16[72,1280]{1,0:T(8,128)(2,1)S(1)}, bf16[72,1280]{1,0:T(8,128)(2,1)S(1)}, u32[]{:S(2)}, u32[]{:S(2)}) collective-permute-start(bf16[72,1280]{1,0:T(8,128)(2,1)S(1)} %dynamic_slice.79), channel_id=1, source_target_pairs={{0,1},{1,0},{2,3},{3,2},{4,5},{5,4},{6,7},{7,6},{8,9},{9,8},{10,11... | collective-permute-start | bytes 552968 | tf_op jit(solution)/shard_map/ppermute | solution.py:832
  40.0 128.9 %all-gather.5.cloned.1.call-start = ((), (), s32[]{:S(2)}) async-start(), calls=%async_computation.3 | async-start | bytes 5734400 | tf_op jit(solution)/shard_map/all_gather | solution.py:1003
  40.2 39.1 %collective-permute-start.4 = (bf16[288,1152]{1,0:T(8,128)(2,1)S(1)}, bf16[288,1152]{1,0:T(8,128)(2,1)S(1)}, u32[]{:S(2)}, u32[]{:S(2)}) collective-permute-start(bf16[288,1152]{1,0:T(8,128)(2,1)S(1)} %constant_dynamic-update-slice_fusion), channel_id=1, source_target_pairs={{0,8},{8,0},{16,24},{24,16},{1,9},{9,1},{17,25},{25,17},{2,10},{10... | collective-permute-start | bytes 1990664 | tf_op jit(solution)/shard_map/ppermute | solution.py:832
  41.7 37.5 %collective-permute-start.5 = (bf16[288,1152]{1,0:T(8,128)(2,1)S(1)}, bf16[288,1152]{1,0:T(8,128)(2,1)}, u32[]{:S(2)}, u32[]{:S(2)}) collective-permute-start(bf16[288,1152]{1,0:T(8,128)(2,1)S(1)} %constant_dynamic-update-slice_fusion), channel_id=1, source_target_pairs={{0,16},{8,24},{16,0},{24,8},{1,17},{9,25},{17,1},{25,9},{2,18},{10... | collective-permute-start | bytes 1990664 | tf_op jit(solution)/shard_map/ppermute | solution.py:832
  43.2 36.0 %collective-permute-start.6 = (bf16[288,1152]{1,0:T(8,128)(2,1)S(1)}, bf16[288,1152]{1,0:T(8,128)(2,1)}, u32[]{:S(2)}, u32[]{:S(2)}) collective-permute-start(bf16[288,1152]{1,0:T(8,128)(2,1)S(1)} %constant_dynamic-update-slice_fusion), channel_id=1, source_target_pairs={{0,24},{8,16},{16,8},{24,0},{1,25},{9,17},{17,9},{25,1},{2,26},{10... | collective-permute-start | bytes 1990664 | tf_op jit(solution)/shard_map/ppermute | solution.py:832
  43.7 35.5 %collective-permute-start.7 = (bf16[144,1280]{1,0:T(8,128)(2,1)S(1)}, bf16[144,1280]{1,0:T(8,128)(2,1)S(1)}, u32[]{:S(2)}, u32[]{:S(2)}) collective-permute-start(bf16[144,1280]{1,0:T(8,128)(2,1)S(1)} %constant_dynamic-update-slice_fusion.4), channel_id=1, source_target_pairs={{0,2},{1,3},{2,0},{3,1},{4,6},{5,7},{6,4},{7,5},{8,10},{9,11},{10,... | collective-permute-start | bytes 1105928 | tf_op jit(solution)/shard_map/ppermute | solution.py:832
  86.7 7.3 %collective-permute-start.8 = (bf16[1152,1152]{1,0:T(8,128)(2,1)}, bf16[1152,1152]{1,0:T(8,128)(2,1)}, u32[]{:S(2)}, u32[]{:S(2)}) collective-permute-start(bf16[1152,1152]{1,0:T(8,128)(2,1)} %constant_dynamic-update-slice_fusion.6.own_ref), channel_id=1, source_target_pairs={{0,4},{4,0},{1,5},{5,1},{2,6},{6,2},{3,7},{7,3},{8,12},{12,8},{9,1... | collective-permute-start | bytes 7962632 | tf_op jit(solution)/shard_map/ppermute | solution.py:832
  89.5 52.0 %collective-permute-start.9 = (bf16[288,1280]{1,0:T(8,128)(2,1)}, bf16[288,1280]{1,0:T(8,128)(2,1)}, u32[]{:S(2)}, u32[]{:S(2)}) collective-permute-start(bf16[288,1280]{1,0:T(8,128)(2,1)} %constant_dynamic-update-slice_fusion.10), channel_id=1, source_target_pairs={{0,8},{8,0},{16,24},{24,16},{1,9},{9,1},{17,25},{25,17},{2,10},{10... | collective-permute-start | bytes 2211848 | tf_op jit(solution)/shard_map/ppermute | solution.py:832
  91.0 50.5 %collective-permute-start.10 = (bf16[288,1280]{1,0:T(8,128)(2,1)}, bf16[288,1280]{1,0:T(8,128)(2,1)}, u32[]{:S(2)}, u32[]{:S(2)}) collective-permute-start(bf16[288,1280]{1,0:T(8,128)(2,1)} %constant_dynamic-update-slice_fusion.10), channel_id=1, source_target_pairs={{0,16},{8,24},{16,0},{24,8},{1,17},{9,25},{17,1},{25,9},{2,18},{10... | collective-permute-start | bytes 2211848 | tf_op jit(solution)/shard_map/ppermute | solution.py:832
  92.5 49.0 %collective-permute-start.11 = (bf16[288,1280]{1,0:T(8,128)(2,1)}, bf16[288,1280]{1,0:T(8,128)(2,1)}, u32[]{:S(2)}, u32[]{:S(2)}) collective-permute-start(bf16[288,1280]{1,0:T(8,128)(2,1)} %constant_dynamic-update-slice_fusion.10), channel_id=1, source_target_pairs={{0,24},{8,16},{16,8},{24,0},{1,25},{9,17},{17,9},{25,1},{2,26},{10... | collective-permute-start | bytes 2211848 | tf_op jit(solution)/shard_map/ppermute | solution.py:832
  93.0 289.4 %reduce-scatter.2.cloned.1.call-start = ((), (), s32[]{:S(2)}) async-start(), calls=%async_computation.4 | async-start | bytes 2867200 | tf_op jit(solution)/shard_map/reduce_scatter | solution.py:1221
  146.4 5.6 %collective-permute-start.12 = (bf16[1152,1280]{1,0:T(8,128)(2,1)S(1)}, bf16[1152,1280]{1,0:T(8,128)(2,1)}, u32[]{:S(2)}, u32[]{:S(2)}) collective-permute-start(bf16[1152,1280]{1,0:T(8,128)(2,1)S(1)} %constant_dynamic-update-slice_fusion.12.own_ref), channel_id=1, source_target_pairs={{0,4},{4,0},{1,5},{5,1},{2,6},{6,2},{3,7},{7,3},{8,12},{12,8},{9,1... | collective-permute-start | bytes 8847368 | tf_op jit(solution)/shard_map/ppermute | solution.py:832
  168.9 8.1 %collective-permute-start.13 = (bf16[640,3584]{1,0:T(8,128)(2,1)}, bf16[640,3584]{1,0:T(8,128)(2,1)}, u32[]{:S(2)}, u32[]{:S(2)}) collective-permute-start(bf16[640,3584]{1,0:T(8,128)(2,1)} %all-gather.5.cloned.1.call-done.near_ref), channel_id=1, source_target_pairs={{0,4},{4,0},{1,5},{5,1},{2,6},{6,2},{3,7},{7,3},{8,12},{12,8},{9,1... | collective-permute-start | bytes 13762568 | tf_op jit(solution)/shard_map/ppermute | solution.py:832
  216.7 27.5 %collective-permute-start.14 = (bf16[640,3584]{1,0:T(8,128)(2,1)}, bf16[640,3584]{1,0:T(8,128)(2,1)}, u32[]{:S(2)}, u32[]{:S(2)}) collective-permute-start(bf16[640,3584]{1,0:T(8,128)(2,1)} %get-tuple-element.173), channel_id=1, source_target_pairs={{0,4},{4,0},{1,5},{5,1},{2,6},{6,2},{3,7},{7,3},{8,12},{12,8},{9,1... | collective-permute-start | bytes 13762568 | tf_op jit(solution)/shard_map/ppermute | solution.py:832
  243.8 59.9 %collective-permute-start.15 = (f32[1152,1280]{1,0:T(8,128)}, f32[1152,1280]{1,0:T(8,128)}, u32[]{:S(2)}, u32[]{:S(2)}) collective-permute-start(f32[1152,1280]{1,0:T(8,128)} %get-tuple-element.186), channel_id=1, source_target_pairs={{0,4},{4,0},{1,5},{5,1},{2,6},{6,2},{3,7},{7,3},{8,12},{12,8},{9,1... | collective-permute-start | bytes 17694728 | tf_op jit(solution)/shard_map/ppermute | solution.py:832
  250.3 42.3 %collective-permute-start.16 = (bf16[160,3584]{1,0:T(8,128)(2,1)}, bf16[160,3584]{1,0:T(8,128)(2,1)S(1)}, u32[]{:S(2)}, u32[]{:S(2)}) collective-permute-start(bf16[160,3584]{1,0:T(8,128)(2,1)} %get-tuple-element.336), channel_id=1, source_target_pairs={{0,8},{8,0},{16,24},{24,16},{1,9},{9,1},{17,25},{25,17},{2,10},{10... | collective-permute-start | bytes 3440648 | tf_op jit(solution)/shard_map/ppermute | solution.py:832
  251.8 51.9 %collective-permute-start.17 = (bf16[160,3584]{1,0:T(8,128)(2,1)}, bf16[160,3584]{1,0:T(8,128)(2,1)}, u32[]{:S(2)}, u32[]{:S(2)}) collective-permute-start(bf16[160,3584]{1,0:T(8,128)(2,1)} %get-tuple-element.335), channel_id=1, source_target_pairs={{0,16},{8,24},{16,0},{24,8},{1,17},{9,25},{17,1},{25,9},{2,18},{10... | collective-permute-start | bytes 3440648 | tf_op jit(solution)/shard_map/ppermute | solution.py:832
  252.3 51.4 %collective-permute-start.18 = (bf16[160,3584]{1,0:T(8,128)(2,1)}, bf16[160,3584]{1,0:T(8,128)(2,1)}, u32[]{:S(2)}, u32[]{:S(2)}) collective-permute-start(bf16[160,3584]{1,0:T(8,128)(2,1)} %get-tuple-element.334), channel_id=1, source_target_pairs={{0,24},{8,16},{16,8},{24,0},{1,25},{9,17},{17,9},{25,1},{2,26},{10... | collective-permute-start | bytes 3440648 | tf_op jit(solution)/shard_map/ppermute | solution.py:832
  292.5 51.2 %collective-permute-start.22 = (f32[1152,768]{1,0:T(8,128)}, f32[1152,768]{1,0:T(8,128)}, u32[]{:S(2)}, u32[]{:S(2)}) collective-permute-start(f32[1152,768]{1,0:T(8,128)} %get-tuple-element.194), channel_id=1, source_target_pairs={{0,4},{4,0},{1,5},{5,1},{2,6},{6,2},{3,7},{7,3},{8,12},{12,8},{9,1... | collective-permute-start | bytes 10616840 | tf_op jit(solution)/shard_map/ppermute | solution.py:832
  292.6 11.1 %copy-start.11 = (bf16[160,3584]{1,0:T(8,128)(2,1)}, bf16[160,3584]{1,0:T(8,128)(2,1)S(1)}, u32[]{:S(2)}) copy-start(bf16[160,3584]{1,0:T(8,128)(2,1)S(1)} %collective-permute-done.16) | copy-start | bytes 3440644
  303.7 9.6 %copy-start.12 = (bf16[160,3584]{1,0:T(8,128)(2,1)S(1)}, bf16[160,3584]{1,0:T(8,128)(2,1)}, u32[]{:S(2)}) copy-start(bf16[160,3584]{1,0:T(8,128)(2,1)} %copy-done.11) | copy-start | bytes 3440644
  309.9 26.8 %collective-permute-start.19 = (bf16[288,1280]{1,0:T(8,128)(2,1)}, bf16[288,1280]{1,0:T(8,128)(2,1)}, u32[]{:S(2)}, u32[]{:S(2)}) collective-permute-start(bf16[288,1280]{1,0:T(8,128)(2,1)} %get-tuple-element.332), channel_id=1, source_target_pairs={{0,8},{8,0},{16,24},{24,16},{1,9},{9,1},{17,25},{25,17},{2,10},{10... | collective-permute-start | bytes 2211848 | tf_op jit(solution)/shard_map/ppermute | solution.py:832
  310.4 33.3 %collective-permute-start.20 = (bf16[288,1280]{1,0:T(8,128)(2,1)}, bf16[288,1280]{1,0:T(8,128)(2,1)}, u32[]{:S(2)}, u32[]{:S(2)}) collective-permute-start(bf16[288,1280]{1,0:T(8,128)(2,1)} %get-tuple-element.331), channel_id=1, source_target_pairs={{0,16},{8,24},{16,0},{24,8},{1,17},{9,25},{17,1},{25,9},{2,18},{10... | collective-permute-start | bytes 2211848 | tf_op jit(solution)/shard_map/ppermute | solution.py:832
  311.9 31.8 %collective-permute-start.21 = (bf16[288,1280]{1,0:T(8,128)(2,1)}, bf16[288,1280]{1,0:T(8,128)(2,1)}, u32[]{:S(2)}, u32[]{:S(2)}) collective-permute-start(bf16[288,1280]{1,0:T(8,128)(2,1)} %get-tuple-element.330), channel_id=1, source_target_pairs={{0,24},{8,16},{16,8},{24,0},{1,25},{9,17},{17,9},{25,1},{2,26},{10... | collective-permute-start | bytes 2211848 | tf_op jit(solution)/shard_map/ppermute | solution.py:832
  348.3 16.0 %collective-permute-start.23 = (bf16[288,768]{1,0:T(8,128)(2,1)}, bf16[288,768]{1,0:T(8,128)(2,1)S(1)}, u32[]{:S(2)}, u32[]{:S(2)}) collective-permute-start(bf16[288,768]{1,0:T(8,128)(2,1)} %get-tuple-element.340), channel_id=1, source_target_pairs={{0,8},{8,0},{16,24},{24,16},{1,9},{9,1},{17,25},{25,17},{2,10},{10... | collective-permute-start | bytes 1327112 | tf_op jit(solution)/shard_map/ppermute | solution.py:832
  349.8 19.5 %collective-permute-start.24 = (bf16[288,768]{1,0:T(8,128)(2,1)}, bf16[288,768]{1,0:T(8,128)(2,1)}, u32[]{:S(2)}, u32[]{:S(2)}) collective-permute-start(bf16[288,768]{1,0:T(8,128)(2,1)} %get-tuple-element.339), channel_id=1, source_target_pairs={{0,16},{8,24},{16,0},{24,8},{1,17},{9,25},{17,1},{25,9},{2,18},{10... | collective-permute-start | bytes 1327112 | tf_op jit(solution)/shard_map/ppermute | solution.py:832
  350.3 19.0 %collective-permute-start.25 = (bf16[288,768]{1,0:T(8,128)(2,1)}, bf16[288,768]{1,0:T(8,128)(2,1)}, u32[]{:S(2)}, u32[]{:S(2)}) collective-permute-start(bf16[288,768]{1,0:T(8,128)(2,1)} %get-tuple-element.338), channel_id=1, source_target_pairs={{0,24},{8,16},{16,8},{24,0},{1,25},{9,17},{17,9},{25,1},{2,26},{10... | collective-permute-start | bytes 1327112 | tf_op jit(solution)/shard_map/ppermute | solution.py:832
  374.6 7.8 %collective-permute-start.26 = (f32[1152,384]{1,0:T(8,128)}, f32[1152,384]{1,0:T(8,128)}, u32[]{:S(2)}, u32[]{:S(2)}) collective-permute-start(f32[1152,384]{1,0:T(8,128)} %get-tuple-element.349), channel_id=1, source_target_pairs={{0,4},{4,0},{1,5},{5,1},{2,6},{6,2},{3,7},{7,3},{8,12},{12,8},{9,1... | collective-permute-start | bytes 5308424 | tf_op jit(solution)/shard_map/ppermute | solution.py:832
  377.9 10.6 %collective-permute-start.30 = (bf16[72,1280]{1,0:T(8,128)(2,1)S(1)}, bf16[72,1280]{1,0:T(8,128)(2,1)S(1)}, u32[]{:S(2)}, u32[]{:S(2)}) collective-permute-start(bf16[72,1280]{1,0:T(8,128)(2,1)S(1)} %get-tuple-element.366), channel_id=1, source_target_pairs={{0,1},{1,0},{2,3},{3,2},{4,5},{5,4},{6,7},{7,6},{8,9},{9,8},{10,11... | collective-permute-start | bytes 552968 | tf_op jit(solution)/shard_map/ppermute | solution.py:832
  379.3 16.3 %collective-permute-start.31 = (bf16[72,1280]{1,0:T(8,128)(2,1)S(1)}, bf16[72,1280]{1,0:T(8,128)(2,1)S(1)}, u32[]{:S(2)}, u32[]{:S(2)}) collective-permute-start(bf16[72,1280]{1,0:T(8,128)(2,1)S(1)} %get-tuple-element.365), channel_id=1, source_target_pairs={{0,2},{1,3},{2,0},{3,1},{4,6},{5,7},{6,4},{7,5},{8,10},{9,11},{10,... | collective-permute-start | bytes 552968 | tf_op jit(solution)/shard_map/ppermute | solution.py:832
  381.8 13.9 %collective-permute-start.32 = (bf16[72,1280]{1,0:T(8,128)(2,1)S(1)}, bf16[72,1280]{1,0:T(8,128)(2,1)S(1)}, u32[]{:S(2)}, u32[]{:S(2)}) collective-permute-start(bf16[72,1280]{1,0:T(8,128)(2,1)S(1)} %get-tuple-element.364), channel_id=1, source_target_pairs={{0,3},{1,2},{2,1},{3,0},{4,7},{5,6},{6,5},{7,4},{8,11},{9,10},{10,... | collective-permute-start | bytes 552968 | tf_op jit(solution)/shard_map/ppermute | solution.py:832
  382.3 7.6 %copy-start.4 = (f32[288,768]{1,0:T(8,128)S(1)}, f32[288,768]{1,0:T(8,128)}, u32[]{:S(2)}) copy-start(f32[288,768]{1,0:T(8,128)} %get-tuple-element.224) | copy-start | bytes 2654212
  382.3 7.6 %copy-start.17 = (bf16[288,768]{1,0:T(8,128)(2,1)S(1)}, bf16[288,768]{1,0:T(8,128)(2,1)}, u32[]{:S(2)}) copy-start(bf16[288,768]{1,0:T(8,128)(2,1)} %copy-done.16) | copy-start | bytes 1327108
  384.2 7.1 %copy-start.9 = (f32[40,3584]{1,0:T(8,128)S(1)}, f32[40,3584]{1,0:T(8,128)}, u32[]{:S(2)}) copy-start(f32[40,3584]{1,0:T(8,128)} %reduce-scatter.2.cloned.1.call-done.grad) | copy-start | bytes 1720324
  384.2 11.5 %collective-permute-start.27 = (bf16[288,384]{1,0:T(8,128)(2,1)S(1)}, bf16[288,384]{1,0:T(8,128)(2,1)S(1)}, u32[]{:S(2)}, u32[]{:S(2)}) collective-permute-start(bf16[288,384]{1,0:T(8,128)(2,1)S(1)} %get-tuple-element.346), channel_id=1, source_target_pairs={{0,8},{8,0},{16,24},{24,16},{1,9},{9,1},{17,25},{25,17},{2,10},{10... | collective-permute-start | bytes 663560 | tf_op jit(solution)/shard_map/ppermute | solution.py:832
  384.8 10.9 %collective-permute-start.28 = (bf16[288,384]{1,0:T(8,128)(2,1)S(1)}, bf16[288,384]{1,0:T(8,128)(2,1)S(1)}, u32[]{:S(2)}, u32[]{:S(2)}) collective-permute-start(bf16[288,384]{1,0:T(8,128)(2,1)S(1)} %get-tuple-element.345), channel_id=1, source_target_pairs={{0,16},{8,24},{16,0},{24,8},{1,17},{9,25},{17,1},{25,9},{2,18},{10... | collective-permute-start | bytes 663560 | tf_op jit(solution)/shard_map/ppermute | solution.py:832
  388.5 8.0 %collective-permute-start.29 = (bf16[288,384]{1,0:T(8,128)(2,1)S(1)}, bf16[288,384]{1,0:T(8,128)(2,1)S(1)}, u32[]{:S(2)}, u32[]{:S(2)}) collective-permute-start(bf16[288,384]{1,0:T(8,128)(2,1)S(1)} %get-tuple-element.344), channel_id=1, source_target_pairs={{0,24},{8,16},{16,8},{24,0},{1,25},{9,17},{17,9},{25,1},{2,26},{10... | collective-permute-start | bytes 663560 | tf_op jit(solution)/shard_map/ppermute | solution.py:832
  396.7 9.5 %collective-permute-start.33 = (bf16[72,1152]{1,0:T(8,128)(2,1)S(1)}, bf16[72,1152]{1,0:T(8,128)(2,1)S(1)}, u32[]{:S(2)}, u32[]{:S(2)}) collective-permute-start(bf16[72,1152]{1,0:T(8,128)(2,1)S(1)} %get-tuple-element.369), channel_id=1, source_target_pairs={{0,1},{1,0},{2,3},{3,2},{4,5},{5,4},{6,7},{7,6},{8,9},{9,8},{10,11... | collective-permute-start | bytes 497672 | tf_op jit(solution)/shard_map/ppermute | solution.py:832
  400.5 16.4 %collective-permute-start.36 = (bf16[72,1280]{1,0:T(8,128)(2,1)S(1)}, bf16[72,1280]{1,0:T(8,128)(2,1)S(1)}, u32[]{:S(2)}, u32[]{:S(2)}) collective-permute-start(bf16[72,1280]{1,0:T(8,128)(2,1)S(1)} %get-tuple-element.239), channel_id=1, source_target_pairs={{0,8},{8,0},{16,24},{24,16},{1,9},{9,1},{17,25},{25,17},{2,10},{10... | collective-permute-start | bytes 552968 | tf_op jit(solution)/shard_map/ppermute | solution.py:832
  401.0 15.8 %collective-permute-start.37 = (bf16[72,1280]{1,0:T(8,128)(2,1)S(1)}, bf16[72,1280]{1,0:T(8,128)(2,1)S(1)}, u32[]{:S(2)}, u32[]{:S(2)}) collective-permute-start(bf16[72,1280]{1,0:T(8,128)(2,1)S(1)} %get-tuple-element.239), channel_id=1, source_target_pairs={{0,16},{8,24},{16,0},{24,8},{1,17},{9,25},{17,1},{25,9},{2,18},{10... | collective-permute-start | bytes 552968 | tf_op jit(solution)/shard_map/ppermute | solution.py:832
  402.6 14.3 %collective-permute-start.38 = (bf16[72,1280]{1,0:T(8,128)(2,1)S(1)}, bf16[72,1280]{1,0:T(8,128)(2,1)S(1)}, u32[]{:S(2)}, u32[]{:S(2)}) collective-permute-start(bf16[72,1280]{1,0:T(8,128)(2,1)S(1)} %get-tuple-element.239), channel_id=1, source_target_pairs={{0,24},{8,16},{16,8},{24,0},{1,25},{9,17},{17,9},{25,1},{2,26},{10... | collective-permute-start | bytes 552968 | tf_op jit(solution)/shard_map/ppermute | solution.py:832
  404.0 12.9 %collective-permute-start.34 = (bf16[72,1152]{1,0:T(8,128)(2,1)S(1)}, bf16[72,1152]{1,0:T(8,128)(2,1)S(1)}, u32[]{:S(2)}, u32[]{:S(2)}) collective-permute-start(bf16[72,1152]{1,0:T(8,128)(2,1)S(1)} %get-tuple-element.368), channel_id=1, source_target_pairs={{0,2},{1,3},{2,0},{3,1},{4,6},{5,7},{6,4},{7,5},{8,10},{9,11},{10,... | collective-permute-start | bytes 497672 | tf_op jit(solution)/shard_map/ppermute | solution.py:832
  406.2 10.6 %collective-permute-start.35 = (bf16[72,1152]{1,0:T(8,128)(2,1)S(1)}, bf16[72,1152]{1,0:T(8,128)(2,1)S(1)}, u32[]{:S(2)}, u32[]{:S(2)}) collective-permute-start(bf16[72,1152]{1,0:T(8,128)(2,1)S(1)} %get-tuple-element.367), channel_id=1, source_target_pairs={{0,3},{1,2},{2,1},{3,0},{4,7},{5,6},{6,5},{7,4},{8,11},{9,10},{10,... | collective-permute-start | bytes 497672 | tf_op jit(solution)/shard_map/ppermute | solution.py:832
  418.3 4.2 collective-permute-start.39
  419.0 30.4 %collective-permute-start.46 = (bf16[72,1152]{1,0:T(8,128)(2,1)S(1)}, bf16[72,1152]{1,0:T(8,128)(2,1)S(1)}, u32[]{:S(2)}, u32[]{:S(2)}) collective-permute-start(bf16[72,1152]{1,0:T(8,128)(2,1)S(1)} %get-tuple-element.362), channel_id=1, source_target_pairs={{0,24},{8,16},{16,8},{24,0},{1,25},{9,17},{17,9},{25,1},{2,26},{10... | collective-permute-start | bytes 497672 | tf_op jit(solution)/shard_map/ppermute | solution.py:832
  420.5 28.9 %collective-permute-start.45 = (bf16[72,1152]{1,0:T(8,128)(2,1)S(1)}, bf16[72,1152]{1,0:T(8,128)(2,1)S(1)}, u32[]{:S(2)}, u32[]{:S(2)}) collective-permute-start(bf16[72,1152]{1,0:T(8,128)(2,1)S(1)} %get-tuple-element.362), channel_id=1, source_target_pairs={{0,16},{8,24},{16,0},{24,8},{1,17},{9,25},{17,1},{25,9},{2,18},{10... | collective-permute-start | bytes 497672 | tf_op jit(solution)/shard_map/ppermute | solution.py:832
  421.0 28.4 %collective-permute-start.44 = (bf16[72,1152]{1,0:T(8,128)(2,1)S(1)}, bf16[72,1152]{1,0:T(8,128)(2,1)S(1)}, u32[]{:S(2)}, u32[]{:S(2)}) collective-permute-start(bf16[72,1152]{1,0:T(8,128)(2,1)S(1)} %get-tuple-element.362), channel_id=1, source_target_pairs={{0,8},{8,0},{16,24},{24,16},{1,9},{9,1},{17,25},{25,17},{2,10},{10... | collective-permute-start | bytes 497672 | tf_op jit(solution)/shard_map/ppermute | solution.py:832
  422.5 7.3 %collective-permute-start.40 = (f32[33,128]{1,0:T(8,128)S(1)}, f32[33,128]{1,0:T(8,128)S(1)}, u32[]{:S(2)}, u32[]{:S(2)}) collective-permute-start(f32[33,128]{1,0:T(8,128)S(1)} %fusion.22), channel_id=1, source_target_pairs={{0,8},{8,0},{16,24},{24,16},{1,9},{9,1},{17,25},{25,17},{2,10},{10... | collective-permute-start | bytes 50696 | tf_op jit(solution)/shard_map/ppermute | solution.py:832
  429.8 3.8 collective-permute-start.41
  433.6 5.3 %collective-permute-start.42 = (f32[33,128]{1,0:T(8,128)S(1)}, f32[33,128]{1,0:T(8,128)S(1)}, u32[]{:S(2)}, u32[]{:S(2)}) collective-permute-start(f32[33,128]{1,0:T(8,128)S(1)} %add.262), channel_id=1, source_target_pairs={{0,1},{1,0},{2,3},{3,2},{4,5},{5,4},{6,7},{7,6},{8,9},{9,8},{10,11... | collective-permute-start | bytes 50696 | tf_op jit(solution)/shard_map/ppermute | solution.py:832
  438.9 4.7 collective-permute-start.43
  441.7 7.8 %copy-start.10 = (bf16[288,1280]{1,0:T(8,128)(2,1)}, bf16[288,1280]{1,0:T(8,128)(2,1)S(1)}, u32[]{:S(2)}) copy-start(bf16[288,1280]{1,0:T(8,128)(2,1)S(1)} %constant_dynamic-update-slice_fusion.18.refs_2_) | copy-start | bytes 2211844
  441.7 20.7 %collective-permute-start.48 = (bf16[288,1280]{1,0:T(8,128)(2,1)S(1)}, bf16[288,1280]{1,0:T(8,128)(2,1)S(1)}, u32[]{:S(2)}, u32[]{:S(2)}) collective-permute-start(bf16[288,1280]{1,0:T(8,128)(2,1)S(1)} %constant_dynamic-update-slice_fusion.18.refs_2_), channel_id=1, source_target_pairs={{0,4},{4,0},{1,5},{5,1},{2,6},{6,2},{3,7},{7,3},{8,12},{12,8},{9,1... | collective-permute-start | bytes 2211848 | tf_op jit(solution)/shard_map/ppermute | solution.py:832
  444.2 7.6 %copy-start.28 = (f32[512,8]{0,1:T(8,128)S(1)}, f32[512,8]{0,1:T(8,128)}, u32[]{:S(2)}) copy-start(f32[512,8]{0,1:T(8,128)} %param.39) | copy-start | bytes 49156
  449.5 2.9 collective-permute-start.47
  451.8 10.6 %copy-start.24 = (f32[512,8]{0,1:T(8,128)}, f32[512,8]{0,1:T(8,128)S(1)}, u32[]{:S(2)}) copy-start(f32[512,8]{0,1:T(8,128)S(1)} %get-tuple-element.323) | copy-start | bytes 49156
  463.2 12.1 %copy-start.1 = (s32[64]{0:T(128)S(1)}, s32[64]{0:T(128)}, u32[]{:S(2)}) copy-start(s32[64]{0:T(128)} %param.21) | copy-start | bytes 772
  (21 other events, 84.3 us)
Sparse Core Ops, SparseCore 0:
  40.1 40.7 all-gather.2
  93.1 75.7 all-gather.4
  317.1 46.9 reduce-scatter.1
